TPU v7x, 32 devices: a whole 2x2x4 slice. The times are simulated.
32 devices in a mesh: seq: 8 (over z, y), head: 4 (over x, core).
Axes of the slice: x: 2, y: 2, z: 4, core: 2. Of those that a mesh axis runs over, the one named last changes fastest.
Arguments:
- tokens: bfloat16 [8, 1024, 2048], P(None, 'seq'), may hold values from -6 to 6
- cotangent: bfloat16 [8, 1024, 2048], P(None, 'seq'), may hold values from -6 to 6
- first_norm_gain: bfloat16 [2048], replicated, may hold values from 0.5 to 1.5
- second_norm_gain: bfloat16 [2048], replicated, may hold values from 0.5 to 1.5
- query_weight: bfloat16 [2048, 2048], P('seq', 'head'), may hold values from -0.125 to 0.125
- key_weight: bfloat16 [2048, 512], P('seq', 'head'), may hold values from -0.125 to 0.125
- value_weight: bfloat16 [2048, 512], P('seq', 'head'), may hold values from -0.125 to 0.125
- output_weight: bfloat16 [2048, 2048], P('head', 'seq'), may hold values from -0.75 to 0.75
- gate_weight: bfloat16 [2048, 8192], P('seq', 'head'), may hold values from -0.125 to 0.125
- up_weight: bfloat16 [2048, 8192], P('seq', 'head'), may hold values from -0.125 to 0.125
- down_weight: bfloat16 [8192, 2048], P('head', 'seq'), may hold values from -0.0625 to 0.0625
- adapter_down_weight: bfloat16 [2048, 24], replicated, may hold values from -0.125 to 0.125
- adapter_query_weight: bfloat16 [8, 2048], P(None, 'head'), may hold values from -0.5 to 0.5
- adapter_key_weight: bfloat16 [8, 512], P(None, 'head'), may hold values from -0.5 to 0.5
- adapter_value_weight: bfloat16 [8, 512], P(None, 'head'), may hold values from -0.5 to 0.5
- adapter_output_down: bfloat16 [2048, 8], P('head'), may hold values from -0.75 to 0.75
- adapter_output_up: bfloat16 [8, 2048], replicated, may hold values from -1 to 1
- hedgehog_query_weight: bfloat16 [32, 64, 64], P('head'), may hold values from -1 to 1
- hedgehog_key_weight: bfloat16 [8, 64, 64], P('head'), may hold values from -1 to 1
- document_index: int32 [8, 1024], replicated, may hold values from 0 to 4, as said below
Outputs:
- layer_out: bfloat16 [8, 1024, 2048], P(None, 'seq')
- grad_tokens: float32 [8, 1024, 2048], P(None, 'seq')
- grad_gain_one: float32 [2048], replicated
- grad_gain_two: float32 [2048], replicated
- grad_w_query: float32 [2048, 2048], P('seq', 'head')
- grad_w_key: float32 [2048, 512], P('seq', 'head')
- grad_w_value: float32 [2048, 512], P('seq', 'head')
- grad_w_out: float32 [2048, 2048], P('head', 'seq')
- grad_w_gate: float32 [2048, 8192], P('seq', 'head')
- grad_w_up: float32 [2048, 8192], P('seq', 'head')
- grad_w_down: float32 [8192, 2048], P('head', 'seq')
- adapter_down_gradient: float32 [2048, 24], replicated
- adapter_query_gradient: float32 [8, 2048], P(None, 'head')
- adapter_key_gradient: float32 [8, 512], P(None, 'head')
- adapter_value_gradient: float32 [8, 512], P(None, 'head')
- adapter_output_down_gradient: float32 [2048, 8], P('head')
- adapter_output_up_gradient: float32 [8, 2048], replicated
- grad_map_query: float32 [32, 64, 64], P('head')
- grad_map_key: float32 [8, 64, 64], P('head')
Inputs may be any that keep to these rules, and one draw needn't show every extreme that they name: `document_index`: in each row the ids start at 0, never fall, and end at 4; where the id changes a new document begins.
All inputs are finite; a program needn't handle non-finite values.
Results may differ from a plain program's by a relative error of at most 0.023.
Values may be sent and summed in bfloat16 or wider, within the bound.
No kernel may reach another device: no remote copies, remote signals or barrier semaphores. Data moves between devices by JAX's collectives and lax.ppermute only.
A program may use at most 256 MiB of HBM per device.

v0:
```python
import jax
import jax.numpy as jnp
from jax import lax
from jax.sharding import PartitionSpec as P

WIN = 64


epsilon = 1e-05
rope_base = 500000.0
highest = lax.Precision.HIGHEST
adapter_scale = 2.0


def shifted(block, axis, distance):
    devices = range(lax.axis_size(axis))
    route = [(i - distance, i) for i in devices if i - distance in devices]
    return lax.ppermute(block, axis, route)


def carried_in(value, axis, join, neutral):
    count, mine = (lax.axis_size(axis), lax.axis_index(axis))
    pieces = jax.tree.map(lambda part: lax.all_gather(part, axis), value)
    so_far = jax.tree.map(
        lambda part, zero: jnp.full_like(part, 0) + jnp.asarray(zero, part.dtype), value, neutral
    )

    def turn(position, so_far):
        longer = join(so_far, jax.tree.map(lambda part: part[position], pieces))
        return jax.tree.map(lambda new, old: jnp.where(position < mine, new, old), longer, so_far)

    return lax.fori_loop(0, count - 1, turn, so_far)


def carried_in_2(value, axis, join, neutral):
    count = lax.axis_size(axis)
    place = lax.axis_index(axis)
    ahead = count - 1 - place
    gathered = jax.tree.map(
        lambda a, kind: lax.all_gather(a.astype(kind), axis),
        value,
        (jnp.bfloat16, jnp.bfloat16, jnp.bfloat16),
    )
    state = jax.tree.map(lambda a, e: jnp.zeros_like(a) + jnp.asarray(e, a.dtype), value, neutral)

    def one(turn, state):
        source = count - 1 - turn
        return join(
            state,
            jax.tree.map(
                lambda a, own: lax.dynamic_index_in_dim(a, source, 0, False).astype(own.dtype),
                gathered,
                value,
            ),
        )

    return lax.fori_loop(0, ahead, one, state)


def precise_product(left, right):
    return jnp.matmul(left, right, precision=highest)


def forward_product(left, right):
    return jnp.dot(left, right, preferred_element_type=jnp.float32)


def left_dot(left, right):
    return lax.dot_general(
        left, right, (((0,), (0,)), ((), ())), preferred_element_type=jnp.float32
    )


def right_dot(left, right):
    return lax.dot_general(
        left, right, (((1,), (1,)), ((), ())), preferred_element_type=jnp.float32
    )


def rope_tables(positions, size):
    inverse = rope_base ** (-jnp.arange(0, size, 2, dtype=jnp.float32) / size)
    angle = positions.astype(jnp.float32)[:, None] * inverse[None, :]
    cosine_table = jnp.concatenate([jnp.cos(angle), jnp.cos(angle)], axis=-1)
    sine_table = jnp.concatenate([jnp.sin(angle), jnp.sin(angle)], axis=-1)
    return (cosine_table, sine_table)


def apply_rotation(values, cosine_table, sine_table):
    half = values.shape[-1] // 2
    swapped = jnp.concatenate([-values[..., half:], values[..., :half]], axis=-1)
    return values * cosine_table[:, None, :] + swapped * sine_table[:, None, :]


def unrotate(grads, cosine_table, sine_table):
    half = grads.shape[-1] // 2
    scaled = grads * sine_table[:, None, :]
    swapped = jnp.concatenate([scaled[..., half:], -scaled[..., :half]], axis=-1)
    return grads * cosine_table[:, None, :] + swapped


def feature_pair(projected):
    return (jax.nn.softmax(projected, axis=-1), jax.nn.softmax(-projected, axis=-1))


def feature_back(grads, plus, minus):
    half = plus.shape[-1]
    grad_plus = grads[..., :half]
    grad_minus = grads[..., half:]
    first = plus * (grad_plus - jnp.sum(grad_plus * plus, axis=-1, keepdims=True))
    second = minus * (grad_minus - jnp.sum(grad_minus * minus, axis=-1, keepdims=True))
    return first - second


def combine_states(earlier, later):
    state_a, total_a, label_a = earlier
    state_b, total_b, label_b = later
    empty = label_b < 0
    joined = label_a == label_b

    def choose(first, second):
        extra = (1,) * (first.ndim - 1)
        vacant = empty.reshape(empty.shape + extra)
        linked = joined.reshape(joined.shape + extra)
        return jnp.where(vacant, first, jnp.where(linked, first + second, second))

    return (choose(state_a, state_b), choose(total_a, total_b), jnp.where(empty, label_a, label_b))


def body(
    tokens,
    cotangent,
    first_norm_gain,
    second_norm_gain,
    query_weight,
    key_weight,
    value_weight,
    output_weight,
    gate_weight,
    up_weight,
    down_weight,
    adapter_down_weight,
    adapter_query_weight,
    adapter_key_weight,
    adapter_value_weight,
    adapter_output_down,
    adapter_output_up,
    hedgehog_query_weight,
    hedgehog_key_weight,
    document_index,
):
    row_count, shard, width = tokens.shape
    window = WIN
    seq_index = lax.axis_index("seq")
    heads_here = hedgehog_query_weight.shape[0]
    kv_here = hedgehog_key_weight.shape[0]
    head_group = heads_here // kv_here
    size = hedgehog_query_weight.shape[1]
    adapter_rank = adapter_query_weight.shape[0]
    tokens_here = row_count * shard
    weights = (
        query_weight,
        key_weight,
        value_weight,
        output_weight,
        gate_weight,
        up_weight,
        down_weight,
    )
    gathered = (
        lax.all_gather(weights[0], "seq", axis=0, tiled=True),
        lax.all_gather(weights[1], "seq", axis=0, tiled=True),
        lax.all_gather(weights[2], "seq", axis=0, tiled=True),
        lax.all_gather(weights[3], "seq", axis=1, tiled=True),
        lax.all_gather(weights[4], "seq", axis=0, tiled=True),
        lax.all_gather(weights[5], "seq", axis=0, tiled=True),
        lax.all_gather(weights[6], "seq", axis=1, tiled=True),
    )
    complete_query, complete_key, complete_value, full_out, full_gate, full_up, full_down = gathered
    flattened = tokens.reshape(tokens_here, width).astype(jnp.float32)
    scale_one = lax.rsqrt(jnp.mean(flattened * flattened, axis=-1, keepdims=True) + epsilon)
    unit_one = flattened * scale_one
    normalized_input = (unit_one * first_norm_gain.astype(jnp.float32)).astype(jnp.bfloat16)
    lowrank_input = forward_product(normalized_input, adapter_down_weight)
    query_linear = forward_product(
        normalized_input, complete_query
    ) + adapter_scale * precise_product(
        lowrank_input[:, :adapter_rank], adapter_query_weight.astype(jnp.float32)
    )
    key_linear = forward_product(normalized_input, complete_key) + adapter_scale * precise_product(
        lowrank_input[:, adapter_rank : 2 * adapter_rank], adapter_key_weight.astype(jnp.float32)
    )
    value_linear = forward_product(
        normalized_input, complete_value
    ) + adapter_scale * precise_product(
        lowrank_input[:, 2 * adapter_rank :], adapter_value_weight.astype(jnp.float32)
    )
    positions = seq_index * shard + jnp.arange(shard)
    cosine_table, sine_table = rope_tables(positions, size)
    query_rot = apply_rotation(
        query_linear.reshape(row_count, shard, heads_here, size), cosine_table, sine_table
    ).astype(jnp.bfloat16)
    key_rot = apply_rotation(
        key_linear.reshape(row_count, shard, kv_here, size), cosine_table, sine_table
    ).astype(jnp.bfloat16)
    value_low = value_linear.reshape(row_count, shard, kv_here, size).astype(jnp.bfloat16)
    query_plus, query_minus = feature_pair(
        jnp.einsum(
            "rthd,hdf->rthf", query_rot, hedgehog_query_weight, preferred_element_type=jnp.float32
        )
    )
    key_plus, key_minus = feature_pair(
        jnp.einsum(
            "rthd,hdf->rthf", key_rot, hedgehog_key_weight, preferred_element_type=jnp.float32
        )
    )
    query_features = jnp.concatenate([query_plus, query_minus], axis=-1).astype(jnp.bfloat16)
    phi_key = jnp.concatenate([key_plus, key_minus], axis=-1).astype(jnp.bfloat16)
    tails = (
        key_rot[:, shard - window :],
        value_low[:, shard - window :],
        phi_key[:, shard - window :],
    )
    halo_key, halo_value, halo_phi = shifted((tails[0], tails[1], tails[2]), "seq", 1)
    all_key = jnp.concatenate([halo_key, key_rot], axis=1)
    all_value = jnp.concatenate([halo_value, value_low], axis=1)
    all_phi = jnp.concatenate([halo_phi, phi_key], axis=1)
    padded_seg = jnp.concatenate(
        [jnp.full((row_count, window), -1, jnp.int32), document_index], axis=1
    )
    key_seg = lax.dynamic_slice_in_dim(padded_seg, seq_index * shard, shard + window, 1)
    query_seg = key_seg[:, window:]
    label_here = key_seg[:, shard - 1].astype(jnp.float32)
    keep = key_seg[:, :shard] == key_seg[:, shard - 1 : shard]
    kept_phi = all_phi[:, :shard] * keep[:, :, None, None].astype(jnp.bfloat16)
    element_state = jnp.einsum(
        "rjgf,rjgh->rgfh", kept_phi, all_value[:, :shard], preferred_element_type=jnp.float32
    )
    element_total = jnp.sum(kept_phi.astype(jnp.float32), axis=1)
    identity = (
        jnp.zeros_like(element_state),
        jnp.zeros_like(element_total),
        jnp.full_like(label_here, -1.0),
    )
    carry_state, carry_total, carry_label = carried_in(
        (element_state, element_total, label_here), "seq", combine_states, identity
    )
    query_grouped = query_rot.reshape(row_count, shard, kv_here, head_group, size)
    phi_grouped = query_features.reshape(
        row_count, shard, kv_here, head_group, query_features.shape[-1]
    )
    same = query_seg[:, :, None] == key_seg[:, None, :]
    row_pos = jnp.arange(shard)[:, None]
    col_pos = jnp.arange(shard + window)[None, :]
    inside = (same & (col_pos > row_pos) & (col_pos <= row_pos + window))[:, None, None]
    older = (same & (col_pos <= row_pos))[:, None, None]
    factor = size ** (-0.5)
    scores = (
        jnp.einsum("rigch,rjgh->rgcij", query_grouped, all_key, preferred_element_type=jnp.float32)
        * factor
    )
    near_weight = jnp.where(inside, jnp.exp(scores), 0.0)
    probs = near_weight.astype(jnp.bfloat16)
    num_window = jnp.einsum(
        "rgcij,rjgh->rigch", probs, all_value, preferred_element_type=jnp.float32
    )
    den_window = jnp.sum(near_weight, axis=-1).transpose(0, 3, 1, 2)
    kernel = jnp.where(
        older,
        jnp.einsum("rigcf,rjgf->rgcij", phi_grouped, all_phi, preferred_element_type=jnp.float32),
        0.0,
    )
    value_wide = all_value.astype(jnp.float32)
    phi_wide = phi_grouped.astype(jnp.float32)
    num_linear = jnp.einsum("rgcij,rjgh->rigch", kernel, value_wide, precision=highest)
    den_linear = jnp.sum(kernel, axis=-1).transpose(0, 3, 1, 2)
    reaches = (query_seg.astype(jnp.float32) == carry_label[:, None])[:, :, None, None]
    carried = jnp.einsum("rigcf,rgfh->rigch", phi_wide, carry_state, precision=highest)
    num_linear = num_linear + jnp.where(reaches[..., None], carried, 0.0)
    carried_total = jnp.einsum("rigcf,rgf->rigc", phi_wide, carry_total, precision=highest)
    den_linear = den_linear + jnp.where(reaches, carried_total, 0.0)
    denominator = den_window + den_linear
    mixed = (num_window + num_linear) / denominator[..., None]
    attention_result = mixed.astype(jnp.bfloat16).reshape(tokens_here, heads_here * size)
    out_part = forward_product(attention_result, full_out)
    lowrank_slice = forward_product(attention_result, adapter_output_down)
    output_sum, lowrank_output = lax.psum((out_part, lowrank_slice), "head")
    hidden_state = (
        flattened
        + output_sum
        + adapter_scale * precise_product(lowrank_output, adapter_output_up.astype(jnp.float32))
    )
    scale_two = lax.rsqrt(jnp.mean(hidden_state * hidden_state, axis=-1, keepdims=True) + epsilon)
    unit_two = hidden_state * scale_two
    normed_rows = (unit_two * second_norm_gain.astype(jnp.float32)).astype(jnp.bfloat16)
    gate = forward_product(normed_rows, full_gate)
    up = forward_product(normed_rows, full_up)
    sigmoid_gate = jax.nn.sigmoid(gate)
    swish = gate * sigmoid_gate
    inner = (swish * up).astype(jnp.bfloat16)
    down_part = forward_product(inner, full_down)
    mlp_out = lax.psum(down_part.astype(jnp.bfloat16), "head").astype(jnp.float32)
    layer_rows = (hidden_state + mlp_out).astype(jnp.bfloat16)
    grad_out = cotangent.reshape(tokens_here, width)
    grad_w_down = left_dot(inner, grad_out)
    grad_inner = right_dot(grad_out, full_down)
    grad_gate = (grad_inner * up * sigmoid_gate * (1.0 + gate * (1.0 - sigmoid_gate))).astype(
        jnp.bfloat16
    )
    grad_up = (grad_inner * swish).astype(jnp.bfloat16)
    grad_w_gate = left_dot(normed_rows, grad_gate)
    grad_w_up = left_dot(normed_rows, grad_up)
    normed_two_part = right_dot(grad_gate, full_gate) + right_dot(grad_up, full_up)
    grad_normed_two = lax.psum(normed_two_part, "head")
    grad_out_rows = grad_out.astype(jnp.float32)
    grad_gain_two = jnp.sum(grad_normed_two * unit_two, axis=0)
    inner_two = grad_normed_two * second_norm_gain.astype(jnp.float32)
    grad_hidden = grad_out_rows + scale_two * (
        inner_two - unit_two * jnp.mean(inner_two * unit_two, axis=-1, keepdims=True)
    )
    branch_gradient_rows = grad_hidden.astype(jnp.bfloat16)
    adapter_output_up_gradient = adapter_scale * precise_product(
        lowrank_output.T, branch_gradient_rows.astype(jnp.float32)
    )
    branch_gradient_wide = branch_gradient_rows.astype(jnp.float32)
    grad_w_out = left_dot(attention_result, branch_gradient_rows)
    lowrank_output_gradient = adapter_scale * precise_product(
        branch_gradient_wide, adapter_output_up.astype(jnp.float32).T
    )
    adapter_output_down_gradient = precise_product(
        attention_result.astype(jnp.float32).T, lowrank_output_gradient
    )
    grad_attended = right_dot(branch_gradient_rows, full_out) + precise_product(
        lowrank_output_gradient, adapter_output_down.astype(jnp.float32).T
    )
    grad_mixed = (
        grad_attended.astype(jnp.bfloat16)
        .astype(jnp.float32)
        .reshape(row_count, shard, kv_here, head_group, size)
    )
    grad_num = grad_mixed / denominator[..., None]
    grad_den = -jnp.sum(grad_mixed * mixed, axis=-1) / denominator
    grad_near = grad_num.astype(jnp.bfloat16)
    grad_den_cols = grad_den.transpose(0, 2, 3, 1)[..., None]
    grad_probs = jnp.einsum(
        "rigch,rjgh->rgcij", grad_near, all_value, preferred_element_type=jnp.float32
    )
    grad_value_all = jnp.einsum(
        "rgcij,rigch->rjgh", probs, grad_near, preferred_element_type=jnp.float32
    )
    grad_scores = ((grad_probs + grad_den_cols) * near_weight).astype(jnp.bfloat16)
    grad_query_att = (
        jnp.einsum("rgcij,rjgh->rigch", grad_scores, all_key, preferred_element_type=jnp.float32)
        * factor
    )
    grad_key_all = (
        jnp.einsum(
            "rgcij,rigch->rjgh", grad_scores, query_grouped, preferred_element_type=jnp.float32
        )
        * factor
    )
    grad_kernel = jnp.where(
        older,
        jnp.einsum("rigch,rjgh->rgcij", grad_num, value_wide, precision=highest) + grad_den_cols,
        0.0,
    )
    grad_value_all = grad_value_all + jnp.einsum(
        "rgcij,rigch->rjgh", kernel, grad_num, precision=highest
    )
    grad_phi_q = jnp.einsum(
        "rgcij,rjgf->rigcf", grad_kernel, all_phi.astype(jnp.float32), precision=highest
    )
    grad_phi_all = jnp.einsum("rgcij,rigcf->rjgf", grad_kernel, phi_wide, precision=highest)
    masked_num = jnp.where(reaches[..., None], grad_num, 0.0)
    masked_den = jnp.where(reaches, grad_den, 0.0)
    grad_phi_q = grad_phi_q + jnp.einsum(
        "rigch,rgfh->rigcf", masked_num, carry_state, precision=highest
    )
    grad_phi_q = grad_phi_q + masked_den[..., None] * carry_total[:, None, :, None, :]
    grad_carry_state = jnp.einsum("rigcf,rigch->rgfh", phi_wide, masked_num, precision=highest)
    grad_carry_total = jnp.einsum("rigcf,rigc->rgf", phi_wide, masked_den, precision=highest)
    back_identity = (
        jnp.zeros_like(grad_carry_state),
        jnp.zeros_like(grad_carry_total),
        jnp.full_like(carry_label, -1.0),
    )
    grad_element_state, grad_element_total, unused = carried_in_2(
        (grad_carry_state, grad_carry_total, carry_label), "seq", combine_states, back_identity
    )
    keep_wide = keep[:, :, None, None].astype(jnp.float32)
    element_phi = keep_wide * (
        jnp.einsum("rjgh,rgfh->rjgf", value_wide[:, :shard], grad_element_state, precision=highest)
        + grad_element_total[:, None]
    )
    element_value = keep_wide * jnp.einsum(
        "rjgf,rgfh->rjgh",
        all_phi[:, :shard].astype(jnp.float32),
        grad_element_state,
        precision=highest,
    )
    grad_phi_all = grad_phi_all + jnp.concatenate(
        [element_phi, jnp.zeros_like(element_phi[:, :window])], axis=1
    )
    grad_value_all = grad_value_all + jnp.concatenate(
        [element_value, jnp.zeros_like(element_value[:, :window])], axis=1
    )
    sent = (grad_key_all[:, :window], grad_value_all[:, :window], grad_phi_all[:, :window])
    back_key, back_value, back_phi = (
        shifted(sent[0].astype(jnp.bfloat16), "seq", -1).astype(jnp.float32),
        shifted(sent[1].astype(jnp.bfloat16), "seq", -1).astype(jnp.float32),
        shifted(sent[2].astype(jnp.bfloat16), "seq", -1).astype(jnp.float32),
    )

    def own(grads_all, returned):
        filler = jnp.zeros((row_count, shard - window) + returned.shape[2:], jnp.float32)
        return grads_all[:, window:] + jnp.concatenate([filler, returned], axis=1)

    grad_key_rot = own(grad_key_all, back_key)
    grad_value_rot = own(grad_value_all, back_value)
    grad_phi_key = own(grad_phi_all, back_phi)
    grad_proj_q = feature_back(
        grad_phi_q.reshape(row_count, shard, heads_here, query_features.shape[-1]),
        query_plus,
        query_minus,
    ).astype(jnp.bfloat16)
    grad_proj_k = feature_back(grad_phi_key, key_plus, key_minus).astype(jnp.bfloat16)
    grad_query_rot = grad_query_att.reshape(row_count, shard, heads_here, size) + jnp.einsum(
        "rthf,hdf->rthd", grad_proj_q, hedgehog_query_weight, preferred_element_type=jnp.float32
    )
    grad_key_rot = grad_key_rot + jnp.einsum(
        "rthf,hdf->rthd", grad_proj_k, hedgehog_key_weight, preferred_element_type=jnp.float32
    )
    grad_map_query = jnp.einsum(
        "rthd,rthf->hdf", query_rot, grad_proj_q, preferred_element_type=jnp.float32
    )
    grad_map_key = jnp.einsum(
        "rthd,rthf->hdf", key_rot, grad_proj_k, preferred_element_type=jnp.float32
    )
    grad_query_lin = (
        unrotate(grad_query_rot, cosine_table, sine_table)
        .astype(jnp.bfloat16)
        .reshape(tokens_here, heads_here * size)
    )
    grad_key_lin = (
        unrotate(grad_key_rot, cosine_table, sine_table)
        .astype(jnp.bfloat16)
        .reshape(tokens_here, kv_here * size)
    )
    grad_value_lin = grad_value_rot.astype(jnp.bfloat16).reshape(tokens_here, kv_here * size)
    grad_w_query = left_dot(normalized_input, grad_query_lin)
    grad_w_key = left_dot(normalized_input, grad_key_lin)
    grad_w_value = left_dot(normalized_input, grad_value_lin)
    query_widened = grad_query_lin.astype(jnp.float32)
    key_widened = grad_key_lin.astype(jnp.float32)
    value_gradient_widened = grad_value_lin.astype(jnp.float32)
    adapter_query_gradient = adapter_scale * precise_product(
        lowrank_input[:, :adapter_rank].T, query_widened
    )
    adapter_key_gradient = adapter_scale * precise_product(
        lowrank_input[:, adapter_rank : 2 * adapter_rank].T, key_widened
    )
    adapter_value_gradient = adapter_scale * precise_product(
        lowrank_input[:, 2 * adapter_rank :].T, value_gradient_widened
    )
    lowrank_gradient = adapter_scale * jnp.concatenate(
        [
            precise_product(query_widened, adapter_query_weight.astype(jnp.float32).T),
            precise_product(key_widened, adapter_key_weight.astype(jnp.float32).T),
            precise_product(value_gradient_widened, adapter_value_weight.astype(jnp.float32).T),
        ],
        axis=1,
    )
    normed_part = (
        right_dot(grad_query_lin, complete_query)
        + right_dot(grad_key_lin, complete_key)
        + right_dot(grad_value_lin, complete_value)
    )
    normalized_gradient, lowrank_gradient_combined = (
        lax.psum(normed_part.astype(jnp.bfloat16), "head").astype(jnp.float32),
        lax.psum(lowrank_gradient.astype(jnp.bfloat16), "head").astype(jnp.float32),
    )
    normalized_gradient = normalized_gradient + precise_product(
        lowrank_gradient_combined, adapter_down_weight.astype(jnp.float32).T
    )
    adapter_down_gradient = precise_product(
        normalized_input.astype(jnp.float32).T, lowrank_gradient_combined
    )
    grad_gain_one = jnp.sum(normalized_gradient * unit_one, axis=0)
    inner_one = normalized_gradient * first_norm_gain.astype(jnp.float32)
    grad_tokens_rows = grad_hidden + scale_one * (
        inner_one - unit_one * jnp.mean(inner_one * unit_one, axis=-1, keepdims=True)
    )
    big = (
        lax.psum_scatter(
            grad_w_query.astype(jnp.bfloat16), "seq", scatter_dimension=0, tiled=True
        ).astype(jnp.float32),
        lax.psum_scatter(
            grad_w_key.astype(jnp.bfloat16), "seq", scatter_dimension=0, tiled=True
        ).astype(jnp.float32),
        lax.psum_scatter(
            grad_w_value.astype(jnp.bfloat16), "seq", scatter_dimension=0, tiled=True
        ).astype(jnp.float32),
        lax.psum_scatter(
            grad_w_out.astype(jnp.bfloat16), "seq", scatter_dimension=1, tiled=True
        ).astype(jnp.float32),
        lax.psum_scatter(
            grad_w_gate.astype(jnp.bfloat16), "seq", scatter_dimension=0, tiled=True
        ).astype(jnp.float32),
        lax.psum_scatter(
            grad_w_up.astype(jnp.bfloat16), "seq", scatter_dimension=0, tiled=True
        ).astype(jnp.float32),
        lax.psum_scatter(
            grad_w_down.astype(jnp.bfloat16), "seq", scatter_dimension=1, tiled=True
        ).astype(jnp.float32),
    )
    small_value = (
        lax.psum(grad_gain_one.astype(jnp.bfloat16), "seq").astype(jnp.float32),
        lax.psum(grad_gain_two.astype(jnp.bfloat16), "seq").astype(jnp.float32),
        lax.psum(adapter_down_gradient.astype(jnp.bfloat16), "seq").astype(jnp.float32),
        lax.psum(adapter_query_gradient.astype(jnp.bfloat16), "seq").astype(jnp.float32),
        lax.psum(adapter_key_gradient.astype(jnp.bfloat16), "seq").astype(jnp.float32),
        lax.psum(adapter_value_gradient.astype(jnp.bfloat16), "seq").astype(jnp.float32),
        lax.psum(adapter_output_down_gradient.astype(jnp.bfloat16), "seq").astype(jnp.float32),
        lax.psum(adapter_output_up_gradient.astype(jnp.bfloat16), "seq").astype(jnp.float32),
        lax.psum(grad_map_query.astype(jnp.bfloat16), "seq").astype(jnp.float32),
        lax.psum(grad_map_key.astype(jnp.bfloat16), "seq").astype(jnp.float32),
    )
    first_gain_sum, second_gain_sum, adapter_down_sum = (
        small_value[0],
        small_value[1],
        small_value[2],
    )
    adapter_query_sum, adapter_key_sum, adapter_value_sum = (
        small_value[3],
        small_value[4],
        small_value[5],
    )
    sum_out_down, sum_out_up, sum_map_query, sum_map_key = (
        small_value[6],
        small_value[7],
        small_value[8],
        small_value[9],
    )
    return (
        layer_rows.reshape(row_count, shard, width),
        grad_tokens_rows.reshape(row_count, shard, width),
        first_gain_sum,
        second_gain_sum,
        big[0],
        big[1],
        big[2],
        big[3],
        big[4],
        big[5],
        big[6],
        adapter_down_sum,
        adapter_query_sum,
        adapter_key_sum,
        adapter_value_sum,
        sum_out_down,
        sum_out_up,
        sum_map_query,
        sum_map_key,
    )


def solution(mesh):
    in_specs = (
        P(None, "seq", None),
        P(None, "seq", None),
        P(),
        P(),
        P("seq", "head"),
        P("seq", "head"),
        P("seq", "head"),
        P("head", "seq"),
        P("seq", "head"),
        P("seq", "head"),
        P("head", "seq"),
        P(),
        P(None, "head"),
        P(None, "head"),
        P(None, "head"),
        P("head", None),
        P(),
        P("head", None, None),
        P("head", None, None),
        P(),
    )
    out_specs = (
        P(None, "seq", None),
        P(None, "seq", None),
        P(),
        P(),
        P("seq", "head"),
        P("seq", "head"),
        P("seq", "head"),
        P("head", "seq"),
        P("seq", "head"),
        P("seq", "head"),
        P("head", "seq"),
        P(),
        P(None, "head"),
        P(None, "head"),
        P(None, "head"),
        P("head", None),
        P(),
        P("head", None, None),
        P("head", None, None),
    )
    return jax.shard_map(body, mesh=mesh, in_specs=in_specs, out_specs=out_specs, check_vma=False)
```

profile of v0, /device:TPU:0, one launch (start us, length us, event | category | flops | bytes accessed | tf_op | source)
XLA Modules:
  0.0 2271.7 jit_solution(1570934032189038193)
XLA Ops:
  11.9 33.9 %all_gather.56 = bf16[2048,128]{1,0:T(8,128)(2,1)S(1)} all-gather(bf16[256,128]{1,0:T(8,128)(2,1)S(1)} %copy-done.102), channel_id=1, replica_groups=mesh['seq'=8,'head'=4] {'seq'}, dimensions={0}, use_global_device_ids=true | all-gather | bytes 589824 | tf_op jit(solution)/shard_map/all_gather | solution.py:171
  57.9 38.9 %all_gather.55 = bf16[2048,128]{1,0:T(8,128)(2,1)S(1)} all-gather(bf16[256,128]{1,0:T(8,128)(2,1)S(1)} %copy-done.103), channel_id=1, replica_groups=mesh['seq'=8,'head'=4] {'seq'}, dimensions={0}, use_global_device_ids=true | all-gather | bytes 589824 | tf_op jit(solution)/shard_map/all_gather | solution.py:172
  141.5 33.2 %all-gather.2 = f32[64,2,128]{2,1,0:T(2,128)} all-gather(f32[8,2,128]{2,1,0:T(2,128)S(1)} %copy.139), channel_id=4, replica_groups=mesh['seq'=8,'head'=4] {'seq'}, dimensions={0}, use_global_device_ids=true | all-gather | bytes 73728 | tf_op jit(solution)/shard_map/all_gather | solution.py:23
  206.3 58.7 %while.35 = (s32[]{:T(128)}, f32[8,2,128,64]{3,2,1,0:T(8,128)}, f32[8,2,128]{2,1,0:T(2,128)S(1)}, f32[8]{0:T(128)}, s32[]{:T(128)}, /*index=5*/f32[8,8]{1,0:T(8,...) while((s32[]{:T(128)}, f32[8,2,128,64]{3,2,1,0:T(8,128)}, ...), condition=%wide.region_11.12_spmd.clone, body=%wide.region_10.11_spmd.clone.sunk | while | flops 665660 | bytes 3694942 | solution.py:32
  305.7 136.6 %all-reduce.17.cloned.1.call-done = f32[1024,2048]{1,0:T(8,128)} async-done(((f32[1024,2048]{1,0:T(8,128)}), f32[1024,2048]{1,0:T(8,128)}) %all-reduce.17.cloned.1.call-update) | async-done | bytes 8388624 | tf_op jit(solution)/shard_map/psum | solution.py:286
  456.9 112.5 %all-gather.18.cloned.1.call-done = bf16[2048,2048]{1,0:T(8,128)(2,1)} async-done(((bf16[256,2048]{1,0:T(8,128)(2,1)}), bf16[2048,2048]{1,0:T(8,128)(2,1)}) %all-gather.18.cloned.1.call-update) | async-done | bytes 8388624 | tf_op jit(solution)/shard_map/all_gather | solution.py:174
  583.8 110.7 %all-gather.20.cloned.1.call-done = bf16[2048,2048]{1,0:T(8,128)(2,1)} async-done(((bf16[256,2048]{1,0:T(8,128)(2,1)}), bf16[2048,2048]{1,0:T(8,128)(2,1)}) %all-gather.20.cloned.1.call-update) | async-done | bytes 8388624 | tf_op jit(solution)/shard_map/all_gather | solution.py:175
  709.1 111.0 %all-gather.22.cloned.1.call-done = bf16[2048,2048]{1,0:T(8,128)(2,1)} async-done(((bf16[2048,256]{1,0:T(8,128)(2,1)}), bf16[2048,2048]{1,0:T(8,128)(2,1)}) %all-gather.22.cloned.1.call-update) | async-done | bytes 8388624 | tf_op jit(solution)/shard_map/all_gather | solution.py:176
  820.1 22.0 multiply_convert_fusion
  870.7 18.8 all-reduce.7
  904.1 116.9 %all-reduce.19.cloned.1.call-done = f32[1024,2048]{1,0:T(8,128)} async-done(((f32[1024,2048]{1,0:T(8,128)}), f32[1024,2048]{1,0:T(8,128)}) %all-reduce.19.cloned.1.call-update) | async-done | bytes 8388624 | tf_op jit(solution)/shard_map/psum | solution.py:313
  1102.7 39.6 %all-gather.5 = bf16[64,2,128]{2,1,0:T(2,128)(2,1)} all-gather(bf16[8,2,128]{2,1,0:T(2,128)(2,1)S(1)} %convert_element_type.365), channel_id=7, replica_groups=mesh['seq'=8,'head'=4] {'seq'}, dimensions={0}, use_global_device_ids=true | all-gather | bytes 36864 | tf_op jit(solution)/shard_map/all_gather | solution.py:40
  1147.8 43.4 %while.34 = (s32[]{:T(128)}, f32[8,2,128,64]{3,2,1,0:T(8,128)S(1)}, f32[8,2,128]{2,1,0:T(2,128)S(1)}, f32[8]{0:T(128)}, s32[]{:T(128)}, /*index=5*/bf16[8,8]{1,0...) while((s32[]{:T(128)}, f32[8,2,128,64]{3,2,1,0:T(8,128)S(1)}, ...), condition=%wide.region_24.25_spmd, body=%wide.region_23.24_spmd.sunk | while | flops 532534 | bytes 2380131 | solution.py:57
  1288.6 92.7 %all-reduce.25.cloned.1.call-done = (bf16[1024,2048]{1,0:T(8,128)(2,1)}, bf16[1024,2048]{1,0:T(8,128)(2,1)}) async-done(((bf16[1024,2048]{1,0:T(8,128)(2,1)}, bf16[1024,2048]{1,0:T(8,128)(2,1)}), (bf16[1024,2048]{1,0:T(8,128)(2,1)}, bf16[1024,2048]{1,0:T(8,128)(2,1)})) %all-reduce.25.cloned.1.call-update) | async-done | bytes 8388624 | tf_op jit(solution)/shard_map/psum | solution.py:301
  1432.1 24.5 %all-reduce.23.cloned.1.call-done = (bf16[2048,24]{0,1:T(8,128)(2,1)}, bf16[8,64,64]{2,1,0:T(8,128)(2,1)}) async-done(((bf16[2048,24]{0,1:T(8,128)(2,1)}, bf16[8,64,64]{2,1,0:T(8,128)(2,1)}), (bf16[2048,24]{0,1:T(8,128)(2,1)}, bf16[8,64,64]{2,1,0:T(8,128)(2,1)})) %all-reduce.23.cloned.1.call-update) | async-done | bytes 163856 | tf_op jit(solution)/shard_map/psum | solution.py:518
  1459.9 68.7 %reduce-scatter.14.cloned.1.call-done = bf16[512,256]{1,0:T(8,128)(2,1)} async-done(((bf16[512,2048]{1,0:T(8,128)(2,1)}), bf16[512,256]{1,0:T(8,128)(2,1)}) %reduce-scatter.14.cloned.1.call-update) | async-done | bytes 262160 | tf_op jit(solution)/shard_map/reduce_scatter | solution.py:502
  1530.4 69.7 %reduce-scatter.8.cloned.1.call-done = bf16[256,512]{1,0:T(8,128)(2,1)} async-done(((bf16[2048,512]{1,0:T(8,128)(2,1)}), bf16[256,512]{1,0:T(8,128)(2,1)}) %reduce-scatter.8.cloned.1.call-update) | async-done | bytes 262160 | tf_op jit(solution)/shard_map/reduce_scatter | solution.py:493
  1601.9 62.7 %reduce-scatter.12.cloned.1.call-done = bf16[256,128]{1,0:T(8,128)(2,1)} async-done(((bf16[2048,128]{1,0:T(8,128)(2,1)}), bf16[256,128]{1,0:T(8,128)(2,1)}) %reduce-scatter.12.cloned.1.call-update) | async-done | bytes 65552 | tf_op jit(solution)/shard_map/reduce_scatter | solution.py:499
  1666.1 63.2 %reduce-scatter.10.cloned.1.call-done = bf16[256,128]{1,0:T(8,128)(2,1)} async-done(((bf16[2048,128]{1,0:T(8,128)(2,1)}), bf16[256,128]{1,0:T(8,128)(2,1)}) %reduce-scatter.10.cloned.1.call-update) | async-done | bytes 65552 | tf_op jit(solution)/shard_map/reduce_scatter | solution.py:496
  1730.8 19.6 fusion.26
  1750.5 55.3 %all-reduce.21.cloned.1.call-done = (bf16[2048]{0:T(1024)(128)(2,1)}, bf16[2048]{0:T(1024)(128)(2,1)}, bf16[8,512]{1,0:T(8,128)(2,1)}, bf16[8,128]{1,0:T(8,128)(...) async-done(((bf16[2048]{0:T(1024)(128)(2,1)}, bf16[2048]{0:T(1024)(128)(2,1)}, ...) | async-done | bytes 77840 | tf_op jit(solution)/shard_map/psum | solution.py:516
  1816.2 141.8 %reduce-scatter.16.cloned.1.call-done = bf16[256,2048]{1,0:T(8,128)(2,1)} async-done(((bf16[2048,2048]{1,0:T(8,128)(2,1)}), bf16[256,2048]{1,0:T(8,128)(2,1)}) %reduce-scatter.16.cloned.1.call-update) | async-done | bytes 1048592 | tf_op jit(solution)/shard_map/reduce_scatter | solution.py:505
  1960.8 148.8 %reduce-scatter.18.cloned.1.call-done = bf16[256,2048]{1,0:T(8,128)(2,1)} async-done(((bf16[2048,2048]{1,0:T(8,128)(2,1)}), bf16[256,2048]{1,0:T(8,128)(2,1)}) %reduce-scatter.18.cloned.1.call-update) | async-done | bytes 1048592 | tf_op jit(solution)/shard_map/reduce_scatter | solution.py:508
  2112.4 149.7 %reduce-scatter.20.cloned.1.call-done = bf16[2048,256]{1,0:T(8,128)(2,1)} async-done(((bf16[2048,2048]{1,0:T(8,128)(2,1)}), bf16[2048,256]{1,0:T(8,128)(2,1)}) %reduce-scatter.20.cloned.1.call-update) | async-done | bytes 1048592 | tf_op jit(solution)/shard_map/reduce_scatter | solution.py:511
  (577 shorter events, 583.4 us)
Async XLA Ops:
  7.2 167.4 %all-gather.14.cloned.1.call-start = ((), (), s32[]{:S(2)}) async-start(), calls=%async_computation.7 | async-start | bytes 2359296 | tf_op jit(solution)/shard_map/all_gather | solution.py:170
  8.0 198.4 %all-gather.24.cloned.1.call-start = ((), (), s32[]{:S(2)}) async-start(), calls=%async_computation.21 | async-start | bytes 4718592 | tf_op jit(solution)/shard_map/all_gather | solution.py:23
  53.3 53.9 %collective-permute-start.2 = (bf16[8,64,2,128]{1,3,0,2:T(8,128)(2,1)S(1)}, bf16[8,64,2,128]{1,3,0,2:T(8,128)(2,1)}, u32[]{:S(2)}, u32[]{:S(2)}) collective-permute-start(bf16[8,64,2,128]{1,3,0,2:T(8,128)(2,1)S(1)} %pad_maximum_fusion.2), channel_id=1, source_target_pairs={{0,4},{4,8},{8,12},{12,16},{16,20},{20,24},{24,28},{1,5},{5,9},{9,... | collective-permute-start | bytes 786440 | tf_op jit(solution)/shard_map/ppermute | solution.py:18
  112.4 171.3 %all-gather.16.cloned.1.call-start = ((), (), s32[]{:S(2)}) async-start(), calls=%async_computation.8 | async-start | bytes 2359296 | tf_op jit(solution)/shard_map/all_gather | solution.py:173
  113.3 155.5 %collective-permute-start.1 = (bf16[8,64,2,64]{1,3,2,0:T(8,128)(2,1)}, bf16[8,64,2,64]{1,3,2,0:T(8,128)(2,1)}, u32[]{:S(2)}, u32[]{:S(2)}) collective-permute-start(bf16[8,64,2,64]{1,3,2,0:T(8,128)(2,1)} %slice.130), channel_id=1, source_target_pairs={{0,4},{4,8},{8,12},{12,16},{16,20},{20,24},{24,28},{1,5},{5,9},{9,... | collective-permute-start | bytes 393224 | tf_op jit(solution)/shard_map/ppermute | solution.py:18
  118.4 323.8 %all-reduce.17.cloned.1.call-start = ((), (), s32[]{:S(2)}) async-start(), calls=%async_computation.9 | async-start | bytes 16777216 | tf_op jit(solution)/shard_map/psum | solution.py:286
  291.9 277.5 %all-gather.18.cloned.1.call-start = ((), (), s32[]{:S(2)}) async-start(), calls=%async_computation.10 | async-start | bytes 9437184 | tf_op jit(solution)/shard_map/all_gather | solution.py:174
  292.4 402.0 %all-gather.20.cloned.1.call-start = ((), (), s32[]{:S(2)}) async-start(), calls=%async_computation.11 | async-start | bytes 9437184 | tf_op jit(solution)/shard_map/all_gather | solution.py:175
  293.0 527.1 %all-gather.22.cloned.1.call-start = ((), (), s32[]{:S(2)}) async-start(), calls=%async_computation.12 | async-start | bytes 9437184 | tf_op jit(solution)/shard_map/all_gather | solution.py:176
  293.8 727.2 %all-reduce.19.cloned.1.call-start = ((), (), s32[]{:S(2)}) async-start(), calls=%async_computation.13 | async-start | bytes 16777216 | tf_op jit(solution)/shard_map/psum | solution.py:313
  869.8 277.4 %all-gather.26.cloned.1.call-start = ((), (), s32[]{:S(2)}) async-start(), calls=%async_computation.22 | async-start | bytes 2359296 | tf_op jit(solution)/shard_map/all_gather | solution.py:40
  1072.3 308.9 %all-reduce.25.cloned.1.call-start = ((), (), s32[]{:S(2)}) async-start(), calls=%async_computation.25 | async-start | bytes 16777216 | tf_op jit(solution)/shard_map/psum | solution.py:301
  1100.5 122.0 %collective-permute-start.3 = (bf16[8,64,2,64]{1,3,2,0:T(8,128)(2,1)}, bf16[8,64,2,64]{1,3,2,0:T(8,128)(2,1)}, u32[]{:S(2)}, u32[]{:S(2)}) collective-permute-start(bf16[8,64,2,64]{1,3,2,0:T(8,128)(2,1)} %slice.223), channel_id=1, source_target_pairs={{4,0},{8,4},{12,8},{16,12},{20,16},{24,20},{28,24},{5,1},{9,5},{13... | collective-permute-start | bytes 393224 | tf_op jit(solution)/shard_map/ppermute | solution.py:18
  1201.6 19.5 collective-permute-start.4
  1211.7 8.9 collective-permute-start.5
  1228.9 227.8 %all-reduce.23.cloned.1.call-start = ((), (), s32[]{:S(2)}) async-start(), calls=%async_computation.24 | async-start | bytes 458752 | tf_op jit(solution)/shard_map/psum | solution.py:518
  1256.0 272.6 %reduce-scatter.14.cloned.1.call-start = ((), (), s32[]{:S(2)}) async-start(), calls=%async_computation.17 | async-start | bytes 2359296 | tf_op jit(solution)/shard_map/reduce_scatter | solution.py:502
  1262.0 338.1 %reduce-scatter.8.cloned.1.call-start = ((), (), s32[]{:S(2)}) async-start(), calls=%async_computation.14 | async-start | bytes 2359296 | tf_op jit(solution)/shard_map/reduce_scatter | solution.py:493
  1271.5 393.0 %reduce-scatter.12.cloned.1.call-start = ((), (), s32[]{:S(2)}) async-start(), calls=%async_computation.16 | async-start | bytes 589824 | tf_op jit(solution)/shard_map/reduce_scatter | solution.py:499
  1277.5 451.8 %reduce-scatter.10.cloned.1.call-start = ((), (), s32[]{:S(2)}) async-start(), calls=%async_computation.15 | async-start | bytes 589824 | tf_op jit(solution)/shard_map/reduce_scatter | solution.py:496
  1286.8 519.0 %all-reduce.21.cloned.1.call-start = ((), (), s32[]{:S(2)}) async-start(), calls=%async_computation.23 | async-start | bytes 188416 | tf_op jit(solution)/shard_map/psum | solution.py:516
  1389.2 568.8 %reduce-scatter.16.cloned.1.call-start = ((), (), s32[]{:S(2)}) async-start(), calls=%async_computation.18 | async-start | bytes 9437184 | tf_op jit(solution)/shard_map/reduce_scatter | solution.py:505
  1403.6 706.0 %reduce-scatter.18.cloned.1.call-start = ((), (), s32[]{:S(2)}) async-start(), calls=%async_computation.19 | async-start | bytes 9437184 | tf_op jit(solution)/shard_map/reduce_scatter | solution.py:508
  1417.7 844.3 %reduce-scatter.20.cloned.1.call-start = ((), (), s32[]{:S(2)}) async-start(), calls=%async_computation.20 | async-start | bytes 9437184 | tf_op jit(solution)/shard_map/reduce_scatter | solution.py:511
  (132 other events, 4553.2 us)
Sparse Core Ops, SparseCore 0:
  10.2 57.3 all-gather.13
  112.5 75.5 all-gather.23
  190.1 49.3 all-gather.15
  292.0 150.2 all-reduce.16
  444.2 125.0 all-gather.17
  571.3 123.1 all-gather.19
  696.5 123.5 all-gather.21
  869.9 151.0 all-reduce.18
  1072.4 55.1 all-gather.25
  1229.0 152.2 all-reduce.24
  1385.9 70.7 all-reduce.22
  1461.1 67.4 reduce-scatter.13
  1533.1 66.9 reduce-scatter.7
  1603.7 60.8 reduce-scatter.11
  1668.3 60.9 reduce-scatter.9
  1735.7 70.0 all-reduce.20
  1809.7 148.2 reduce-scatter.15
  1961.5 148.0 reduce-scatter.17
  2113.6 148.3 reduce-scatter.19
where the time goes:
time: 2280 us; the launch traced here: 2270 us
  waiting for transfers between devices  1480 us (65%)
  matrix products  310 us (14%)
  blocking collectives  207 us (9%)
  other arithmetic  160 us (7%)
  local copies, waits for them, and re-layouts  85.1 us (4%)
    reduce_scatter x1, waiting for transfers between devices, body(): lax.psum_scatter(grad_w_down.astype(jnp.bfloat16), 'seq', scatter_dimensi...  150 us
    reduce_scatter x1, waiting for transfers between devices, body(): lax.psum_scatter(grad_w_up.astype(jnp.bfloat16), 'seq', scatter_dimension...  149 us
    reduce_scatter x1, waiting for transfers between devices, body(): lax.psum_scatter(grad_w_gate.astype(jnp.bfloat16), 'seq', scatter_dimensi...  142 us
    psum x1, waiting for transfers between devices, body(): output_sum, lowrank_output = lax.psum((out_part, lowrank_slice), 'head')  137 us
    psum x1, waiting for transfers between devices, body(): grad_normed_two = lax.psum(normed_two_part, 'head')  117 us
    all_gather x1, waiting for transfers between devices, body(): lax.all_gather(weights[4], 'seq', axis=0, tiled=True)  112 us
    all_gather x1, waiting for transfers between devices, body(): lax.all_gather(weights[6], 'seq', axis=1, tiled=True)  111 us
    all_gather x1, waiting for transfers between devices, body(): lax.all_gather(weights[5], 'seq', axis=0, tiled=True)  111 us
  transfers between devices with their start and end apart: 25, of which 17 were waited for; matrix products, arithmetic and copies ran while one was open for 19% of the time, Pallas kernels for 0%

commit v1 on v0

--- a/solution.py
+++ b/solution.py
@@ -124,6 +124,120 @@
         return jnp.where(vacant, first, jnp.where(linked, first + second, second))
 
     return (choose(state_a, state_b), choose(total_a, total_b), jnp.where(empty, label_a, label_b))
+
+
+def ring_tables(count):
+    order = list(range(0, count, 2)) + list(range(count - 1, 0, -2))
+    place = [order.index(i) for i in range(count)]
+    return order, place
+
+
+def ring_move(block, step):
+    order, _ = ring_tables(lax.axis_size("seq"))
+    count = len(order)
+    return lax.ppermute(block, "seq", [(order[i], order[(i + step) % count]) for i in range(count)])
+
+
+def ring_index(offset):
+    order, place = ring_tables(lax.axis_size("seq"))
+    mine = jnp.asarray(place, jnp.int32)[lax.axis_index("seq")]
+    return jnp.asarray(order, jnp.int32)[(mine + offset) % len(order)]
+
+
+def after(value, *others):
+    return lax.optimization_barrier((value,) + others)[0]
+
+
+def ring_gather(own):
+    half = lax.axis_size("seq") // 2
+    found = {0: own}
+    up = down = own
+    for step in range(1, half):
+        up, down = ring_move(up, 1), ring_move(down, -1)
+        found[-step], found[step] = up, down
+    cut = own.shape[0] // 2
+    found[half] = (ring_move(up[:cut], 1), ring_move(down[cut:], -1))
+    return found
+
+
+def assemble(found, first, last):
+    count = lax.axis_size("seq")
+    rows = found[0].shape[0]
+    whole = jnp.zeros((count * rows, last - first), found[0].dtype)
+    for offset, block in found.items():
+        at = ring_index(offset) * rows
+        if isinstance(block, tuple):
+            for part in block:
+                whole = lax.dynamic_update_slice(whole, part[:, first:last], (at, 0))
+                at = at + part.shape[0]
+        else:
+            whole = lax.dynamic_update_slice(whole, block[:, first:last], (at, 0))
+    return whole
+
+
+def ring_scatter(grads, rows):
+    half = lax.axis_size("seq") // 2
+    cut = rows // 2
+
+    def own(offset):
+        at = ring_index(offset) * rows
+        return jnp.concatenate(
+            [lax.dynamic_slice_in_dim(part, at, rows, 0) for part in grads], axis=1
+        )
+
+    far = own(half)
+    up, down = ring_move(far[:cut], 1), ring_move(far[cut:], -1)
+    for step in range(half - 1, 0, -1):
+        above, below = own(step), own(-step)
+        if step == half - 1:
+            up = jnp.concatenate([above[:cut] + up, above[cut:]], axis=0)
+            down = jnp.concatenate([below[:cut], below[cut:] + down], axis=0)
+        else:
+            up, down = above + up, below + down
+        up, down = ring_move(up, 1), ring_move(down, -1)
+    mine = own(0).astype(jnp.float32)
+    return mine + up.astype(jnp.float32) + down.astype(jnp.float32)
+
+
+def core_swap(block):
+    count = lax.axis_size("head")
+    return lax.ppermute(block, "head", [(i, i ^ 1) for i in range(count)])
+
+
+def chip_move(block, step):
+    count = lax.axis_size("head")
+    return lax.ppermute(block, "head", [(i, (i + 2 * step) % count) for i in range(count)])
+
+
+def head_scatter(part):
+    chips = lax.axis_size("head") // 2
+    place = lax.axis_index("head")
+    chip, core = place // 2, place % 2
+    rows = part.shape[0] // (2 * chips)
+    split = part.reshape(chips, 2, rows, part.shape[1])
+    theirs = core_swap(lax.dynamic_index_in_dim(split, 1 - core, 1, False))
+    both = lax.dynamic_index_in_dim(split, core, 1, False).astype(jnp.float32) + theirs
+    total = lax.dynamic_index_in_dim(both, chip, 0, False)
+    for step in range(1, chips):
+        sent = lax.dynamic_index_in_dim(both, (chip + step) % chips, 0, False)
+        total = total + chip_move(sent.astype(part.dtype), step)
+    return total
+
+
+def head_gather(own):
+    chips = lax.axis_size("head") // 2
+    place = lax.axis_index("head")
+    chip, core = place // 2, place % 2
+    whole = jnp.zeros((2 * chips,) + own.shape, own.dtype)
+    for step in range(chips):
+        block = chip_move(own, step) if step else own
+        at = 2 * ((chip - step + chips) % chips)
+        whole = lax.dynamic_update_index_in_dim(whole, block, at + core, 0)
+        whole = lax.dynamic_update_index_in_dim(whole, core_swap(block), at + 1 - core, 0)
+    return whole.reshape((2 * chips * own.shape[0],) + own.shape[1:])
+
+
+MLP_CHUNKS = 4
 
 
 def body(
@@ -157,43 +271,42 @@
     size = hedgehog_query_weight.shape[1]
     adapter_rank = adapter_query_weight.shape[0]
     tokens_here = row_count * shard
-    weights = (
-        query_weight,
-        key_weight,
-        value_weight,
-        output_weight,
-        gate_weight,
-        up_weight,
-        down_weight,
-    )
-    gathered = (
-        lax.all_gather(weights[0], "seq", axis=0, tiled=True),
-        lax.all_gather(weights[1], "seq", axis=0, tiled=True),
-        lax.all_gather(weights[2], "seq", axis=0, tiled=True),
-        lax.all_gather(weights[3], "seq", axis=1, tiled=True),
-        lax.all_gather(weights[4], "seq", axis=0, tiled=True),
-        lax.all_gather(weights[5], "seq", axis=0, tiled=True),
-        lax.all_gather(weights[6], "seq", axis=1, tiled=True),
-    )
-    complete_query, complete_key, complete_value, full_out, full_gate, full_up, full_down = gathered
+    block_rows = query_weight.shape[0]
+    hidden_units = gate_weight.shape[1]
+    chunk = hidden_units // MLP_CHUNKS
+    down_turned = down_weight.T
+    qkv_found = ring_gather(jnp.concatenate([query_weight, key_weight, value_weight], axis=1))
+    query_width, key_width = query_weight.shape[1], key_weight.shape[1]
+    out_found = ring_gather(after(output_weight.T, qkv_found[1]))
+    mlp_found = []
+    earlier = out_found[1]
+    for turn in range(MLP_CHUNKS):
+        span = slice(turn * chunk, (turn + 1) * chunk)
+        payload = jnp.concatenate(
+            [gate_weight[:, span], up_weight[:, span], down_turned[:, span]], axis=1
+        )
+        mlp_found.append(ring_gather(after(payload, earlier)))
+        earlier = mlp_found[-1][2]
+    complete_qkv = assemble(qkv_found, 0, query_width + 2 * key_width)
+    out_turned = assemble(out_found, 0, output_weight.shape[0])
+    adapters = jnp.zeros((3 * adapter_rank, query_width + 2 * key_width), jnp.bfloat16)
+    adapters = lax.dynamic_update_slice(adapters, adapter_query_weight, (0, 0))
+    adapters = lax.dynamic_update_slice(adapters, adapter_key_weight, (adapter_rank, query_width))
+    adapters = lax.dynamic_update_slice(
+        adapters, adapter_value_weight, (2 * adapter_rank, query_width + key_width)
+    )
     flattened = tokens.reshape(tokens_here, width).astype(jnp.float32)
     scale_one = lax.rsqrt(jnp.mean(flattened * flattened, axis=-1, keepdims=True) + epsilon)
     unit_one = flattened * scale_one
     normalized_input = (unit_one * first_norm_gain.astype(jnp.float32)).astype(jnp.bfloat16)
     lowrank_input = forward_product(normalized_input, adapter_down_weight)
-    query_linear = forward_product(
-        normalized_input, complete_query
-    ) + adapter_scale * precise_product(
-        lowrank_input[:, :adapter_rank], adapter_query_weight.astype(jnp.float32)
-    )
-    key_linear = forward_product(normalized_input, complete_key) + adapter_scale * precise_product(
-        lowrank_input[:, adapter_rank : 2 * adapter_rank], adapter_key_weight.astype(jnp.float32)
-    )
-    value_linear = forward_product(
-        normalized_input, complete_value
-    ) + adapter_scale * precise_product(
-        lowrank_input[:, 2 * adapter_rank :], adapter_value_weight.astype(jnp.float32)
-    )
+    lowrank_low = lowrank_input.astype(jnp.bfloat16)
+    linear = forward_product(normalized_input, complete_qkv) + adapter_scale * forward_product(
+        lowrank_low, adapters
+    )
+    query_linear = linear[:, :query_width]
+    key_linear = linear[:, query_width : query_width + key_width]
+    value_linear = linear[:, query_width + key_width :]
     positions = seq_index * shard + jnp.arange(shard)
     cosine_table, sine_table = rope_tables(positions, size)
     query_rot = apply_rotation(
@@ -269,68 +382,71 @@
         jnp.einsum("rigcf,rjgf->rgcij", phi_grouped, all_phi, preferred_element_type=jnp.float32),
         0.0,
     )
-    value_wide = all_value.astype(jnp.float32)
+    value_wide = all_value
     phi_wide = phi_grouped.astype(jnp.float32)
-    num_linear = jnp.einsum("rgcij,rjgh->rigch", kernel, value_wide, precision=highest)
+    num_linear = jnp.einsum("rgcij,rjgh->rigch", kernel, value_wide, preferred_element_type=jnp.float32)
     den_linear = jnp.sum(kernel, axis=-1).transpose(0, 3, 1, 2)
     reaches = (query_seg.astype(jnp.float32) == carry_label[:, None])[:, :, None, None]
-    carried = jnp.einsum("rigcf,rgfh->rigch", phi_wide, carry_state, precision=highest)
+    carried = jnp.einsum("rigcf,rgfh->rigch", phi_wide, carry_state, preferred_element_type=jnp.float32)
     num_linear = num_linear + jnp.where(reaches[..., None], carried, 0.0)
-    carried_total = jnp.einsum("rigcf,rgf->rigc", phi_wide, carry_total, precision=highest)
+    carried_total = jnp.einsum("rigcf,rgf->rigc", phi_wide, carry_total, preferred_element_type=jnp.float32)
     den_linear = den_linear + jnp.where(reaches, carried_total, 0.0)
     denominator = den_window + den_linear
     mixed = (num_window + num_linear) / denominator[..., None]
     attention_result = mixed.astype(jnp.bfloat16).reshape(tokens_here, heads_here * size)
-    out_part = forward_product(attention_result, full_out)
-    lowrank_slice = forward_product(attention_result, adapter_output_down)
-    output_sum, lowrank_output = lax.psum((out_part, lowrank_slice), "head")
-    hidden_state = (
-        flattened
-        + output_sum
-        + adapter_scale * precise_product(lowrank_output, adapter_output_up.astype(jnp.float32))
-    )
+    lowrank_output = forward_product(attention_result, adapter_output_down)
+    out_part = right_dot(attention_result, out_turned) + adapter_scale * forward_product(
+        lowrank_output.astype(jnp.bfloat16), adapter_output_up
+    )
+    own_rows = row_count // lax.axis_size("head")
+    first_row = lax.axis_index("head") * own_rows
+    own_tokens = lax.dynamic_slice_in_dim(tokens, first_row, own_rows, 0)
+    own_tokens = own_tokens.reshape(own_rows * shard, width).astype(jnp.float32)
+    own_cotangent = lax.dynamic_slice_in_dim(cotangent, first_row, own_rows, 0)
+    own_cotangent = own_cotangent.reshape(own_rows * shard, width).astype(jnp.float32)
+    hidden_state = own_tokens + head_scatter(out_part.astype(jnp.bfloat16))
     scale_two = lax.rsqrt(jnp.mean(hidden_state * hidden_state, axis=-1, keepdims=True) + epsilon)
     unit_two = hidden_state * scale_two
-    normed_rows = (unit_two * second_norm_gain.astype(jnp.float32)).astype(jnp.bfloat16)
-    gate = forward_product(normed_rows, full_gate)
-    up = forward_product(normed_rows, full_up)
-    sigmoid_gate = jax.nn.sigmoid(gate)
-    swish = gate * sigmoid_gate
-    inner = (swish * up).astype(jnp.bfloat16)
-    down_part = forward_product(inner, full_down)
-    mlp_out = lax.psum(down_part.astype(jnp.bfloat16), "head").astype(jnp.float32)
-    layer_rows = (hidden_state + mlp_out).astype(jnp.bfloat16)
+    own_normed = (unit_two * second_norm_gain.astype(jnp.float32)).astype(jnp.bfloat16)
+    normed_rows = head_gather(own_normed)
     grad_out = cotangent.reshape(tokens_here, width)
-    grad_w_down = left_dot(inner, grad_out)
-    grad_inner = right_dot(grad_out, full_down)
-    grad_gate = (grad_inner * up * sigmoid_gate * (1.0 + gate * (1.0 - sigmoid_gate))).astype(
-        jnp.bfloat16
-    )
-    grad_up = (grad_inner * swish).astype(jnp.bfloat16)
-    grad_w_gate = left_dot(normed_rows, grad_gate)
-    grad_w_up = left_dot(normed_rows, grad_up)
-    normed_two_part = right_dot(grad_gate, full_gate) + right_dot(grad_up, full_up)
-    grad_normed_two = lax.psum(normed_two_part, "head")
-    grad_out_rows = grad_out.astype(jnp.float32)
+    down_part, normed_two_part = 0.0, 0.0
+    mlp_sums = []
+    for found in mlp_found:
+        gate_up_weight = assemble(found, 0, 2 * chunk)
+        down_chunk = assemble(found, 2 * chunk, 3 * chunk)
+        grad_inner = forward_product(grad_out, down_chunk)
+        gate_up = forward_product(normed_rows, gate_up_weight)
+        gate, up = gate_up[:, :chunk], gate_up[:, chunk:]
+        sigmoid_gate = jax.nn.sigmoid(gate)
+        swish = gate * sigmoid_gate
+        inner = (swish * up).astype(jnp.bfloat16)
+        grad_gate = grad_inner * up * sigmoid_gate * (1.0 + gate * (1.0 - sigmoid_gate))
+        grad_gate_up = jnp.concatenate([grad_gate, grad_inner * swish], axis=1).astype(jnp.bfloat16)
+        normed_two_part = normed_two_part + right_dot(grad_gate_up, gate_up_weight)
+        down_part = down_part + right_dot(inner, down_chunk)
+        grad_w_gate_up = left_dot(normed_rows, grad_gate_up).astype(jnp.bfloat16)
+        grad_w_down = left_dot(grad_out, inner).astype(jnp.bfloat16)
+        mlp_sums.append(ring_scatter([grad_w_gate_up, grad_w_down], block_rows))
+    grad_normed_two = head_scatter(normed_two_part.astype(jnp.bfloat16))
+    layer_rows = head_gather(
+        (hidden_state + head_scatter(down_part.astype(jnp.bfloat16))).astype(jnp.bfloat16)
+    )
     grad_gain_two = jnp.sum(grad_normed_two * unit_two, axis=0)
     inner_two = grad_normed_two * second_norm_gain.astype(jnp.float32)
-    grad_hidden = grad_out_rows + scale_two * (
+    grad_hidden = own_cotangent + scale_two * (
         inner_two - unit_two * jnp.mean(inner_two * unit_two, axis=-1, keepdims=True)
     )
-    branch_gradient_rows = grad_hidden.astype(jnp.bfloat16)
-    adapter_output_up_gradient = adapter_scale * precise_product(
-        lowrank_output.T, branch_gradient_rows.astype(jnp.float32)
-    )
-    branch_gradient_wide = branch_gradient_rows.astype(jnp.float32)
-    grad_w_out = left_dot(attention_result, branch_gradient_rows)
-    lowrank_output_gradient = adapter_scale * precise_product(
-        branch_gradient_wide, adapter_output_up.astype(jnp.float32).T
-    )
-    adapter_output_down_gradient = precise_product(
-        attention_result.astype(jnp.float32).T, lowrank_output_gradient
-    )
-    grad_attended = right_dot(branch_gradient_rows, full_out) + precise_product(
-        lowrank_output_gradient, adapter_output_down.astype(jnp.float32).T
+    branch_gradient_rows = head_gather(grad_hidden.astype(jnp.bfloat16))
+    adapter_output_up_gradient = adapter_scale * left_dot(
+        lowrank_output.astype(jnp.bfloat16), branch_gradient_rows
+    )
+    grad_w_out = left_dot(branch_gradient_rows, attention_result).astype(jnp.bfloat16)
+    lowrank_output_gradient = adapter_scale * right_dot(branch_gradient_rows, adapter_output_up)
+    lowrank_output_gradient = lowrank_output_gradient.astype(jnp.bfloat16)
+    adapter_output_down_gradient = left_dot(attention_result, lowrank_output_gradient)
+    grad_attended = forward_product(branch_gradient_rows, out_turned) + right_dot(
+        lowrank_output_gradient, adapter_output_down
     )
     grad_mixed = (
         grad_attended.astype(jnp.bfloat16)
@@ -360,24 +476,24 @@
     )
     grad_kernel = jnp.where(
         older,
-        jnp.einsum("rigch,rjgh->rgcij", grad_num, value_wide, precision=highest) + grad_den_cols,
+        jnp.einsum("rigch,rjgh->rgcij", grad_num, value_wide, preferred_element_type=jnp.float32) + grad_den_cols,
         0.0,
     )
     grad_value_all = grad_value_all + jnp.einsum(
-        "rgcij,rigch->rjgh", kernel, grad_num, precision=highest
+        "rgcij,rigch->rjgh", kernel, grad_num, preferred_element_type=jnp.float32
     )
     grad_phi_q = jnp.einsum(
-        "rgcij,rjgf->rigcf", grad_kernel, all_phi.astype(jnp.float32), precision=highest
-    )
-    grad_phi_all = jnp.einsum("rgcij,rigcf->rjgf", grad_kernel, phi_wide, precision=highest)
+        "rgcij,rjgf->rigcf", grad_kernel, all_phi.astype(jnp.float32), preferred_element_type=jnp.float32
+    )
+    grad_phi_all = jnp.einsum("rgcij,rigcf->rjgf", grad_kernel, phi_wide, preferred_element_type=jnp.float32)
     masked_num = jnp.where(reaches[..., None], grad_num, 0.0)
     masked_den = jnp.where(reaches, grad_den, 0.0)
     grad_phi_q = grad_phi_q + jnp.einsum(
-        "rigch,rgfh->rigcf", masked_num, carry_state, precision=highest
+        "rigch,rgfh->rigcf", masked_num, carry_state, preferred_element_type=jnp.float32
     )
     grad_phi_q = grad_phi_q + masked_den[..., None] * carry_total[:, None, :, None, :]
-    grad_carry_state = jnp.einsum("rigcf,rigch->rgfh", phi_wide, masked_num, precision=highest)
-    grad_carry_total = jnp.einsum("rigcf,rigc->rgf", phi_wide, masked_den, precision=highest)
+    grad_carry_state = jnp.einsum("rigcf,rigch->rgfh", phi_wide, masked_num, preferred_element_type=jnp.float32)
+    grad_carry_total = jnp.einsum("rigcf,rigc->rgf", phi_wide, masked_den, preferred_element_type=jnp.float32)
     back_identity = (
         jnp.zeros_like(grad_carry_state),
         jnp.zeros_like(grad_carry_total),
@@ -388,14 +504,14 @@
     )
     keep_wide = keep[:, :, None, None].astype(jnp.float32)
     element_phi = keep_wide * (
-        jnp.einsum("rjgh,rgfh->rjgf", value_wide[:, :shard], grad_element_state, precision=highest)
+        jnp.einsum("rjgh,rgfh->rjgf", value_wide[:, :shard], grad_element_state, preferred_element_type=jnp.float32)
         + grad_element_total[:, None]
     )
     element_value = keep_wide * jnp.einsum(
         "rjgf,rgfh->rjgh",
         all_phi[:, :shard].astype(jnp.float32),
         grad_element_state,
-        precision=highest,
+        preferred_element_type=jnp.float32,
     )
     grad_phi_all = grad_phi_all + jnp.concatenate(
         [element_phi, jnp.zeros_like(element_phi[:, :window])], axis=1
@@ -446,120 +562,69 @@
         .reshape(tokens_here, kv_here * size)
     )
     grad_value_lin = grad_value_rot.astype(jnp.bfloat16).reshape(tokens_here, kv_here * size)
-    grad_w_query = left_dot(normalized_input, grad_query_lin)
-    grad_w_key = left_dot(normalized_input, grad_key_lin)
-    grad_w_value = left_dot(normalized_input, grad_value_lin)
-    query_widened = grad_query_lin.astype(jnp.float32)
-    key_widened = grad_key_lin.astype(jnp.float32)
-    value_gradient_widened = grad_value_lin.astype(jnp.float32)
-    adapter_query_gradient = adapter_scale * precise_product(
-        lowrank_input[:, :adapter_rank].T, query_widened
-    )
-    adapter_key_gradient = adapter_scale * precise_product(
-        lowrank_input[:, adapter_rank : 2 * adapter_rank].T, key_widened
-    )
-    adapter_value_gradient = adapter_scale * precise_product(
-        lowrank_input[:, 2 * adapter_rank :].T, value_gradient_widened
-    )
-    lowrank_gradient = adapter_scale * jnp.concatenate(
-        [
-            precise_product(query_widened, adapter_query_weight.astype(jnp.float32).T),
-            precise_product(key_widened, adapter_key_weight.astype(jnp.float32).T),
-            precise_product(value_gradient_widened, adapter_value_weight.astype(jnp.float32).T),
-        ],
-        axis=1,
-    )
-    normed_part = (
-        right_dot(grad_query_lin, complete_query)
-        + right_dot(grad_key_lin, complete_key)
-        + right_dot(grad_value_lin, complete_value)
-    )
-    normalized_gradient, lowrank_gradient_combined = (
-        lax.psum(normed_part.astype(jnp.bfloat16), "head").astype(jnp.float32),
-        lax.psum(lowrank_gradient.astype(jnp.bfloat16), "head").astype(jnp.float32),
-    )
-    normalized_gradient = normalized_gradient + precise_product(
-        lowrank_gradient_combined, adapter_down_weight.astype(jnp.float32).T
-    )
-    adapter_down_gradient = precise_product(
-        normalized_input.astype(jnp.float32).T, lowrank_gradient_combined
-    )
-    grad_gain_one = jnp.sum(normalized_gradient * unit_one, axis=0)
+    grad_linear = jnp.concatenate([grad_query_lin, grad_key_lin, grad_value_lin], axis=1)
+    grad_w_qkv = left_dot(normalized_input, grad_linear).astype(jnp.bfloat16)
+    adapter_gradient = adapter_scale * left_dot(lowrank_low, grad_linear)
+    lowrank_gradient = (adapter_scale * right_dot(grad_linear, adapters)).astype(jnp.bfloat16)
+    normed_part = right_dot(grad_linear, complete_qkv) + right_dot(
+        lowrank_gradient, adapter_down_weight
+    )
+    adapter_down_gradient = left_dot(normalized_input, lowrank_gradient)
+    normalized_gradient = head_scatter(normed_part.astype(jnp.bfloat16))
+    own_scale = lax.rsqrt(jnp.mean(own_tokens * own_tokens, axis=-1, keepdims=True) + epsilon)
+    own_unit = own_tokens * own_scale
+    grad_gain_one = jnp.sum(normalized_gradient * own_unit, axis=0)
     inner_one = normalized_gradient * first_norm_gain.astype(jnp.float32)
-    grad_tokens_rows = grad_hidden + scale_one * (
-        inner_one - unit_one * jnp.mean(inner_one * unit_one, axis=-1, keepdims=True)
-    )
-    big = (
-        lax.psum_scatter(
-            grad_w_query.astype(jnp.bfloat16), "seq", scatter_dimension=0, tiled=True
-        ).astype(jnp.float32),
-        lax.psum_scatter(
-            grad_w_key.astype(jnp.bfloat16), "seq", scatter_dimension=0, tiled=True
-        ).astype(jnp.float32),
-        lax.psum_scatter(
-            grad_w_value.astype(jnp.bfloat16), "seq", scatter_dimension=0, tiled=True
-        ).astype(jnp.float32),
-        lax.psum_scatter(
-            grad_w_out.astype(jnp.bfloat16), "seq", scatter_dimension=1, tiled=True
-        ).astype(jnp.float32),
-        lax.psum_scatter(
-            grad_w_gate.astype(jnp.bfloat16), "seq", scatter_dimension=0, tiled=True
-        ).astype(jnp.float32),
-        lax.psum_scatter(
-            grad_w_up.astype(jnp.bfloat16), "seq", scatter_dimension=0, tiled=True
-        ).astype(jnp.float32),
-        lax.psum_scatter(
-            grad_w_down.astype(jnp.bfloat16), "seq", scatter_dimension=1, tiled=True
-        ).astype(jnp.float32),
-    )
-    small_value = (
-        lax.psum(grad_gain_one.astype(jnp.bfloat16), "seq").astype(jnp.float32),
-        lax.psum(grad_gain_two.astype(jnp.bfloat16), "seq").astype(jnp.float32),
-        lax.psum(adapter_down_gradient.astype(jnp.bfloat16), "seq").astype(jnp.float32),
-        lax.psum(adapter_query_gradient.astype(jnp.bfloat16), "seq").astype(jnp.float32),
-        lax.psum(adapter_key_gradient.astype(jnp.bfloat16), "seq").astype(jnp.float32),
-        lax.psum(adapter_value_gradient.astype(jnp.bfloat16), "seq").astype(jnp.float32),
-        lax.psum(adapter_output_down_gradient.astype(jnp.bfloat16), "seq").astype(jnp.float32),
-        lax.psum(adapter_output_up_gradient.astype(jnp.bfloat16), "seq").astype(jnp.float32),
-        lax.psum(grad_map_query.astype(jnp.bfloat16), "seq").astype(jnp.float32),
-        lax.psum(grad_map_key.astype(jnp.bfloat16), "seq").astype(jnp.float32),
-    )
-    first_gain_sum, second_gain_sum, adapter_down_sum = (
-        small_value[0],
-        small_value[1],
-        small_value[2],
-    )
-    adapter_query_sum, adapter_key_sum, adapter_value_sum = (
-        small_value[3],
-        small_value[4],
-        small_value[5],
-    )
-    sum_out_down, sum_out_up, sum_map_query, sum_map_key = (
-        small_value[6],
-        small_value[7],
-        small_value[8],
-        small_value[9],
-    )
+    own_grad_tokens = grad_hidden + own_scale * (
+        inner_one - own_unit * jnp.mean(inner_one * own_unit, axis=-1, keepdims=True)
+    )
+    grad_tokens_rows = head_gather(own_grad_tokens.astype(jnp.bfloat16)).astype(jnp.float32)
+    out_sum = ring_scatter([grad_w_out], block_rows)
+    qkv_sum = ring_scatter([grad_w_qkv], block_rows)
+    query_adapter_sum = adapter_gradient[:adapter_rank, :query_width]
+    key_adapter_sum = adapter_gradient[
+        adapter_rank : 2 * adapter_rank, query_width : query_width + key_width
+    ]
+    value_adapter_sum = adapter_gradient[2 * adapter_rank :, query_width + key_width :]
+    everywhere = (grad_gain_one, grad_gain_two, adapter_down_gradient, adapter_output_up_gradient)
+    everywhere = jax.tree.map(
+        lambda part: lax.psum(part.astype(jnp.bfloat16), ("seq", "head")).astype(jnp.float32),
+        everywhere,
+    )
+    along = (
+        query_adapter_sum,
+        key_adapter_sum,
+        value_adapter_sum,
+        adapter_output_down_gradient,
+        grad_map_query,
+        grad_map_key,
+    )
+    along = jax.tree.map(
+        lambda part: lax.psum(part.astype(jnp.bfloat16), "seq").astype(jnp.float32), along
+    )
+    grad_gate_sum = jnp.concatenate([part[:, :chunk] for part in mlp_sums], axis=1)
+    grad_up_sum = jnp.concatenate([part[:, chunk : 2 * chunk] for part in mlp_sums], axis=1)
+    grad_down_sum = jnp.concatenate([part[:, 2 * chunk :].T for part in mlp_sums], axis=0)
     return (
         layer_rows.reshape(row_count, shard, width),
         grad_tokens_rows.reshape(row_count, shard, width),
-        first_gain_sum,
-        second_gain_sum,
-        big[0],
-        big[1],
-        big[2],
-        big[3],
-        big[4],
-        big[5],
-        big[6],
-        adapter_down_sum,
-        adapter_query_sum,
-        adapter_key_sum,
-        adapter_value_sum,
-        sum_out_down,
-        sum_out_up,
-        sum_map_query,
-        sum_map_key,
+        everywhere[0],
+        everywhere[1],
+        qkv_sum[:, :query_width],
+        qkv_sum[:, query_width : query_width + key_width],
+        qkv_sum[:, query_width + key_width :],
+        out_sum.T,
+        grad_gate_sum,
+        grad_up_sum,
+        grad_down_sum,
+        everywhere[2],
+        along[0],
+        along[1],
+        along[2],
+        along[3],
+        everywhere[3],
+        along[4],
+        along[5],
     )
 
 

time: 2280 us -> 1550 us (0.68)
  waiting for transfers between devices: 1480 us -> 527 us
  local copies, waits for them, and re-layouts: 85.1 us -> 250 us
  starting transfers between devices: 17.1 us -> 115 us
  matrix products: 310 us -> 261 us
  blocking collectives: 207 us -> 183 us
    reduce_scatter x7 -> x0, waiting for transfers between devices: 705 us -> none  [the longest x1 150 us: body(): lax.psum_scatter(grad_w_down.astype(jnp.bfloat16), 'seq', scatter_dimensi...]
    ppermute x0 -> x116, waiting for transfers between devices: none -> 447 us  [the longest x96 382 us: ring_move(): lax.ppermute(block, 'seq', [(order[i], order[(i + step) % count]) for i i...]
    psum x5 -> x2, waiting for transfers between devices: 426 us -> 73.3 us  [the longest x1 73.3 us: body(): lax.psum(part.astype(jnp.bfloat16), ('seq', 'head')).astype(jnp.float32)]
    all_gather x5 -> x0, waiting for transfers between devices: 334 us -> none  [the longest x1 112 us: body(): lax.all_gather(weights[4], 'seq', axis=0, tiled=True)]
    ppermute x0 -> x116, starting transfers between devices: none -> 101 us  [the longest x96 88.2 us: ring_move(): lax.ppermute(block, 'seq', [(order[i], order[(i + step) % count]) for i i...]
    dynamic_update_slice x0 -> x105, local copies, waits for them, and re-layouts: none -> 86.6 us  [the longest x70 55.1 us: assemble(): whole = lax.dynamic_update_slice(whole, block[:, first:last], (at, 0))]
    all_gather x2 -> x0, blocking collectives: 72.8 us -> none  [the longest x1 38.9 us: body(): lax.all_gather(weights[2], 'seq', axis=0, tiled=True)]
    dot_general x25 -> x9, matrix products: 73.3 us -> 20.1 us  [the longest x1 4.46 us: body(): jnp.einsum('rigch,rgfh->rigcf', masked_num, carry_state, preferred_elemen...]
  transfers between devices with their start and end apart: 25 -> 126, of which waited for: 17 -> 57; matrix products, arithmetic and copies ran while one was open for 19% -> 32% of each run, Pallas kernels for 0% -> 0%
where the time goes in v1:
time: 1550 us; the launch traced here: 1540 us
  waiting for transfers between devices  527 us (34%)
  matrix products  261 us (17%)
  local copies, waits for them, and re-layouts  250 us (16%)
  blocking collectives  183 us (12%)
  other arithmetic  171 us (11%)
  starting transfers between devices  115 us (7%)
  between operations  30.3 us (2%)
    ppermute x96, waiting for transfers between devices, ring_move(): lax.ppermute(block, 'seq', [(order[i], order[(i + step) % count]) for i i...  382 us
    ppermute x96, starting transfers between devices, ring_move(): lax.ppermute(block, 'seq', [(order[i], order[(i + step) % count]) for i i...  88.2 us
    dot_general x14, matrix products, right_dot(): lax.dot_general(left, right, (((1,), (1,)), ((), ())), preferred_element_...  78.3 us
    psum x1, waiting for transfers between devices, body(): lax.psum(part.astype(jnp.bfloat16), ('seq', 'head')).astype(jnp.float32)  73.3 us
    ppermute x8, waiting for transfers between devices, chip_move(): lax.ppermute(block, 'head', [(i, (i + 2 * step) % count) for i in range(c...  65 us
    dot_general x14, matrix products, left_dot(): lax.dot_general(left, right, (((0,), (0,)), ((), ())), preferred_element_...  58.4 us
    unnamed x493, local copies, waits for them, and re-layouts  56.4 us
    dynamic_update_slice x70, local copies, waits for them, and re-layouts, assemble(): whole = lax.dynamic_update_slice(whole, block[:, first:last], (at, 0))  55.1 us
  transfers between devices with their start and end apart: 126, of which 57 were waited for; matrix products, arithmetic and copies ran while one was open for 32% of the time, Pallas kernels for 0%

profile of v1, /device:TPU:0, one launch (start us, length us, event | category | flops | bytes accessed | tf_op | source)
XLA Modules:
  0.0 1537.5 jit_solution(5110381584066748286)
XLA Ops:
  48.2 22.1 %all-reduce.7 = f32[64]{0:T(128)S(1)} all-reduce(f32[64]{0:T(128)S(1)} %dynamic-update-slice), channel_id=2, replica_groups=mesh['seq'=8,'head'=4] {'seq'}, use_global_device_ids=true, to_apply=%add.7 | all-reduce | flops 64 | bytes 512
  118.2 14.8 collective-permute-done.14
  221.8 32.8 %all-gather.2 = f32[64,2,128]{2,1,0:T(2,128)} all-gather(f32[8,2,128]{2,1,0:T(2,128)S(1)} %copy.423), channel_id=4, replica_groups=mesh['seq'=8,'head'=4] {'seq'}, dimensions={0}, use_global_device_ids=true | all-gather | bytes 73728 | tf_op jit(solution)/shard_map/all_gather | solution.py:23
  266.9 50.2 %collective-permute-done.28 = bf16[256,1536]{0,1:T(8,128)(2,1)S(1)} collective-permute-done((bf16[256,1536]{0,1:T(8,128)(2,1)}, bf16[256,1536]{0,1:T(8,128)(2,1)S(1)}, u32[]{:S(2)}, u32[]{:S(2)}) %collective-permute-start.28) | collective-permute-done | bytes 786464 | tf_op jit(solution)/shard_map/ppermute | solution.py:138
  335.3 14.7 collective-permute-done.35
  359.9 22.3 %collective-permute-done.36 = bf16[256,1536]{0,1:T(8,128)(2,1)S(1)} collective-permute-done((bf16[256,1536]{0,1:T(8,128)(2,1)S(1)}, bf16[256,1536]{0,1:T(8,128)(2,1)S(1)}, u32[]{:S(2)}, u32[]{:S(2)}) %collective-permute-start.36) | collective-permute-done | bytes 786464 | tf_op jit(solution)/shard_map/ppermute | solution.py:138
  395.1 16.6 %collective-permute-done.43 = bf16[256,1536]{0,1:T(8,128)(2,1)S(1)} collective-permute-done((bf16[256,1536]{0,1:T(8,128)(2,1)S(1)}, bf16[256,1536]{0,1:T(8,128)(2,1)S(1)}, u32[]{:S(2)}, u32[]{:S(2)}) %collective-permute-start.43) | collective-permute-done | bytes 786464 | tf_op jit(solution)/shard_map/ppermute | solution.py:138
  424.6 18.2 %collective-permute-done.44 = bf16[256,1536]{0,1:T(8,128)(2,1)S(1)} collective-permute-done((bf16[256,1536]{0,1:T(8,128)(2,1)S(1)}, bf16[256,1536]{0,1:T(8,128)(2,1)S(1)}, u32[]{:S(2)}, u32[]{:S(2)}) %collective-permute-start.44) | collective-permute-done | bytes 786464 | tf_op jit(solution)/shard_map/ppermute | solution.py:138
  453.3 62.9 %while.35 = (s32[]{:T(128)}, f32[8,2,128,64]{3,2,1,0:T(8,128)}, f32[8,2,128]{2,1,0:T(2,128)S(1)}, f32[8]{0:T(128)}, s32[]{:T(128)}, /*index=5*/f32[8,8]{1,0:T(8,...) while((s32[]{:T(128)}, f32[8,2,128,64]{3,2,1,0:T(8,128)}, ...), condition=%wide.region_11.12_spmd.clone, body=%wide.region_10.11_spmd.clone.sunk | while | flops 665660 | bytes 3695062 | solution.py:32
  593.7 19.3 %collective-permute-done.22 = bf16[256,2048]{1,0:T(8,128)(2,1)S(1)} collective-permute-done((bf16[256,2048]{1,0:T(8,128)(2,1)S(1)}, bf16[256,2048]{1,0:T(8,128)(2,1)S(1)}, u32[]{:S(2)}, u32[]{:S(2)}) %collective-permute-start.22) | collective-permute-done | bytes 1048608 | tf_op jit(solution)/shard_map/ppermute | solution.py:209
  614.6 18.9 %all-reduce.8 = bf16[64]{0:T(256)(128)(2,1)S(1)} all-reduce(bf16[64]{0:T(256)(128)(2,1)S(1)} %dynamic-update-slice.1), channel_id=5, replica_groups=mesh['seq'=8,'head'=4] {'seq'}, use_global_device_ids=true, to_apply=%add.8 | all-reduce | flops 64 | bytes 256
  760.2 17.1 %add_convert_fusion.1 = bf16[1024,2048]{1,0:T(8,128)(2,1)} fusion(f32[1024,2048]{1,0:T(8,128)} %fusion.113, f32[1024,2048]{1,0:T(8,128)} %fusion.115, f32[1024,2048]{1,0:T(8,128)} %fusion.114, bf16[2048,1024]{0,1:T(8,128)(2,1)} %slice_dynamic-update-slice_fusion.34, bf16[1024,512]{0,1:T(8,128)(2,1)} %copy-done.234, bf16[1024,512]{0,1:T(8,128)(2,1)S(1)} %get-tuple-element.474), kind=kOutput, calls=%fused_computation.36 | convolution fusion | flops 4307550208 | bytes 35651584 | tf_op jit(solution)/shard_map/dot_general | solution.py:75
  856.0 14.3 collective-permute-done.99
  872.8 14.3 collective-permute-done.107
  889.7 14.3 collective-permute-done.115
  906.5 14.3 collective-permute-done.92
  923.4 14.3 collective-permute-done.100
  957.1 14.3 collective-permute-done.116
  1078.0 19.0 %collective-permute-done.59 = bf16[256,2048]{1,0:T(8,128)(2,1)} collective-permute-done((bf16[256,2048]{1,0:T(8,128)(2,1)}, bf16[256,2048]{1,0:T(8,128)(2,1)}, u32[]{:S(2)}, u32[]{:S(2)}) %collective-permute-start.59) | collective-permute-done | bytes 1048608 | tf_op jit(solution)/shard_map/ppermute | solution.py:209
  1186.0 32.2 %all-gather.5 = bf16[64,2,128]{2,1,0:T(2,128)(2,1)} all-gather(bf16[8,2,128]{2,1,0:T(2,128)(2,1)S(1)} %convert_element_type.511), channel_id=7, replica_groups=mesh['seq'=8,'head'=4] {'seq'}, dimensions={0}, use_global_device_ids=true | all-gather | bytes 36864 | tf_op jit(solution)/shard_map/all_gather | solution.py:40
  1223.7 31.4 %while.34 = (s32[]{:T(128)}, f32[8,2,128,64]{3,2,1,0:T(8,128)S(1)}, f32[8,2,128]{2,1,0:T(2,128)S(1)}, f32[8]{0:T(128)}, s32[]{:T(128)}, /*index=5*/bf16[8,8]{1,0...) while((s32[]{:T(128)}, f32[8,2,128,64]{3,2,1,0:T(8,128)S(1)}, ...), condition=%wide.region_21.22_spmd, body=%wide.region_20.21_spmd.sunk | while | flops 532534 | bytes 2380131 | solution.py:57
  1361.5 35.2 %all-reduce.10 = (bf16[8,512]{1,0:T(8,128)(2,1)S(1)}, bf16[8,128]{1,0:T(8,128)(2,1)S(1)}, bf16[8,128]{1,0:T(8,128)(2,1)S(1)}, bf16[512,8]{0,1:T(8,128)(2,1)S(1)}, bf16[2,64,64]{2,1,0:T(8,128)(2,1)S(1)}) all-reduce(bf16[8,512]{1,0:T(8,128)(2,1)S(1)} %slice.911, ...), channel_id=1, replica_groups=mesh['seq'=8,'head'=4] {'seq'}, use_global_device_ids=true, to_apply=%region_30.31 | all-reduce | flops 18432 | bytes 73728 | tf_op jit(solution)/shard_map/psum | solution.py:603
  1399.8 73.3 %all-reduce.14.cloned.1.call-done = bf16[2048,24]{0,1:T(8,128)(2,1)} async-done(((bf16[2048,24]{0,1:T(8,128)(2,1)}), bf16[2048,24]{0,1:T(8,128)(2,1)}) %all-reduce.14.cloned.1.call-update) | async-done | bytes 98320 | tf_op jit(solution)/shard_map/psum | solution.py:591
  1477.5 41.5 %all-reduce.9 = (bf16[2048]{0:T(1024)(128)(2,1)S(1)}, bf16[2048]{0:T(1024)(128)(2,1)S(1)}, bf16[8,2048]{1,0:T(8,128)(2,1)S(1)}) all-reduce(bf16[2048]{0:T(1024)(128)(2,1)S(1)} %get-tuple-element.412, bf16[2048]{0:T(1024)(128)(2,1)S(1)} %copy-done.214, ...), channel_id=1, replica_groups=mesh['seq'=8,'head'=4] {'seq','head'}, use_global_device_ids=true, to_apply=%region_26.27 | all-reduce | flops 20480 | bytes 81920 | tf_op jit(solution)/shard_map/psum | solution.py:591
  (1248 shorter events, 972.4 us)
Async XLA Ops:
  7.2 446.1 %all-gather.9.cloned.1.call-start = ((), (), s32[]{:S(2)}) async-start(), calls=%async_computation.2 | async-start | bytes 4718592 | tf_op jit(solution)/shard_map/all_gather | solution.py:23
  12.0 80.7 %collective-permute-start.1 = (bf16[256,768]{1,0:T(8,128)(2,1)}, bf16[256,768]{1,0:T(8,128)(2,1)}, u32[]{:S(2)}, u32[]{:S(2)}) collective-permute-start(bf16[256,768]{1,0:T(8,128)(2,1)} %constant_dynamic-update-slice_fusion.18), channel_id=1, source_target_pairs={{0,4},{8,0},{16,8},{24,16},{28,24},{20,28},{12,20},{4,12},{1,5},{9... | collective-permute-start | bytes 1179656 | tf_op jit(solution)/shard_map/ppermute | solution.py:138
  15.0 79.9 %collective-permute-start = (bf16[256,768]{1,0:T(8,128)(2,1)}, bf16[256,768]{1,0:T(8,128)(2,1)}, u32[]{:S(2)}, u32[]{:S(2)}) collective-permute-start(bf16[256,768]{1,0:T(8,128)(2,1)} %constant_dynamic-update-slice_fusion.18), channel_id=1, source_target_pairs={{0,8},{8,16},{16,24},{24,28},{28,20},{20,12},{12,4},{4,0},{1,9},{9... | collective-permute-start | bytes 1179656 | tf_op jit(solution)/shard_map/ppermute | solution.py:138
  102.1 103.5 %collective-permute-start.25 = (bf16[256,1536]{0,1:T(8,128)(2,1)}, bf16[256,1536]{0,1:T(8,128)(2,1)}, u32[]{:S(2)}, u32[]{:S(2)}) collective-permute-start(bf16[256,1536]{0,1:T(8,128)(2,1)} %pad_maximum_fusion.18), channel_id=1, source_target_pairs={{0,4},{8,0},{16,8},{24,16},{28,24},{20,28},{12,20},{4,12},{1,5},{9... | collective-permute-start | bytes 2359304 | tf_op jit(solution)/shard_map/ppermute | solution.py:138
  134.2 72.2 %collective-permute-start.24 = (bf16[256,1536]{0,1:T(8,128)(2,1)}, bf16[256,1536]{0,1:T(8,128)(2,1)}, u32[]{:S(2)}, u32[]{:S(2)}) collective-permute-start(bf16[256,1536]{0,1:T(8,128)(2,1)} %pad_maximum_fusion.18), channel_id=1, source_target_pairs={{0,8},{8,16},{16,24},{24,28},{28,20},{20,12},{12,4},{4,0},{1,9},{9... | collective-permute-start | bytes 2359304 | tf_op jit(solution)/shard_map/ppermute | solution.py:138
  189.9 331.7 %collective-permute-start.9 = (bf16[8,64,2,64]{1,3,2,0:T(8,128)(2,1)}, bf16[8,64,2,64]{1,3,2,0:T(8,128)(2,1)}, u32[]{:S(2)}, u32[]{:S(2)}) collective-permute-start(bf16[8,64,2,64]{1,3,2,0:T(8,128)(2,1)} %slice.765), channel_id=1, source_target_pairs={{0,4},{4,8},{8,12},{12,16},{16,20},{20,24},{24,28},{1,5},{5,9},{9,... | collective-permute-start | bytes 393224 | tf_op jit(solution)/shard_map/ppermute | solution.py:18
  220.9 1002.1 %all-gather.11.cloned.1.call-start = ((), (), s32[]{:S(2)}) async-start(), calls=%async_computation.3 | async-start | bytes 2359296 | tf_op jit(solution)/shard_map/all_gather | solution.py:40
  254.5 69.7 %collective-permute-start.32 = (bf16[256,1536]{0,1:T(8,128)(2,1)}, bf16[256,1536]{0,1:T(8,128)(2,1)S(1)}, u32[]{:S(2)}, u32[]{:S(2)}) collective-permute-start(bf16[256,1536]{0,1:T(8,128)(2,1)} %pad_maximum_fusion.19), channel_id=1, source_target_pairs={{0,8},{8,16},{16,24},{24,28},{28,20},{20,12},{12,4},{4,0},{1,9},{9... | collective-permute-start | bytes 2359304 | tf_op jit(solution)/shard_map/ppermute | solution.py:138
  254.6 71.8 %collective-permute-start.33 = (bf16[256,1536]{0,1:T(8,128)(2,1)}, bf16[256,1536]{0,1:T(8,128)(2,1)S(1)}, u32[]{:S(2)}, u32[]{:S(2)}) collective-permute-start(bf16[256,1536]{0,1:T(8,128)(2,1)} %pad_maximum_fusion.19), channel_id=1, source_target_pairs={{0,4},{8,0},{16,8},{24,16},{28,24},{20,28},{12,20},{4,12},{1,5},{9... | collective-permute-start | bytes 2359304 | tf_op jit(solution)/shard_map/ppermute | solution.py:138
  443.5 102.2 %collective-permute-start.46 = (bf16[128,1536]{0,1:T(8,128)(2,1)}, bf16[128,1536]{0,1:T(8,128)(2,1)}, u32[]{:S(2)}, u32[]{:S(2)}) collective-permute-start(bf16[128,1536]{0,1:T(8,128)(2,1)} %slice.823), channel_id=1, source_target_pairs={{0,8},{8,16},{16,24},{24,28},{28,20},{20,12},{12,4},{4,0},{1,9},{9... | collective-permute-start | bytes 1179656 | tf_op jit(solution)/shard_map/ppermute | solution.py:138
  446.8 100.5 %collective-permute-start.47 = (bf16[128,1536]{0,1:T(8,128)(2,1)}, bf16[128,1536]{0,1:T(8,128)(2,1)}, u32[]{:S(2)}, u32[]{:S(2)}) collective-permute-start(bf16[128,1536]{0,1:T(8,128)(2,1)} %slice.825), channel_id=1, source_target_pairs={{0,4},{8,0},{16,8},{24,16},{28,24},{20,28},{12,20},{4,12},{1,5},{9... | collective-permute-start | bytes 1179656 | tf_op jit(solution)/shard_map/ppermute | solution.py:138
  446.8 105.4 %collective-permute-start.50 = (bf16[256,1536]{0,1:T(8,128)(2,1)}, bf16[256,1536]{0,1:T(8,128)(2,1)}, u32[]{:S(2)}, u32[]{:S(2)}) collective-permute-start(bf16[256,1536]{0,1:T(8,128)(2,1)} %collective-permute-done.48), channel_id=1, source_target_pairs={{0,8},{8,16},{16,24},{24,28},{28,20},{20,12},{12,4},{4,0},{1,9},{9... | collective-permute-start | bytes 2359304 | tf_op jit(solution)/shard_map/ppermute | solution.py:138
  448.8 105.5 %collective-permute-start.51 = (bf16[256,1536]{0,1:T(8,128)(2,1)}, bf16[256,1536]{0,1:T(8,128)(2,1)}, u32[]{:S(2)}, u32[]{:S(2)}) collective-permute-start(bf16[256,1536]{0,1:T(8,128)(2,1)} %collective-permute-done.49), channel_id=1, source_target_pairs={{0,4},{8,0},{16,8},{24,16},{28,24},{20,28},{12,20},{4,12},{1,5},{9... | collective-permute-start | bytes 2359304 | tf_op jit(solution)/shard_map/ppermute | solution.py:138
  780.6 193.3 %collective-permute-start.61 = (bf16[2,256,2048]{2,1,0:T(8,128)(2,1)}, bf16[2,256,2048]{2,1,0:T(8,128)(2,1)}, u32[]{:S(2)}, u32[]{:S(2)}) collective-permute-start(bf16[2,256,2048]{2,1,0:T(8,128)(2,1)} %dynamic-slice_bitcast_fusion.1), channel_id=1, source_target_pairs={{0,1},{1,0},{2,3},{3,2},{4,5},{5,4},{6,7},{7,6},{8,9},{9,8},{10,11... | collective-permute-start | bytes 6291464 | tf_op jit(solution)/shard_map/ppermute | solution.py:204
  830.9 147.4 %collective-permute-start.56 = (bf16[2,256,2048]{2,1,0:T(8,128)(2,1)S(1)}, bf16[2,256,2048]{2,1,0:T(8,128)(2,1)S(1)}, u32[]{:S(2)}, u32[]{:S(2)}) collective-permute-start(bf16[2,256,2048]{2,1,0:T(8,128)(2,1)S(1)} %dynamic-slice_bitcast_fusion.2), channel_id=1, source_target_pairs={{0,1},{1,0},{2,3},{3,2},{4,5},{5,4},{6,7},{7,6},{8,9},{9,8},{10,11... | collective-permute-start | bytes 6291464 | tf_op jit(solution)/shard_map/ppermute | solution.py:204
  1097.0 86.3 %collective-permute-start.60 = (bf16[256,2048]{1,0:T(8,128)(2,1)}, bf16[256,2048]{1,0:T(8,128)(2,1)}, u32[]{:S(2)}, u32[]{:S(2)}) collective-permute-start(bf16[256,2048]{1,0:T(8,128)(2,1)} %collective-permute-done.59), channel_id=1, source_target_pairs={{0,1},{1,0},{2,3},{3,2},{4,5},{5,4},{6,7},{7,6},{8,9},{9,8},{10,11... | collective-permute-start | bytes 3145736 | tf_op jit(solution)/shard_map/ppermute | solution.py:204
  1123.8 168.2 %all-reduce.16.cloned.1.call-start = ((), (), s32[]{:S(2)}) async-start(), calls=%async_computation.1 | async-start | bytes 262144 | tf_op jit(solution)/shard_map/psum | solution.py:603
  1138.7 141.2 %collective-permute-start.66 = (bf16[8,64,2,64]{1,3,2,0:T(8,128)(2,1)}, bf16[8,64,2,64]{1,3,2,0:T(8,128)(2,1)}, u32[]{:S(2)}, u32[]{:S(2)}) collective-permute-start(bf16[8,64,2,64]{1,3,2,0:T(8,128)(2,1)} %slice.1163), channel_id=1, source_target_pairs={{4,0},{8,4},{12,8},{16,12},{20,16},{24,20},{28,24},{5,1},{9,5},{13... | collective-permute-start | bytes 393224 | tf_op jit(solution)/shard_map/ppermute | solution.py:18
  1174.8 298.4 %all-reduce.14.cloned.1.call-start = ((), (), s32[]{:S(2)}) async-start(), calls=%async_computation | async-start | bytes 196608 | tf_op jit(solution)/shard_map/psum | solution.py:591
  1220.3 73.4 %collective-permute-start.87 = (bf16[256,512]{1,0:T(8,128)(2,1)}, bf16[256,512]{1,0:T(8,128)(2,1)}, u32[]{:S(2)}, u32[]{:S(2)}) collective-permute-start(bf16[256,512]{1,0:T(8,128)(2,1)} %pad_maximum_fusion.39), channel_id=1, source_target_pairs={{0,4},{8,0},{16,8},{24,16},{28,24},{20,28},{12,20},{4,12},{1,5},{9... | collective-permute-start | bytes 786440 | tf_op jit(solution)/shard_map/ppermute | solution.py:138
  1352.2 123.7 %collective-permute-start.72 = (bf16[256,2048]{1,0:T(8,128)(2,1)}, bf16[256,2048]{1,0:T(8,128)(2,1)S(1)}, u32[]{:S(2)}, u32[]{:S(2)}) collective-permute-start(bf16[256,2048]{1,0:T(8,128)(2,1)} %get-tuple-element.652), channel_id=1, source_target_pairs={{0,2},{1,3},{2,0},{3,1},{4,6},{5,7},{6,4},{7,5},{8,10},{9,11},{10,... | collective-permute-start | bytes 3145736 | tf_op jit(solution)/shard_map/ppermute | solution.py:209
  1354.9 119.8 %collective-permute-start.77 = (bf16[256,768]{1,0:T(8,128)(2,1)}, bf16[256,768]{1,0:T(8,128)(2,1)S(1)}, u32[]{:S(2)}, u32[]{:S(2)}) collective-permute-start(bf16[256,768]{1,0:T(8,128)(2,1)} %get-tuple-element.518), channel_id=1, source_target_pairs={{0,8},{8,16},{16,24},{24,28},{28,20},{20,12},{12,4},{4,0},{1,9},{9... | collective-permute-start | bytes 1179656 | tf_op jit(solution)/shard_map/ppermute | solution.py:138
  1355.5 165.3 %collective-permute-start.71 = (bf16[256,2048]{1,0:T(8,128)(2,1)}, bf16[256,2048]{1,0:T(8,128)(2,1)S(1)}, u32[]{:S(2)}, u32[]{:S(2)}) collective-permute-start(bf16[256,2048]{1,0:T(8,128)(2,1)} %get-tuple-element.652), channel_id=1, source_target_pairs={{0,1},{1,0},{2,3},{3,2},{4,5},{5,4},{6,7},{7,6},{8,9},{9,8},{10,11... | collective-permute-start | bytes 3145736 | tf_op jit(solution)/shard_map/ppermute | solution.py:204
  1357.5 117.2 %collective-permute-start.81 = (bf16[256,768]{1,0:T(8,128)(2,1)}, bf16[256,768]{1,0:T(8,128)(2,1)S(1)}, u32[]{:S(2)}, u32[]{:S(2)}) collective-permute-start(bf16[256,768]{1,0:T(8,128)(2,1)} %dynamic-slice_add_fusion.1), channel_id=1, source_target_pairs={{0,4},{8,0},{16,8},{24,16},{28,24},{20,28},{12,20},{4,12},{1,5},{9... | collective-permute-start | bytes 1179656 | tf_op jit(solution)/shard_map/ppermute | solution.py:138
  (352 other events, 6231.3 us)
Sparse Core Ops, SparseCore 0:
  221.0 96.6 all-gather.8
  1123.9 47.2 all-gather.10
  1174.9 69.3 all-reduce.15
  1355.0 118.0 all-reduce.13

commit v2 on v1

v2 whole, which is shorter than its diff:
```python
import functools

import jax
import jax.numpy as jnp
from jax import lax
from jax.experimental import pallas as pl
from jax.experimental.pallas import tpu as pltpu
from jax.sharding import PartitionSpec as P

WIN = 64
LANES = 128
STATE_ROWS = 80
MLP_CHUNKS = 2

epsilon = 1e-05
rope_base = 500000.0
adapter_scale = 2.0


def forward_product(left, right):
    return jnp.dot(left, right, preferred_element_type=jnp.float32)


def left_dot(left, right):
    return lax.dot_general(
        left, right, (((0,), (0,)), ((), ())), preferred_element_type=jnp.float32
    )


def right_dot(left, right):
    return lax.dot_general(
        left, right, (((1,), (1,)), ((), ())), preferred_element_type=jnp.float32
    )


def shifted(block, distance):
    devices = range(lax.axis_size("seq"))
    route = [(i - distance, i) for i in devices if i - distance in devices]
    return lax.ppermute(block, "seq", route)


def ring_order(count):
    return list(range(0, count, 2)) + list(range(count - 1, 0, -2))


def ring_move(block, step):
    order = ring_order(lax.axis_size("seq"))
    count = len(order)
    return lax.ppermute(block, "seq", [(order[i], order[(i + step) % count]) for i in range(count)])


def ring_index(offset):
    count = lax.axis_size("seq")
    mine = lax.axis_index("seq")
    place = jnp.where(mine % 2 == 0, mine // 2, count - 1 - mine // 2)
    there = (place + offset + count) % count
    return jnp.where(there < count // 2, 2 * there, 2 * (count - 1 - there) + 1)


def after(value, *others):
    return lax.optimization_barrier((value,) + others)[0]


class Gather:
    def __init__(self, own):
        self.half = lax.axis_size("seq") // 2
        self.found = {0: own}
        self.up = self.down = own
        self.step = 0

    def advance(self, *gates, quarters=1):
        for _ in range(quarters * max(1, self.half // 4)):
            if self.step == self.half:
                return
            self.step += 1
            cut = self.up.shape[0] // 2
            up, down = self.up, self.down
            if gates:
                up, down = after(up, *gates), after(down, *gates)
            if self.step < self.half:
                self.up, self.down = ring_move(up, 1), ring_move(down, -1)
                self.found[-self.step], self.found[self.step] = self.up, self.down
            else:
                self.found[self.half] = (ring_move(up[:cut], 1), ring_move(down[cut:], -1))

    def edge(self):
        return self.up, self.down

    def assemble(self, *widths):
        self.advance(quarters=4)
        count = lax.axis_size("seq")
        rows = self.found[0].shape[0]
        offsets = sorted(self.found)
        places = jnp.stack([ring_index(offset) * rows for offset in offsets]).astype(jnp.int32)
        pieces, origins = [], []
        for at, offset in enumerate(offsets):
            block, shift = self.found[offset], 0
            for part in block if isinstance(block, tuple) else (block,):
                pieces.append(part)
                origins.append((at, shift))
                shift += part.shape[0]
        starts = [sum(widths[:i]) for i in range(len(widths))]

        def kernel(places_ref, *refs):
            sources, rest = refs[: len(pieces)], refs[len(pieces) :]
            targets, buffers, semaphores = rest[: len(widths)], rest[len(widths) : -1], rest[-1]
            inward, outward = [], []
            for turn, (source, (at, shift)) in enumerate(zip(sources, origins, strict=True)):
                length = source.shape[0]
                held = buffers[turn]
                inward.append(pltpu.make_async_copy(source, held, semaphores.at[turn]))
                first = pl.multiple_of(places_ref[at] + shift, length)
                for target, start, width in zip(targets, starts, widths, strict=True):
                    outward.append(
                        pltpu.make_async_copy(
                            held.at[:, pl.ds(start, width)],
                            target.at[pl.ds(first, length), :],
                            semaphores.at[len(sources) + len(outward)],
                        )
                    )
            for copy in inward:
                copy.start()
            for turn, copy in enumerate(inward):
                copy.wait()
                for back in outward[turn * len(widths) : (turn + 1) * len(widths)]:
                    back.start()
            for copy in outward:
                copy.wait()

        anywhere = pl.BlockSpec(memory_space=pl.ANY)
        size = sum(piece.size for piece in pieces) * 2
        return pl.pallas_call(
            kernel,
            grid_spec=pltpu.PrefetchScalarGridSpec(
                num_scalar_prefetch=1,
                grid=(1,),
                in_specs=[anywhere] * len(pieces),
                out_specs=[anywhere] * len(widths),
                scratch_shapes=[pltpu.VMEM(piece.shape, piece.dtype) for piece in pieces]
                + [pltpu.SemaphoreType.DMA((len(pieces) * (1 + len(widths)),))],
            ),
            out_shape=[
                jax.ShapeDtypeStruct((count * rows, width), pieces[0].dtype) for width in widths
            ],
            compiler_params=pltpu.CompilerParams(vmem_limit_bytes=size + 4 * 1024 * 1024),
            cost_estimate=told(1 + size // 4_000_000),
            name="assemble",
        )(places, *pieces)


class Scatter:
    def __init__(self, grads, rows):
        self.grads, self.rows = grads, rows
        self.half = lax.axis_size("seq") // 2
        self.step = 0

    def own(self, offset):
        at = ring_index(offset) * self.rows
        parts = [lax.dynamic_slice_in_dim(part, at, self.rows, 0) for part in self.grads]
        return parts[0] if len(parts) == 1 else jnp.concatenate(parts, axis=1)

    def advance(self, *gates, quarters=1):
        for _ in range(quarters * max(1, self.half // 4)):
            if self.step == self.half:
                return
            self.step += 1
            offset = self.half - self.step + 1
            cut = self.rows // 2
            if self.step == 1:
                far = self.own(offset)
                up, down = far[:cut], far[cut:]
            else:
                above, below = self.own(offset), self.own(-offset)
                if self.step == 2:
                    up = jnp.concatenate([above[:cut] + self.up, above[cut:]], axis=0)
                    down = jnp.concatenate([below[:cut], below[cut:] + self.down], axis=0)
                else:
                    up, down = above + self.up, below + self.down
            if gates:
                up, down = after(up, *gates), after(down, *gates)
            self.up, self.down = ring_move(up, 1), ring_move(down, -1)

    def edge(self):
        return self.up, self.down

    def total(self):
        self.advance(quarters=4)
        mine = self.own(0).astype(jnp.float32)
        return mine + self.up.astype(jnp.float32) + self.down.astype(jnp.float32)


def core_swap(block):
    count = lax.axis_size("head")
    return lax.ppermute(block, "head", [(i, i ^ 1) for i in range(count)])


def chip_move(block, step):
    count = lax.axis_size("head")
    return lax.ppermute(block, "head", [(i, (i + 2 * step) % count) for i in range(count)])


def head_pair_sum(part):
    chips = lax.axis_size("head") // 2
    core = lax.axis_index("head") % 2
    rows = part.shape[0] // (2 * chips)
    split = part.reshape(chips, 2, rows, part.shape[1])
    theirs = core_swap(lax.dynamic_index_in_dim(split, 1 - core, 1, False))
    return lax.dynamic_index_in_dim(split, core, 1, False).astype(jnp.float32) + theirs


def head_finish(both, *gates):
    chips = lax.axis_size("head") // 2
    chip = lax.axis_index("head") // 2
    total = lax.dynamic_index_in_dim(both, chip, 0, False)
    for step in range(1, chips):
        sent = lax.dynamic_index_in_dim(both, (chip + step) % chips, 0, False)
        sent = sent.astype(jnp.bfloat16)
        total = total + chip_move(after(sent, *gates) if gates else sent, step)
    return total


def head_scatter(part):
    return head_finish(head_pair_sum(part))


def head_gather(own):
    chips = lax.axis_size("head") // 2
    place = lax.axis_index("head")
    chip, core = place // 2, place % 2
    whole = jnp.zeros((2 * chips,) + own.shape, own.dtype)
    for step in range(chips):
        block = chip_move(own, step) if step else own
        at = 2 * ((chip - step + chips) % chips)
        whole = lax.dynamic_update_index_in_dim(whole, block, at + core, 0)
        whole = lax.dynamic_update_index_in_dim(whole, core_swap(block), at + 1 - core, 0)
    return whole.reshape((2 * chips * own.shape[0],) + own.shape[1:])


def exchange_sum(block, axis, bits):
    devices = range(lax.axis_size(axis))
    block = block.astype(jnp.bfloat16)
    for bit in bits:
        other = lax.ppermute(block, axis, [(i, i ^ bit) for i in devices])
        block = (block.astype(jnp.float32) + other.astype(jnp.float32)).astype(jnp.bfloat16)
    return block


def bits_of(axis):
    bits, bit = [], 1
    while bit < lax.axis_size(axis):
        bits.append(bit)
        bit *= 2
    return bits


def lane_of(shape):
    return lax.broadcasted_iota(jnp.int32, shape, 1)


def rolled(values, shift):
    return pltpu.roll(values, shift % LANES, 1)


def swapped_halves(values):
    lane = lane_of(values.shape)
    return jnp.where(lane % 64 < 32, rolled(values, -32), rolled(values, 32))


def half_lanes(values, half):
    lane = lane_of(values.shape)
    return jnp.where(lane < 64 if half == 0 else lane >= 64, values, 0.0)


def in_half(values, have, want):
    kept = half_lanes(values, have)
    return kept if have == want else rolled(kept, 64)


def half_sums(values):
    row = lax.broadcasted_iota(jnp.int32, (LANES, LANES), 0)
    ones = jnp.where(row // 64 == lane_of((LANES, LANES)) // 64, 1.0, 0.0).astype(jnp.bfloat16)
    return forward_product(values.astype(jnp.bfloat16), ones)


def half_softmax(values):
    lane = lane_of(values.shape)
    low = lane < 64
    first = jnp.max(jnp.where(low, values, -jnp.inf), axis=1, keepdims=True)
    second = jnp.max(jnp.where(low, -jnp.inf, values), axis=1, keepdims=True)
    powers = jnp.exp(values - jnp.where(low, first, second))
    first = jnp.sum(jnp.where(low, powers, 0.0), axis=1, keepdims=True)
    second = jnp.sum(jnp.where(low, 0.0, powers), axis=1, keepdims=True)
    return powers * jnp.where(low, 1.0 / first, 1.0 / second)


def group(ref_or_value, index):
    return ref_or_value[:, index * LANES : (index + 1) * LANES]


class Sizes:
    def __init__(self, shard, heads, kv_heads):
        self.shard, self.heads, self.kv = shard, heads, kv_heads
        self.each = heads // kv_heads
        self.query_groups = heads // 2
        self.key_groups = (kv_heads + 1) // 2
        self.linear = (heads + 2 * kv_heads) * 64
        self.span = shard + WIN
        self.kv_lanes = 2 * kv_heads * 64
        self.halo_lanes = self.kv_lanes + kv_heads * LANES

    def key_place(self, g):
        return g // 2, g % 2

    def value_place(self, g):
        return (self.kv + g) // 2, (self.kv + g) % 2


def prepare_kernel(sizes, lin_ref, cos_ref, sin_ref, meta_ref, mapq_ref, mapk_ref, rot_ref, phi_ref, halo_ref, whole_ref, first_ref):
    shard = sizes.shard
    wide = []
    for index in range(sizes.linear // LANES):
        part = group(lin_ref, index)
        turned = part * group(cos_ref, index) + swapped_halves(part) * group(sin_ref, index)
        rot_ref[:, index * LANES : (index + 1) * LANES] = turned.astype(jnp.bfloat16)
        wide.append(turned.astype(jnp.bfloat16))
    for index in range(sizes.query_groups):
        both = forward_product(wide[index], mapq_ref[index])
        for half in range(2):
            at = (2 * index + half) * LANES
            phi = half_softmax(group(both, half))
            phi_ref[:, at : at + LANES] = phi.astype(jnp.bfloat16)
    kv_groups = wide[sizes.query_groups :]
    phis = []
    for index in range(sizes.key_groups):
        both = forward_product(kv_groups[index], mapk_ref[index])
        for half in range(min(2, sizes.kv - 2 * index)):
            at = (sizes.heads + 2 * index + half) * LANES
            phi = half_softmax(group(both, half)).astype(jnp.bfloat16)
            phi_ref[:, at : at + LANES] = phi
            phis.append(phi)
    halo_ref[:, : sizes.kv_lanes] = jnp.concatenate(kv_groups, axis=1)[shard - WIN :]
    halo_ref[:, sizes.kv_lanes :] = jnp.concatenate(phis, axis=1)[shard - WIN :]
    keep_whole, keep_first = meta_ref[:, 0:1], meta_ref[:, 1:2]
    for g in range(sizes.kv):
        at, half = sizes.value_place(g)
        values = in_half(kv_groups[at].astype(jnp.float32), half, 0)
        values = jnp.where(lane_of(values.shape) == 64, 1.0, values).astype(jnp.bfloat16)
        phi = phis[g].astype(jnp.float32)
        for keep, ref in ((keep_whole, whole_ref), (keep_first, first_ref)):
            state = left_dot(values, (phi * keep).astype(jnp.bfloat16))
            ref[g] = state[:STATE_ROWS].astype(jnp.bfloat16)


def near_and_far(sizes, meta_ref, keys_ref):
    shape = (sizes.shard, sizes.span)
    row = lax.broadcasted_iota(jnp.int32, shape, 0)
    column = lax.broadcasted_iota(jnp.int32, shape, 1)
    same = meta_ref[:, 2:3] == keys_ref[0:1, :]
    near = same & (column > row) & (column <= row + WIN)
    far = same & (column <= row)
    return near, far


def twice(values):
    return jnp.concatenate([values] * 2, axis=0)


def stacked(parts):
    return jnp.concatenate(parts, axis=0)


def with_halo(sizes, rot_ref, phi_ref, halo_ref, g):
    out = []
    for at, half in (sizes.key_place(g), sizes.value_place(g)):
        own = group(rot_ref, sizes.query_groups + at)
        before = group(halo_ref, at)
        wide = stacked([before, own]).astype(jnp.float32)
        out.append([in_half(wide, half, want) for want in range(2)])
    phi = stacked(
        [
            halo_ref[:, sizes.kv_lanes + g * LANES : sizes.kv_lanes + (g + 1) * LANES],
            group(phi_ref, sizes.heads + g),
        ]
    )
    return out[0], out[1], phi


def value_sides(values, weight):
    ones = jnp.full(values[0].shape, weight, jnp.float32)
    sides = []
    for half in range(2):
        side = jnp.concatenate([values[half], half_lanes(ones, half)], axis=1)
        sides.append(side.astype(jnp.bfloat16))
    return sides


def state_sides(state, weight):
    totals = jnp.broadcast_to(state[64:65].astype(jnp.float32) * weight, (64, LANES))
    totals = totals.astype(jnp.bfloat16)
    none = jnp.zeros_like(totals)
    return [
        stacked([state[:64], none, totals, none]),
        stacked([none, state[:64], none, totals]),
    ]


def pairs_of(sizes, g):
    return range(g * sizes.each // 2, (g + 1) * sizes.each // 2)


def attend_kernel(sizes, rot_ref, phi_ref, halo_ref, state_ref, meta_ref, keys_ref, att_ref, den_ref):
    shard = sizes.shard
    near, far = near_and_far(sizes, meta_ref, keys_ref)
    reach = meta_ref[:, 3:4]
    for g in range(sizes.kv):
        pairs = pairs_of(sizes, g)
        count = len(pairs)
        near_all, far_all = stacked([near] * count), stacked([far] * count)
        keys, values, phi_key = with_halo(sizes, rot_ref, phi_ref, halo_ref, g)
        value_pair = value_sides(values, 1.0)
        state_pair = state_sides(state_ref[g], 1.0)
        queries = stacked([group(rot_ref, p) for p in pairs])
        total = None
        for half in range(2):
            scores = right_dot(queries, keys[half].astype(jnp.bfloat16)) * 0.125
            phi = stacked([group(phi_ref, 2 * p + half) for p in pairs])
            kernel = right_dot(phi, phi_key)
            weights = jnp.where(near_all, jnp.exp(scores), jnp.where(far_all, kernel, 0.0))
            reached = (phi.astype(jnp.float32) * stacked([reach] * count)).astype(jnp.bfloat16)
            term = forward_product(weights.astype(jnp.bfloat16), value_pair[half])
            term = term + right_dot(reached, state_pair[half])
            total = term if total is None else total + term
        mixed = total[:, :LANES] / total[:, LANES:]
        for turn, p in enumerate(pairs):
            rows = slice(turn * shard, (turn + 1) * shard)
            lanes = slice(p * LANES, (p + 1) * LANES)
            att_ref[:, lanes] = mixed[rows].astype(jnp.bfloat16)
            den_ref[:, lanes] = total[rows, LANES:]


def feature_back(phi, grads):
    phi = phi.astype(jnp.float32)
    return (phi * (grads - half_sums(phi * grads))).astype(jnp.bfloat16)


def unrotated(grads, cos, sin):
    return grads * cos - swapped_halves(grads) * sin


def backward_kernel(sizes, rot_ref, phi_ref, halo_ref, state_ref, meta_ref, keys_ref, att_ref, den_ref, grad_ref, cos_ref, sin_ref, mapq_ref, lin_ref, own_ref, back_ref, carry_ref, map_ref):
    shard = sizes.shard
    near, far = near_and_far(sizes, meta_ref, keys_ref)
    reach = meta_ref[:, 3:4]

    @pl.when(pl.program_id(0) == 0)
    def _():
        map_ref[...] = jnp.zeros_like(map_ref)

    kv_grads = [jnp.zeros((sizes.span, LANES), jnp.float32) for _ in range(sizes.kv_lanes // LANES)]
    for g in range(sizes.kv):
        pairs = pairs_of(sizes, g)
        count = len(pairs)
        near_all, far_all = stacked([near] * count), stacked([far] * count)
        reach_all = stacked([reach] * count)
        keys, values, phi_key = with_halo(sizes, rot_ref, phi_ref, halo_ref, g)
        value_pair = value_sides(values, 1.0 / 32.0)
        state_pair = state_sides(state_ref[g], 1.0 / 32.0)
        queries = stacked([group(rot_ref, p) for p in pairs])
        grads = stacked([group(grad_ref, p) for p in pairs]).astype(jnp.float32)
        mixed = stacked([group(att_ref, p) for p in pairs]).astype(jnp.float32)
        inverse = 1.0 / stacked([group(den_ref, p) for p in pairs])
        grad_num = (grads * inverse).astype(jnp.bfloat16)
        grad_den = -half_sums(grads * mixed) * inverse
        rough = grad_den.astype(jnp.bfloat16)
        rest = (grad_den - rough.astype(jnp.float32)).astype(jnp.bfloat16)
        lane = lane_of(grad_den.shape)
        grad_den = jnp.where(
            lane % 64 < 32, rough.astype(jnp.float32), rest.astype(jnp.float32)
        ).astype(jnp.bfloat16)
        both = jnp.concatenate([grad_num, grad_den], axis=1)
        grad_query = None
        key_sum, value_sum, phi_sum, state_sum = [], [], None, []
        back = [[None, None] for _ in pairs]
        for half in range(2):
            key_half = keys[half].astype(jnp.bfloat16)
            scores = right_dot(queries, key_half) * 0.125
            phi = stacked([group(phi_ref, 2 * p + half) for p in pairs])
            kernel = right_dot(phi, phi_key)
            powers = jnp.exp(scores)
            weights = jnp.where(near_all, powers, jnp.where(far_all, kernel, 0.0))
            weights = weights.astype(jnp.bfloat16)
            grad_weights = right_dot(both, value_pair[half])
            grad_scores = jnp.where(near_all, grad_weights * powers, 0.0).astype(jnp.bfloat16)
            grad_kernel = jnp.where(far_all, grad_weights, 0.0).astype(jnp.bfloat16)
            term = forward_product(grad_scores, key_half)
            grad_query = term if grad_query is None else grad_query + term
            key_sum.append(left_dot(grad_scores, queries))
            value_sum.append(left_dot(weights, grad_num))
            term = left_dot(grad_kernel, phi)
            phi_sum = term if phi_sum is None else phi_sum + term
            reached = (phi.astype(jnp.float32) * reach_all).astype(jnp.bfloat16)
            state_sum.append(left_dot(both, reached))
            grad_phi = forward_product(grad_kernel, phi_key)
            grad_phi = grad_phi + forward_product(both, state_pair[half]) * reach_all
            projected = feature_back(phi, grad_phi)
            for turn in range(count):
                back[turn][half] = projected[turn * shard : (turn + 1) * shard]
        for turn, p in enumerate(pairs):
            pair = jnp.concatenate(back[turn], axis=1)
            grad = grad_query[turn * shard : (turn + 1) * shard] * 0.125
            grad = grad + right_dot(pair, mapq_ref[p])
            grad = unrotated(grad, group(cos_ref, p), group(sin_ref, p))
            lin_ref[:, p * LANES : (p + 1) * LANES] = grad.astype(jnp.bfloat16)
            map_ref[p] += left_dot(group(rot_ref, p), pair)
        for (at, half), sums, scale in (
            (sizes.key_place(g), key_sum, 0.125),
            (sizes.value_place(g), value_sum, 1.0),
        ):
            total = in_half(sums[0], 0, half) + in_half(sums[1], 1, half)
            kv_grads[at] = kv_grads[at] + total * scale
        low, high = state_sum
        totals = low[128:129] + low[160:161] + high[192:193] + high[224:225]
        state_grad = stacked(
            [low[:64] + high[64:128], jnp.broadcast_to(totals, (STATE_ROWS - 64, LANES))]
        )
        carry_ref[g] = state_grad.astype(jnp.bfloat16)
        at = sizes.kv_lanes + g * LANES
        own_ref[:, at : at + LANES] = phi_sum[WIN:]
        back_ref[:, at : at + LANES] = phi_sum[:WIN].astype(jnp.bfloat16)
    for at, grads in enumerate(kv_grads):
        lanes = slice(at * LANES, (at + 1) * LANES)
        own_ref[:, lanes] = grads[WIN:]
        back_ref[:, lanes] = grads[:WIN].astype(jnp.bfloat16)


def key_kernel(sizes, rot_ref, phi_ref, meta_ref, own_ref, back_ref, whole_ref, first_ref, cos_ref, sin_ref, mapk_ref, lin_ref, map_ref):
    shard = sizes.shard

    @pl.when(pl.program_id(0) == 0)
    def _():
        map_ref[...] = jnp.zeros_like(map_ref)

    total = own_ref[...]
    returned = back_ref[...].astype(jnp.float32)
    if shard > WIN:
        total = stacked([total[: shard - WIN], total[shard - WIN :] + returned])
    else:
        total = total + returned
    kv_groups = sizes.kv_lanes // LANES
    kv_grads = [group(total, at) for at in range(kv_groups)]
    back = []
    for g in range(sizes.kv):
        at, half = sizes.value_place(g)
        values = in_half(group(rot_ref, sizes.query_groups + at).astype(jnp.float32), half, 0)
        values = jnp.where(lane_of(values.shape) == 64, 1.0, values).astype(jnp.bfloat16)
        phi = group(phi_ref, sizes.heads + g)
        grad_phi = total[:, sizes.kv_lanes + g * LANES : sizes.kv_lanes + (g + 1) * LANES]
        grad_value = None
        for column, ref in ((0, whole_ref), (1, first_ref)):
            keep = meta_ref[:, column : column + 1]
            state = stacked([ref[g], jnp.zeros((LANES - STATE_ROWS, LANES), jnp.bfloat16)])
            grad_phi = grad_phi + forward_product(values, state) * keep
            term = right_dot(phi, state) * keep
            grad_value = term if grad_value is None else grad_value + term
        kv_grads[at] = kv_grads[at] + in_half(grad_value, 0, half)
        back.append(feature_back(phi, grad_phi))
    if len(back) % 2:
        back.append(jnp.zeros_like(back[0]))
    for index in range(sizes.key_groups):
        pair = jnp.concatenate(back[2 * index : 2 * index + 2], axis=1)
        kv_grads[index] = kv_grads[index] + right_dot(pair, mapk_ref[index])
        map_ref[index] += left_dot(group(rot_ref, sizes.query_groups + index), pair)
    for at in range(kv_groups):
        cos = group(cos_ref, sizes.query_groups + at)
        sin = group(sin_ref, sizes.query_groups + at)
        lanes = slice(at * LANES, (at + 1) * LANES)
        lin_ref[:, lanes] = unrotated(kv_grads[at], cos, sin).astype(jnp.bfloat16)


def told(microseconds):
    return pl.CostEstimate(
        flops=int(microseconds * 500_000_000), bytes_accessed=0, transcendentals=0
    )


def by_row(kernel, name, rows, inputs, outputs, microseconds):
    def spec(shape, kind):
        rest = tuple(shape[1:])
        none = (0,) * len(rest)
        if kind == "all":
            return pl.BlockSpec(shape, lambda r: (0,) + none)
        first = shape[0] // rows if kind == "flat" else None
        return pl.BlockSpec((first,) + rest, lambda r: (r,) + none)

    return pl.pallas_call(
        kernel,
        grid=(rows,),
        in_specs=[spec(a.shape, kind) for a, kind in inputs],
        out_specs=[spec(shape.shape, kind) for shape, kind in outputs],
        out_shape=[shape for shape, _ in outputs],
        compiler_params=pltpu.CompilerParams(vmem_limit_bytes=48 * 1024 * 1024),
        cost_estimate=told(microseconds),
        name=name,
    )(*[a for a, _ in inputs])


def map_pairs(maps):
    count = maps.shape[0]
    wide = jnp.concatenate([maps, -maps], axis=2)
    if count % 2:
        wide = jnp.concatenate([wide, jnp.zeros_like(wide[:1])], axis=0)
    wide = wide.reshape(-1, 2, 64, LANES)
    none = jnp.zeros_like(wide[:, 0])
    return jnp.concatenate(
        [
            jnp.concatenate([wide[:, 0], none], axis=2),
            jnp.concatenate([none, wide[:, 1]], axis=2),
        ],
        axis=1,
    )


def maps_from_pairs(pairs, count):
    first = pairs[:, :64, :64] - pairs[:, :64, 64:128]
    second = pairs[:, 64:, 128:192] - pairs[:, 64:, 192:]
    return jnp.stack([first, second], axis=1).reshape(-1, 64, 64)[:count]


def rope_tables(positions, sizes):
    inverse = rope_base ** (-jnp.arange(0, 64, 2, dtype=jnp.float32) / 64)
    angle = positions.astype(jnp.float32)[:, None] * inverse[None, :]
    cosine, sine = jnp.cos(angle), jnp.sin(angle)
    turning = sizes.heads + sizes.kv
    cosine = jnp.tile(jnp.concatenate([cosine, cosine], axis=1), (1, turning))
    sine = jnp.tile(jnp.concatenate([-sine, sine], axis=1), (1, turning))
    rest = (positions.shape[0], sizes.kv * 64)
    return (
        jnp.concatenate([cosine, jnp.ones(rest, jnp.float32)], axis=1),
        jnp.concatenate([sine, jnp.zeros(rest, jnp.float32)], axis=1),
    )


def fixed(shape):
    return pl.BlockSpec(shape, lambda t: (0,) * len(shape), pipeline_mode=pl.Buffered(1))


def kernel_params():
    return pltpu.CompilerParams(vmem_limit_bytes=56 * 1024 * 1024)


def mlp_forward(rows, cotangent, weights, microseconds):
    count, width = rows.shape
    chunk = weights.shape[1] // 3
    tile = min(256, chunk)
    tiles = chunk // tile
    part = min(512, count)

    def kernel(x_ref, c_ref, gate_ref, up_ref, down_ref, grad_gate_ref, grad_up_ref, inner_ref):
        def one(turn, nothing):
            at = pl.ds(pl.multiple_of(turn * part, part), part)
            x = x_ref[at, :]
            gate = forward_product(x, gate_ref[...])
            up = forward_product(x, up_ref[...])
            grad_inner = forward_product(c_ref[at, :], down_ref[...])
            sigmoid = 1.0 / (1.0 + jnp.exp(-gate))
            swish = gate * sigmoid
            grad_gate = grad_inner * up * (sigmoid * (1.0 + gate * (1.0 - sigmoid)))
            grad_gate_ref[at, :] = grad_gate.astype(jnp.bfloat16)
            grad_up_ref[at, :] = (grad_inner * swish).astype(jnp.bfloat16)
            inner_ref[at, :] = (swish * up).astype(jnp.bfloat16)
            return nothing

        lax.fori_loop(0, count // part, one, 0)

    def columns(shift):
        return pl.BlockSpec((width, tile), lambda t: (0, t + shift))

    out = pl.BlockSpec((count, tile), lambda t: (0, t))
    shape = jax.ShapeDtypeStruct((count, chunk), jnp.bfloat16)
    return pl.pallas_call(
        kernel,
        grid=(tiles,),
        in_specs=[fixed(rows.shape), fixed(cotangent.shape)]
        + [columns(shift * tiles) for shift in range(3)],
        out_specs=[out] * 3,
        out_shape=[shape] * 3,
        compiler_params=kernel_params(),
        cost_estimate=told(microseconds),
        name="hidden_units",
    )(rows, cotangent, weights, weights, weights)


def turned_product(terms, before, dtype, microseconds):
    count, width = terms[0][0].shape[0], terms[0][1].shape[0]
    tile = min(512, width)

    def kernel(*refs):
        total = None if before is None else refs[-2][...]
        for left_ref, weight_ref in zip(refs, refs[len(terms) : 2 * len(terms)], strict=False):
            term = right_dot(left_ref[...], weight_ref[...])
            total = term if total is None else total + term
        refs[-1][...] = total.astype(dtype)

    def rows_of(section, chunk):
        return pl.BlockSpec((tile, chunk), lambda t: (t, section))

    out = pl.BlockSpec((count, tile), lambda t: (0, t))
    lefts = [left for left, _, _ in terms]
    return pl.pallas_call(
        kernel,
        grid=(width // tile,),
        in_specs=[fixed(left.shape) for left in lefts]
        + [rows_of(section, left.shape[1]) for left, _, section in terms]
        + ([] if before is None else [out]),
        out_specs=out,
        out_shape=jax.ShapeDtypeStruct((count, width), dtype),
        compiler_params=kernel_params(),
        cost_estimate=told(microseconds),
        name="turned_product",
    )(*lefts, *[weights for _, weights, _ in terms], *([] if before is None else [before]))


def weight_gradients(rows, cotangent, grad_gate, grad_up, inner, microseconds):
    count, width = rows.shape
    chunk = inner.shape[1]
    tile = min(512, width)

    def kernel(x_ref, c_ref, gate_ref, up_ref, inner_ref, out_ref):
        sides = ((x_ref, gate_ref), (x_ref, up_ref), (c_ref, inner_ref))
        for at, (left_ref, right_ref) in enumerate(sides):
            total = left_dot(left_ref[...], right_ref[...])
            out_ref[:, at * chunk : (at + 1) * chunk] = total.astype(jnp.bfloat16)

    column = pl.BlockSpec((count, tile), lambda t: (0, t))
    return pl.pallas_call(
        kernel,
        grid=(width // tile,),
        in_specs=[column, column] + [fixed(inner.shape)] * 3,
        out_specs=pl.BlockSpec((tile, 3 * chunk), lambda t: (t, 0)),
        out_shape=jax.ShapeDtypeStruct((width, 3 * chunk), jnp.bfloat16),
        compiler_params=kernel_params(),
        cost_estimate=told(microseconds),
        name="weight_gradients",
    )(rows, cotangent, grad_gate, grad_up, inner)


def document_facts(document_index, shard):
    seq_index = lax.axis_index("seq")
    count = lax.axis_size("seq")
    rows = document_index.shape[0]
    documents = document_index.astype(jnp.float32)
    missing = jnp.full((rows, 1), -1.0, jnp.float32)

    def last_of(block):
        at = jnp.clip(block * shard + shard - 1, 0, count * shard - 1)
        found = lax.dynamic_slice_in_dim(documents, at, 1, 1)
        return jnp.where((block >= 0) & (block < count), found, missing)

    def carried_of(block):
        at = jnp.clip(block * shard - WIN - 1, 0, count * shard - 1)
        found = lax.dynamic_slice_in_dim(documents, at, 1, 1)
        return jnp.where((block >= 1) & (block < count), found, missing - 1.0)

    padded = jnp.concatenate([jnp.broadcast_to(missing, (rows, WIN)), documents], axis=1)
    key_documents = lax.dynamic_slice_in_dim(padded, seq_index * shard, shard + WIN, 1)
    own = key_documents[:, WIN:]
    position = jnp.arange(shard)[None, :]
    keep_whole = own == own[:, shard - 1 :]
    keep_first = (position < shard - WIN) & (own == own[:, shard - WIN - 1 : shard - WIN])
    reach = own == carried_of(seq_index)
    columns = [keep_whole, keep_first, own, reach]
    meta = jnp.stack([column.astype(jnp.float32) for column in columns], axis=-1)
    meta = jnp.concatenate([meta, jnp.zeros_like(meta)], axis=-1)
    return meta, key_documents[:, None, :], last_of, carried_of


def masked(block, mask):
    return block.astype(jnp.float32) * mask.astype(jnp.float32).reshape(-1, 1, 1, 1)


class Carries:
    def __init__(self, last_of, carried_of, rows):
        self.index = lax.axis_index("seq")
        self.count = lax.axis_size("seq")
        self.even = self.index % 2 == 0
        self.rows = rows // 2
        self.pair = self.index - self.index % 2
        self.last_of, self.carried_of = last_of, carried_of
        self.steps = []
        distance = 1
        while distance < self.count // 2:
            self.steps.append(distance)
            distance *= 2

    def half(self, values, own):
        at = jnp.where(self.even == own, 0, self.rows)
        return lax.dynamic_slice_in_dim(values, at, self.rows, 0)

    def end(self, back):
        return self.half(self.last_of(self.pair - back), True)

    def other(self, values):
        values = values.astype(jnp.bfloat16)
        return lax.ppermute(values, "seq", [(i, i ^ 1) for i in range(self.count)])

    def pick(self, first, second):
        return jnp.where(self.even, first.astype(jnp.float32), second.astype(jnp.float32))

    def split(self, values):
        mine, theirs = self.half(values, True), self.other(self.half(values, False))
        return self.pick(mine, theirs), self.pick(theirs, mine)

    def join(self, even, odd):
        kept, got = self.pick(even, odd), self.other(self.pick(odd, even))
        return jnp.concatenate([self.pick(kept, got), self.pick(got, kept)], axis=0)

    def reach(self):
        even = self.half(self.carried_of(self.pair), True) == self.end(2)
        odd = self.half(self.carried_of(self.pair + 1), True) == self.end(1)
        return even, odd

    def forward(self, whole, first):
        before = shifted(first, 1)
        even, odd = self.split(whole)
        window = odd + masked(even, self.end(0) == self.end(-1))
        sums = None
        for distance in self.steps:
            if sums is None:
                got = shifted(jnp.stack([window, even]).astype(jnp.bfloat16), 2)
                got = got.astype(jnp.float32)
                sums = got[1], got[0]
                got = got[0]
            else:
                got = shifted(window.astype(jnp.bfloat16), 2 * distance)
                there = self.end(2 * distance - 1)
                sums = (
                    sums[0] + masked(got, there == self.end(2)),
                    sums[1] + masked(got, there == self.end(1)),
                )
            window = window + masked(got, self.end(2 * distance - 1) == self.end(-1))
        reach = self.reach()
        total = self.join(masked(sums[0], reach[0]), masked(sums[1], reach[1]))
        return (total + before.astype(jnp.float32)).astype(jnp.bfloat16)

    def backward(self, grads):
        first = shifted(grads, -1)
        even, odd = self.split(grads)
        reach = self.reach()
        even, odd = masked(even, reach[0]), masked(odd, reach[1])
        window = None
        for distance in reversed(self.steps):
            there = self.end(2 * distance - 1)
            linked = 0.0 if window is None else masked(window, there == self.end(-1))
            if distance == 1:
                sent = jnp.stack([linked + odd, even]).astype(jnp.bfloat16)
                got = shifted(sent, -2).astype(jnp.float32)
                window = got[0] if window is None else window + got[0]
                direct = got[1]
            else:
                sent = linked + masked(odd, there == self.end(1))
                sent = sent + masked(even, there == self.end(2))
                got = shifted(sent.astype(jnp.bfloat16), -2 * distance).astype(jnp.float32)
                window = got if window is None else window + got
        even = masked(window, self.end(0) == self.end(-1)) + direct
        return self.join(even, window).astype(jnp.bfloat16), first


def body(
    tokens,
    cotangent,
    first_norm_gain,
    second_norm_gain,
    query_weight,
    key_weight,
    value_weight,
    output_weight,
    gate_weight,
    up_weight,
    down_weight,
    adapter_down_weight,
    adapter_query_weight,
    adapter_key_weight,
    adapter_value_weight,
    adapter_output_down,
    adapter_output_up,
    hedgehog_query_weight,
    hedgehog_key_weight,
    document_index,
):
    row_count, shard, width = tokens.shape
    seq_index = lax.axis_index("seq")
    heads_here = hedgehog_query_weight.shape[0]
    kv_here = hedgehog_key_weight.shape[0]
    sizes = Sizes(shard, heads_here, kv_here)
    rank = adapter_query_weight.shape[0]
    tokens_here = row_count * shard
    block_rows = query_weight.shape[0]
    hidden_units = gate_weight.shape[1]
    chunk = hidden_units // MLP_CHUNKS
    query_width, key_width = query_weight.shape[1], key_weight.shape[1]
    key_end = query_width + key_width

    out_width = output_weight.shape[0]
    first_gather = Gather(
        jnp.concatenate([query_weight, key_weight, value_weight, output_weight.T], axis=1)
    )
    first_gather.advance(quarters=4)
    down_turned = down_weight.T
    gathers = []
    for turn in range(MLP_CHUNKS):
        span = slice(turn * chunk, (turn + 1) * chunk)
        gathers.append(
            Gather(
                jnp.concatenate(
                    [gate_weight[:, span], up_weight[:, span], down_turned[:, span]], axis=1
                )
            )
        )
    early, late = gathers
    early.advance(*first_gather.found[first_gather.half])
    complete_qkv, out_turned = first_gather.assemble(sizes.linear, out_width)

    adapters = jnp.zeros((3 * rank, sizes.linear), jnp.bfloat16)
    adapters = lax.dynamic_update_slice(adapters, adapter_query_weight, (0, 0))
    adapters = lax.dynamic_update_slice(adapters, adapter_key_weight, (rank, query_width))
    adapters = lax.dynamic_update_slice(adapters, adapter_value_weight, (2 * rank, key_end))
    positions = seq_index * shard + jnp.arange(shard)
    cosine, sine = rope_tables(positions, sizes)
    map_query, map_key = map_pairs(hedgehog_query_weight), map_pairs(hedgehog_key_weight)
    meta, key_documents, last_of, carried_of = document_facts(document_index, shard)

    flattened = tokens.reshape(tokens_here, width).astype(jnp.float32)
    scale_one = lax.rsqrt(jnp.mean(flattened * flattened, axis=-1, keepdims=True) + epsilon)
    normalized_input = flattened * scale_one * first_norm_gain.astype(jnp.float32)
    normalized_input = normalized_input.astype(jnp.bfloat16)
    lowrank_input = forward_product(normalized_input, adapter_down_weight).astype(jnp.bfloat16)
    linear = forward_product(normalized_input, complete_qkv) + adapter_scale * forward_product(
        lowrank_input, adapters
    )
    low = functools.partial(jax.ShapeDtypeStruct, dtype=jnp.bfloat16)
    wide = functools.partial(jax.ShapeDtypeStruct, dtype=jnp.float32)
    phi_lanes = (heads_here + kv_here) * LANES
    states = low((row_count, kv_here, STATE_ROWS, LANES))
    rotated, phi, tail, whole, first = by_row(
        functools.partial(prepare_kernel, sizes),
        "prepare",
        row_count,
        [
            (linear, "flat"),
            (cosine, "all"),
            (sine, "all"),
            (meta, "row"),
            (map_query, "all"),
            (map_key, "all"),
        ],
        [
            (low((tokens_here, sizes.linear)), "flat"),
            (low((tokens_here, phi_lanes)), "flat"),
            (low((row_count, WIN, sizes.halo_lanes)), "row"),
            (states, "row"),
            (states, "row"),
        ],
        16,
    )
    tail, whole, first = after((tail, whole, first), *early.edge())
    halo = shifted(tail, 1)
    carries = Carries(last_of, carried_of, row_count)
    carry = carries.forward(whole, first)
    early.advance(carry, halo)
    attended, denominator = by_row(
        functools.partial(attend_kernel, sizes),
        "attend",
        row_count,
        [
            (rotated, "flat"),
            (phi, "flat"),
            (halo, "row"),
            (carry, "row"),
            (meta, "row"),
            (key_documents, "row"),
        ],
        [
            (low((tokens_here, query_width)), "flat"),
            (wide((tokens_here, query_width)), "flat"),
        ],
        8,
    )

    lowrank_output = forward_product(attended, adapter_output_down).astype(jnp.bfloat16)
    out_part = right_dot(attended, out_turned) + adapter_scale * forward_product(
        lowrank_output, adapter_output_up
    )
    out_part = after(out_part.astype(jnp.bfloat16), *early.edge())
    early.advance(out_part)
    own_rows = row_count // lax.axis_size("head")
    first_row = lax.axis_index("head") * own_rows
    own_tokens = lax.dynamic_slice_in_dim(tokens, first_row, own_rows, 0)
    own_tokens = own_tokens.reshape(own_rows * shard, width).astype(jnp.float32)
    own_cotangent = lax.dynamic_slice_in_dim(cotangent, first_row, own_rows, 0)
    own_cotangent = own_cotangent.reshape(own_rows * shard, width).astype(jnp.float32)
    out_sum = head_scatter(out_part)
    hidden_state = own_tokens + out_sum
    scale_two = lax.rsqrt(jnp.mean(hidden_state * hidden_state, axis=-1, keepdims=True) + epsilon)
    unit_two = hidden_state * scale_two
    own_normed = (unit_two * second_norm_gain.astype(jnp.float32)).astype(jnp.bfloat16)
    own_normed = after(own_normed, *early.edge())
    early.advance(own_normed)
    late.advance(own_normed)
    normed_rows = head_gather(own_normed)

    grad_out = cotangent.reshape(tokens_here, width)

    (weights_early,) = early.assemble(3 * chunk)
    gate_early, up_early, inner_early = mlp_forward(normed_rows, grad_out, weights_early, 22)
    gate_early = after(gate_early, *late.edge())
    late.advance()
    part_early = turned_product(
        [(gate_early, weights_early, 0), (up_early, weights_early, 1)], None, jnp.float32, 14
    )
    grads_early = weight_gradients(
        normed_rows, grad_out, gate_early, up_early, after(inner_early, part_early), 19
    )
    grads_early = after(grads_early, *late.edge())
    late.advance()
    scatter_early = Scatter([grads_early], block_rows)
    scatter_early.advance(*late.edge())
    late.advance()
    (weights_late,) = late.assemble(3 * chunk)
    gate_late, up_late, inner_late = mlp_forward(normed_rows, grad_out, weights_late, 22)
    gate_late = after(gate_late, *scatter_early.edge())
    scatter_early.advance()
    normed_two_part = turned_product(
        [(gate_late, weights_late, 0), (up_late, weights_late, 1)], part_early, jnp.bfloat16, 14
    )
    both_cores = head_pair_sum(normed_two_part)
    scatter_early.advance(normed_two_part)
    grads_late = weight_gradients(
        normed_rows, grad_out, gate_late, up_late, after(inner_late, both_cores), 19
    )
    grad_normed_two = head_finish(both_cores)
    scatter_late = Scatter([grads_late], block_rows)
    scatter_late.advance(*scatter_early.edge())
    scatter_early.advance(grads_late)
    grad_gain_two = jnp.sum(grad_normed_two * unit_two, axis=0, keepdims=True)
    inner_two = grad_normed_two * second_norm_gain.astype(jnp.float32)
    grad_hidden = own_cotangent + scale_two * (
        inner_two - unit_two * jnp.mean(inner_two * unit_two, axis=-1, keepdims=True)
    )
    grad_branch = head_gather(grad_hidden.astype(jnp.bfloat16))
    down_part = turned_product(
        [(inner_early, weights_early, 2), (after(inner_late, grads_late), weights_late, 2)],
        None,
        jnp.bfloat16,
        13,
    )
    down_sum = head_finish(head_pair_sum(down_part), grad_branch)
    scatter_late.advance(grad_hidden)
    grad_branch = after(grad_branch, *scatter_late.edge())
    scatter_late.advance()
    out_up_gradient = adapter_scale * left_dot(lowrank_output, grad_branch)
    grad_w_out = left_dot(grad_branch, attended).astype(jnp.bfloat16)
    grad_lowrank_out = adapter_scale * right_dot(grad_branch, adapter_output_up)
    grad_lowrank_out = grad_lowrank_out.astype(jnp.bfloat16)
    out_down_gradient = left_dot(grad_lowrank_out, attended)
    grad_attended = forward_product(grad_branch, out_turned) + right_dot(
        grad_lowrank_out, adapter_output_down
    )

    own_lanes = sizes.halo_lanes
    grad_query_lin, own_grads, back, carry_grads, map_query_pairs = by_row(
        functools.partial(backward_kernel, sizes),
        "backward",
        row_count,
        [
            (rotated, "flat"),
            (phi, "flat"),
            (halo, "row"),
            (carry, "row"),
            (meta, "row"),
            (key_documents, "row"),
            (attended, "flat"),
            (denominator, "flat"),
            (grad_attended.astype(jnp.bfloat16), "flat"),
            (cosine, "all"),
            (sine, "all"),
            (map_query, "all"),
        ],
        [
            (low((tokens_here, query_width)), "flat"),
            (wide((tokens_here, own_lanes)), "flat"),
            (low((row_count, WIN, own_lanes)), "row"),
            (states, "row"),
            (wide(map_query.shape), "all"),
        ],
        26,
    )
    carry_grads, back = after((carry_grads, back), down_sum, *scatter_late.edge())
    layer_rows = head_gather((hidden_state + down_sum).astype(jnp.bfloat16))
    returned = shifted(back, -1)
    grad_whole, grad_first = carries.backward(carry_grads)
    scatter_late.advance(grad_whole)
    grad_w_query = left_dot(normalized_input, grad_query_lin).astype(jnp.bfloat16)
    query_part = right_dot(grad_query_lin, complete_qkv[:, :query_width])
    grad_key_lin, map_key_pairs = by_row(
        functools.partial(key_kernel, sizes),
        "keys",
        row_count,
        [
            (rotated, "flat"),
            (phi, "flat"),
            (meta, "row"),
            (own_grads, "flat"),
            (returned, "row"),
            (grad_whole, "row"),
            (grad_first, "row"),
            (cosine, "all"),
            (sine, "all"),
            (map_key, "all"),
        ],
        [
            (low((tokens_here, sizes.kv_lanes)), "flat"),
            (wide(map_key.shape), "all"),
        ],
        7,
    )
    grad_linear = jnp.concatenate([grad_query_lin, grad_key_lin], axis=1)
    lowrank_gradient = (adapter_scale * right_dot(grad_linear, adapters)).astype(jnp.bfloat16)
    normed_part = (
        query_part
        + right_dot(grad_key_lin, complete_qkv[:, query_width:])
        + right_dot(lowrank_gradient, adapter_down_weight)
    ).astype(jnp.bfloat16)
    normalized_gradient = head_scatter(after(normed_part, layer_rows))
    grad_w_kv = left_dot(normalized_input, grad_key_lin).astype(jnp.bfloat16)
    last_scatter = Scatter([grad_w_query, grad_w_out, grad_w_kv], block_rows)
    last_scatter.advance(*scatter_late.edge())
    adapter_gradient = adapter_scale * left_dot(lowrank_input, grad_linear)
    down_gradient = left_dot(lowrank_gradient, normalized_input)
    gain_one = normed_part.astype(jnp.float32) * (tokens.reshape(tokens_here, width) * scale_one)
    grad_gain_one = jnp.sum(gain_one, axis=0, keepdims=True)
    own_scale = lax.rsqrt(jnp.mean(own_tokens * own_tokens, axis=-1, keepdims=True) + epsilon)
    own_unit = own_tokens * own_scale
    inner_one = normalized_gradient * first_norm_gain.astype(jnp.float32)
    own_grad_tokens = grad_hidden + own_scale * (
        inner_one - own_unit * jnp.mean(inner_one * own_unit, axis=-1, keepdims=True)
    )
    grad_tokens_rows = head_gather(own_grad_tokens.astype(jnp.bfloat16)).astype(jnp.float32)
    last_sum = last_scatter.total()
    mlp_sums = [scatter_early.total(), scatter_late.total()]

    everywhere = jnp.concatenate(
        [down_gradient, out_up_gradient, grad_gain_one, grad_gain_two], axis=0
    )
    adapter_part = jnp.concatenate(
        [
            adapter_gradient[:rank, :query_width],
            adapter_gradient[rank : 2 * rank, query_width:key_end],
            adapter_gradient[2 * rank :, key_end:],
            out_down_gradient,
        ],
        axis=1,
    )
    maps_part = jnp.concatenate(
        [maps_from_pairs(map_query_pairs, heads_here), maps_from_pairs(map_key_pairs, kv_here)]
    )
    maps_part = jnp.pad(maps_part.reshape(-1, 64), ((0, 0), (0, LANES - 64)))
    small = jnp.concatenate(
        [everywhere.reshape(-1, LANES), adapter_part.reshape(-1, LANES), maps_part], axis=0
    )
    small = after(small.astype(jnp.bfloat16), *scatter_late.edge())
    small = exchange_sum(small, "seq", bits_of("seq"))
    first, second = everywhere.size // LANES, (everywhere.size + adapter_part.size) // LANES
    everywhere = exchange_sum(small[:first], "head", bits_of("head")).astype(jnp.float32)
    everywhere = everywhere.reshape(-1, width)
    small = small.astype(jnp.float32)
    adapter_sum = small[first:second].reshape(adapter_part.shape)
    maps_sum = small[second:, :64].reshape(-1, 64, 64)
    end = 3 * rank + rank

    def columns(at):
        return jnp.concatenate([part[:, at * chunk : (at + 1) * chunk] for part in mlp_sums], axis=1)

    return (
        layer_rows.reshape(row_count, shard, width),
        grad_tokens_rows.reshape(row_count, shard, width),
        everywhere[end],
        everywhere[end + 1],
        last_sum[:, :query_width],
        last_sum[:, query_width + out_width : key_end + out_width],
        last_sum[:, key_end + out_width :],
        last_sum[:, query_width : query_width + out_width].T,
        columns(0),
        columns(1),
        columns(2).T,
        everywhere[: 3 * rank].T,
        adapter_sum[:, :query_width],
        adapter_sum[:, query_width:key_end],
        adapter_sum[:, key_end : sizes.linear],
        adapter_sum[:, sizes.linear :].T,
        everywhere[3 * rank : end],
        maps_sum[:heads_here],
        maps_sum[heads_here:],
    )


def solution(mesh):
    in_specs = (
        P(None, "seq", None),
        P(None, "seq", None),
        P(),
        P(),
        P("seq", "head"),
        P("seq", "head"),
        P("seq", "head"),
        P("head", "seq"),
        P("seq", "head"),
        P("seq", "head"),
        P("head", "seq"),
        P(),
        P(None, "head"),
        P(None, "head"),
        P(None, "head"),
        P("head", None),
        P(),
        P("head", None, None),
        P("head", None, None),
        P(),
    )
    out_specs = (
        P(None, "seq", None),
        P(None, "seq", None),
        P(),
        P(),
        P("seq", "head"),
        P("seq", "head"),
        P("seq", "head"),
        P("head", "seq"),
        P("seq", "head"),
        P("seq", "head"),
        P("head", "seq"),
        P(),
        P(None, "head"),
        P(None, "head"),
        P(None, "head"),
        P("head", None),
        P(),
        P("head", None, None),
        P("head", None, None),
    )
    return jax.shard_map(body, mesh=mesh, in_specs=in_specs, out_specs=out_specs, check_vma=False)
```

time: 1550 us -> 903 us (0.58)
  matrix products: 261 us -> 46.4 us
  Pallas kernels: 0 us -> 191 us
  blocking collectives: 183 us -> 0 us
  waiting for transfers between devices: 527 us -> 349 us
  local copies, waits for them, and re-layouts: 250 us -> 120 us
  other arithmetic: 171 us -> 96.3 us
  between operations: 30.3 us -> 2.9 us
  starting transfers between devices: 115 us -> 90.1 us
    pallas_call x0 -> x14, Pallas kernels: none -> 191 us  [the longest x4 57.9 us: by_row(): pl.pallas_call(kernel, grid=(rows,), in_specs=[spec(a.shape, kind) for a,...]
    ppermute x96 -> x48, waiting for transfers between devices: 382 us -> 212 us  [ring_move(): lax.ppermute(block, 'seq', [(order[i], order[(i + step) % count]) for i i...]
    psum x2 -> x0, blocking collectives: 76.7 us -> none  [the longest x1 41.5 us: body(): lax.psum(part.astype(jnp.bfloat16), ('seq', 'head')).astype(jnp.float32)]
    psum x2 -> x0, waiting for transfers between devices: 73.3 us -> none  [the longest x1 73.3 us: body(): lax.psum(part.astype(jnp.bfloat16), ('seq', 'head')).astype(jnp.float32)]
    ppermute x6 -> x17, waiting for transfers between devices: 7.1 us -> 75.5 us  [the longest x8 44.2 us: shifted(): return lax.ppermute(block, 'seq', route)]
    dynamic_update_slice x92 -> x2, local copies, waits for them, and re-layouts: 67.7 us -> 1.16 us  [the longest x1 0.58 us: body(): lax.dynamic_update_slice(adapters, adapter_key_weight, (rank, query_width))]
    dot_general x24 -> x0, matrix products: 66.5 us -> none  [the longest x1 8.3 us: body(): jnp.einsum('rthf,hdf->rthd', grad_proj_q, hedgehog_query_weight, preferre...]
    all_gather x2 -> x0, blocking collectives: 65 us -> none  [the longest x1 32.8 us: carried_in(): pieces = jax.tree.map(lambda part: lax.all_gather(part, axis), value)]
  transfers between devices with their start and end apart: 126 -> 85, of which waited for: 57 -> 42; matrix products, arithmetic and copies ran while one was open for 32% -> 22% of each run, Pallas kernels for 0% -> 20%
where the time goes in v2:
time: 903 us; the launch traced here: 895 us
  waiting for transfers between devices  349 us (39%)
  Pallas kernels  191 us (21%)
  local copies, waits for them, and re-layouts  120 us (13%)
  other arithmetic  96.3 us (11%)
  starting transfers between devices  90.1 us (10%)
  matrix products  46.4 us (5%)
    ppermute x48, waiting for transfers between devices, ring_move(): lax.ppermute(block, 'seq', [(order[i], order[(i + step) % count]) for i i...  212 us
    pallas_call x4, Pallas kernels, by_row(): pl.pallas_call(kernel, grid=(rows,), in_specs=[spec(a.shape, kind) for a,...  57.9 us
    ppermute x8, waiting for transfers between devices, chip_move(): lax.ppermute(block, 'head', [(i, (i + 2 * step) % count) for i in range(c...  56.9 us
    ppermute x48, starting transfers between devices, ring_move(): lax.ppermute(block, 'seq', [(order[i], order[(i + step) % count]) for i i...  54.1 us
    ppermute x8, waiting for transfers between devices, shifted(): return lax.ppermute(block, 'seq', route)  44.2 us
    pallas_call x3, Pallas kernels, turned_product(): pl.pallas_call(kernel, grid=(width // tile,), in_specs=[fixed(left.shape)...  41.8 us
    pallas_call x2, Pallas kernels, mlp_forward(): pl.pallas_call(kernel, grid=(tiles,), in_specs=[fixed(rows.shape), fixed(...  41.5 us
    pallas_call x2, Pallas kernels, weight_gradients(): pl.pallas_call(kernel, grid=(width // tile,), in_specs=[column, column] +...  39.3 us
  transfers between devices with their start and end apart: 85, of which 42 were waited for; matrix products, arithmetic and copies ran while one was open for 22% of the time, Pallas kernels for 20%

profile of v2, /device:TPU:0, one launch (start us, length us, event | category | flops | bytes accessed | tf_op | source)
XLA Modules:
  0.0 895.3 jit_solution(10131058957327176667)
XLA Ops:
  26.4 10.2 %collective-permute-done.1.refs_1_ = bf16[256,1280]{1,0:T(8,128)(2,1)} collective-permute-done((bf16[256,1280]{1,0:T(8,128)(2,1)S(1)}, bf16[256,1280]{1,0:T(8,128)(2,1)}, u32[]{:S(2)}, u32[]{:S(2)}) %collective-permute-start.1) | collective-permute-done | bytes 655392 | tf_op jit(solution)/shard_map/ppermute | solution.py:49
  84.9 16.5 %prepare.1 = (bf16[1024,768]{1,0:T(8,128)(2,1)S(1)}, bf16[1024,1280]{1,0:T(8,128)(2,1)}, bf16[8,64,512]{2,1,0:T(8,128)(2,1)S(1)}, bf16[8,2,80,128]{3,2,1,0:T(8,128)(2,1)S(1)}, bf16[8,2,80,128]{3,2,1,0:T(8,128)(2,1)S(1)}) custom-call(f32[1024,768]{1,0:T(8,128)} %multiply_add_fusion.lin_ref, f32[128,768]{1,0:T(8,128)S(1)} %copy-done.28, ...), custom_call_target="tpu_custom_call" | custom-call | flops 8000000000 | tf_op jit(solution)/shard_map/prepare/pallas_call | solution.py:595
  145.2 10.2 %collective-permute-done.10.halo_ref = bf16[8,64,512]{2,1,0:T(8,128)(2,1)S(1)} collective-permute-done((bf16[8,64,512]{2,1,0:T(8,128)(2,1)}, bf16[8,64,512]{2,1,0:T(8,128)(2,1)S(1)}, u32[]{:S(2)}, u32[]{:S(2)}) %collective-permute-start.10) | collective-permute-done | bytes 524320 | tf_op jit(solution)/shard_map/ppermute | solution.py:39
  173.9 10.4 %collective-permute-done.17.refs_5_ = bf16[256,3072]{1,0:T(8,128)(2,1)} collective-permute-done((bf16[256,3072]{1,0:T(8,128)(2,1)S(1)}, bf16[256,3072]{1,0:T(8,128)(2,1)}, u32[]{:S(2)}, u32[]{:S(2)}) %collective-permute-start.17) | collective-permute-done | bytes 1572896 | tf_op jit(solution)/shard_map/ppermute | solution.py:49
  200.2 21.0 %collective-permute-done.19 = bf16[256,2048]{1,0:T(8,128)(2,1)} collective-permute-done((bf16[256,2048]{1,0:T(8,128)(2,1)}, bf16[256,2048]{1,0:T(8,128)(2,1)}, u32[]{:S(2)}, u32[]{:S(2)}) %collective-permute-start.19) | collective-permute-done | bytes 1048608 | tf_op jit(solution)/shard_map/ppermute | solution.py:199
  242.9 14.1 %collective-permute-done.26.refs_8_ = bf16[128,3072]{1,0:T(8,128)(2,1)S(1)} collective-permute-done((bf16[128,3072]{1,0:T(8,128)(2,1)S(1)}, bf16[128,3072]{1,0:T(8,128)(2,1)S(1)}, u32[]{:S(2)}, u32[]{:S(2)}) %collective-permute-start.26) | collective-permute-done | bytes 786464 | tf_op jit(solution)/shard_map/ppermute | solution.py:49
  264.0 26.4 %collective-permute-done.25.refs_7_ = bf16[128,3072]{1,0:T(8,128)(2,1)} collective-permute-done((bf16[128,3072]{1,0:T(8,128)(2,1)}, bf16[128,3072]{1,0:T(8,128)(2,1)}, u32[]{:S(2)}, u32[]{:S(2)}) %collective-permute-start.25) | collective-permute-done | bytes 786464 | tf_op jit(solution)/shard_map/ppermute | solution.py:49
  306.1 20.7 %hidden_units.2 = (bf16[1024,1024]{1,0:T(8,128)(2,1)}, bf16[1024,1024]{1,0:T(8,128)(2,1)}, bf16[1024,1024]{1,0:T(8,128)(2,1)}) custom-call(bf16[1024,2048]{1,0:T(8,128)(2,1)} %bitcast.38.x_ref, bf16[1024,2048]{1,0:T(8,128)(2,1)} %bitcast.285, bf16[2048,3072]{1,0:T(8,128)(2,1)} %copy-done.1, bf16[2048,3072]{1,0:T(8,128)(2,1)} %copy-done.1, ...), custom_call_target="tpu_custom_call" | custom-call | flops 11000000512 | tf_op jit(solution)/shard_map/hidden_units/pallas_call | solution.py:680
  337.5 13.7 %turned_product.3.refs_4_ = f32[1024,2048]{1,0:T(8,128)} custom-call(bf16[1024,1024]{1,0:T(8,128)(2,1)} %get-tuple-element.104.refs_0_.gate_ref, bf16[1024,1024]{1,0:T(8,128)(2,1)} %get-tuple-element.105.refs_1_.up_ref, bf16[2048,3072]{1,0:T(8,128)(2,1)} %copy-done.1, bf16[2048,3072]{1,0:T(8,128)(2,1)} %copy-done.1), custom_call_target="tpu_custom_call" | custom-call | flops 7000000000 | tf_op jit(solution)/shard_map/turned_product/pallas_call | solution.py:709
  351.3 19.0 %weight_gradients.2 = bf16[2048,3072]{1,0:T(8,128)(2,1)} custom-call(bf16[1024,2048]{1,0:T(8,128)(2,1)} %bitcast.38.x_ref, bf16[1024,2048]{1,0:T(8,128)(2,1)} %bitcast.286, bf16[1024,1024]{1,0:T(8,128)(2,1)} %get-tuple-element.104.refs_0_.gate_ref, bf16[1024,1024]{1,0:T(8,128)(2,1)} %get-tuple-element.105.refs_1_.up_ref, ...), custom_call_target="tpu_custom_call" | custom-call | flops 9500000256 | tf_op jit(solution)/shard_map/weight_gradients/pallas_call | solution.py:735
  378.4 15.4 %collective-permute-done.36 = bf16[128,3072]{1,0:T(8,128)(2,1)} collective-permute-done((bf16[128,3072]{1,0:T(8,128)(2,1)}, bf16[128,3072]{1,0:T(8,128)(2,1)}, u32[]{:S(2)}, u32[]{:S(2)}) %collective-permute-start.36) | collective-permute-done | bytes 786464 | tf_op jit(solution)/shard_map/ppermute | solution.py:49
  420.6 20.7 %hidden_units.3 = (bf16[1024,1024]{1,0:T(8,128)(2,1)}, bf16[1024,1024]{1,0:T(8,128)(2,1)}, bf16[1024,1024]{1,0:T(8,128)(2,1)}) custom-call(bf16[1024,2048]{1,0:T(8,128)(2,1)} %bitcast.38.x_ref, bf16[1024,2048]{1,0:T(8,128)(2,1)} %bitcast.287, bf16[2048,3072]{1,0:T(8,128)(2,1)} %copy-done.2, bf16[2048,3072]{1,0:T(8,128)(2,1)} %copy-done.2, ...), custom_call_target="tpu_custom_call" | custom-call | flops 11000000512 | tf_op jit(solution)/shard_map/hidden_units/pallas_call | solution.py:680
  441.3 14.7 %turned_product.4 = bf16[1024,2048]{1,0:T(8,128)(2,1)} custom-call(bf16[1024,1024]{1,0:T(8,128)(2,1)} %get-tuple-element.110.refs_0_.gate_ref, bf16[1024,1024]{1,0:T(8,128)(2,1)} %get-tuple-element.111.refs_1_.up_ref, bf16[2048,3072]{1,0:T(8,128)(2,1)} %copy-done.2, bf16[2048,3072]{1,0:T(8,128)(2,1)} %copy-done.2, f32[1024,2048]{1,0:T(8,128)} %turned_product.3.refs_4_), custom_call_target="tpu_custom_call" | custom-call | flops 7000000000 | tf_op jit(solution)/shard_map/turned_product/pallas_call | solution.py:709
  473.1 20.3 %weight_gradients.3 = bf16[2048,3072]{1,0:T(8,128)(2,1)} custom-call(bf16[1024,2048]{1,0:T(8,128)(2,1)} %bitcast.38.x_ref, bf16[1024,2048]{1,0:T(8,128)(2,1)} %bitcast.288, bf16[1024,1024]{1,0:T(8,128)(2,1)} %get-tuple-element.110.refs_0_.gate_ref, bf16[1024,1024]{1,0:T(8,128)(2,1)} %get-tuple-element.111.refs_1_.up_ref, ...), custom_call_target="tpu_custom_call" | custom-call | flops 9500000256 | tf_op jit(solution)/shard_map/weight_gradients/pallas_call | solution.py:735
  494.9 13.4 %turned_product.5 = bf16[1024,2048]{1,0:T(8,128)(2,1)} custom-call(bf16[1024,1024]{1,0:T(8,128)(2,1)} %get-tuple-element.106.inner_ref.refs_0_, bf16[1024,1024]{1,0:T(8,128)(2,1)} %get-tuple-element.113.inner_ref.refs_1_, bf16[2048,3072]{1,0:T(8,128)(2,1)} %copy-done.1, bf16[2048,3072]{1,0:T(8,128)(2,1)} %copy-done.2), custom_call_target="tpu_custom_call" | custom-call | flops 6499999744 | tf_op jit(solution)/shard_map/turned_product/pallas_call | solution.py:709
  533.2 13.7 %collective-permute-done.53 = bf16[128,3072]{1,0:T(8,128)(2,1)S(1)} collective-permute-done((bf16[128,3072]{1,0:T(8,128)(2,1)S(1)}, bf16[128,3072]{1,0:T(8,128)(2,1)S(1)}, u32[]{:S(2)}, u32[]{:S(2)}) %collective-permute-start.53) | collective-permute-done | bytes 786464 | tf_op jit(solution)/shard_map/ppermute | solution.py:49
  556.4 29.6 %collective-permute-done.51 = bf16[128,3072]{1,0:T(8,128)(2,1)S(1)} collective-permute-done((bf16[128,3072]{1,0:T(8,128)(2,1)S(1)}, bf16[128,3072]{1,0:T(8,128)(2,1)S(1)}, u32[]{:S(2)}, u32[]{:S(2)}) %collective-permute-start.51) | collective-permute-done | bytes 786464 | tf_op jit(solution)/shard_map/ppermute | solution.py:49
  592.5 18.4 %collective-permute-done.43 = bf16[256,2048]{1,0:T(8,128)(2,1)S(1)} collective-permute-done((bf16[256,2048]{1,0:T(8,128)(2,1)S(1)}, bf16[256,2048]{1,0:T(8,128)(2,1)S(1)}, u32[]{:S(2)}, u32[]{:S(2)}) %collective-permute-start.43) | collective-permute-done | bytes 1048608 | tf_op jit(solution)/shard_map/ppermute | solution.py:199
  636.0 25.9 %backward.1 = (bf16[1024,512]{1,0:T(8,128)(2,1)S(1)}, f32[1024,512]{1,0:T(8,128)}, bf16[8,64,512]{2,1,0:T(8,128)(2,1)S(1)}, bf16[8,2,80,128]{3,2,1,0:T(8,128)(2,1)S(1)}, f32[4,128,256]{2,1,0:T(8,128)S(1)}) custom-call(bf16[1024,768]{1,0:T(8,128)(2,1)} %copy-done.45, bf16[1024,1280]{1,0:T(8,128)(2,1)} %get-tuple-element.81.phi_ref, ...), custom_call_target="tpu_custom_call" | custom-call | flops 12999999488 | tf_op jit(solution)/shard_map/backward/pallas_call | solution.py:595
  697.1 16.8 %collective-permute-done.60 = bf16[2,4,2,80,128]{4,3,2,1,0:T(8,128)(2,1)S(1)} collective-permute-done((bf16[2,4,2,80,128]{4,3,2,1,0:T(8,128)(2,1)S(1)}, bf16[2,4,2,80,128]{4,3,2,1,0:T(8,128)(2,1)S(1)}, u32[]{:S(2)}, u32[]{:S(2)}) %collective-permute-start.60) | collective-permute-done | bytes 327712 | tf_op jit(solution)/shard_map/ppermute | solution.py:39
  762.5 15.7 %collective-permute-done.69 = bf16[256,3072]{1,0:T(8,128)(2,1)S(1)} collective-permute-done((bf16[256,3072]{1,0:T(8,128)(2,1)}, bf16[256,3072]{1,0:T(8,128)(2,1)S(1)}, u32[]{:S(2)}, u32[]{:S(2)}) %collective-permute-start.69) | collective-permute-done | bytes 1572896 | tf_op jit(solution)/shard_map/ppermute | solution.py:49
  812.0 13.9 %collective-permute-done.72 = bf16[1264,128]{1,0:T(8,128)(2,1)S(1)} collective-permute-done((bf16[1264,128]{1,0:T(8,128)(2,1)S(1)}, bf16[1264,128]{1,0:T(8,128)(2,1)S(1)}, u32[]{:S(2)}, u32[]{:S(2)}) %collective-permute-start.72) | collective-permute-done | bytes 323616 | tf_op jit(solution)/shard_map/ppermute | solution.py:243
  837.9 10.0 %collective-permute-done.77 = bf16[256,1280]{0,1:T(8,128)(2,1)S(1)} collective-permute-done((bf16[256,1280]{0,1:T(8,128)(2,1)S(1)}, bf16[256,1280]{0,1:T(8,128)(2,1)S(1)}, u32[]{:S(2)}, u32[]{:S(2)}) %collective-permute-start.77) | collective-permute-done | bytes 655392 | tf_op jit(solution)/shard_map/ppermute | solution.py:49
  869.2 10.9 %collective-permute-done.66 = bf16[256,2048]{1,0:T(8,128)(2,1)} collective-permute-done((bf16[256,2048]{1,0:T(8,128)(2,1)S(1)}, bf16[256,2048]{1,0:T(8,128)(2,1)}, u32[]{:S(2)}, u32[]{:S(2)}) %collective-permute-start.66) | collective-permute-done | bytes 1048608 | tf_op jit(solution)/shard_map/ppermute | solution.py:199
  (672 shorter events, 490.7 us)
Async XLA Ops:
  197.2 36.6 %collective-permute-start.21 = (bf16[256,3072]{1,0:T(8,128)(2,1)}, bf16[256,3072]{1,0:T(8,128)(2,1)S(1)}, u32[]{:S(2)}, u32[]{:S(2)}) collective-permute-start(bf16[256,3072]{1,0:T(8,128)(2,1)} %collective-permute-done.17.refs_5_), channel_id=1, source_target_pairs={{0,4},{8,0},{16,8},{24,16},{28,24},{20,28},{12,20},{4,12},{1,5},{9... | collective-permute-start | bytes 4718600 | tf_op jit(solution)/shard_map/ppermute | solution.py:49
  238.8 61.9 %collective-permute-start.27 = (bf16[256,3072]{1,0:T(8,128)(2,1)S(1)}, bf16[256,3072]{1,0:T(8,128)(2,1)}, u32[]{:S(2)}, u32[]{:S(2)}) collective-permute-start(bf16[256,3072]{1,0:T(8,128)(2,1)S(1)} %pad_maximum_fusion.3.refs_3_), channel_id=1, source_target_pairs={{0,8},{8,16},{16,24},{24,28},{28,20},{20,12},{12,4},{4,0},{1,9},{9... | collective-permute-start | bytes 4718600 | tf_op jit(solution)/shard_map/ppermute | solution.py:49
  239.2 61.9 %collective-permute-start.30 = (bf16[256,3072]{1,0:T(8,128)(2,1)S(1)}, bf16[256,3072]{1,0:T(8,128)(2,1)}, u32[]{:S(2)}, u32[]{:S(2)}) collective-permute-start(bf16[256,3072]{1,0:T(8,128)(2,1)S(1)} %pad_maximum_fusion.3.refs_3_), channel_id=1, source_target_pairs={{0,4},{8,0},{16,8},{24,16},{28,24},{20,28},{12,20},{4,12},{1,5},{9... | collective-permute-start | bytes 4718600 | tf_op jit(solution)/shard_map/ppermute | solution.py:49
  240.9 57.5 %collective-permute-start.22 = (bf16[256,2048]{1,0:T(8,128)(2,1)}, bf16[256,2048]{1,0:T(8,128)(2,1)}, u32[]{:S(2)}, u32[]{:S(2)}) collective-permute-start(bf16[256,2048]{1,0:T(8,128)(2,1)} %multiply_convert_fusion.1), channel_id=1, source_target_pairs={{0,1},{1,0},{2,3},{3,2},{4,5},{5,4},{6,7},{7,6},{8,9},{9,8},{10,11... | collective-permute-start | bytes 3145736 | tf_op jit(solution)/shard_map/ppermute | solution.py:194
  264.0 41.1 %collective-permute-start.24 = (bf16[256,2048]{1,0:T(8,128)(2,1)}, bf16[256,2048]{1,0:T(8,128)(2,1)S(1)}, u32[]{:S(2)}, u32[]{:S(2)}) collective-permute-start(bf16[256,2048]{1,0:T(8,128)(2,1)} %collective-permute-done.23), channel_id=1, source_target_pairs={{0,1},{1,0},{2,3},{3,2},{4,5},{5,4},{6,7},{7,6},{8,9},{9,8},{10,11... | collective-permute-start | bytes 3145736 | tf_op jit(solution)/shard_map/ppermute | solution.py:194
  335.4 37.5 %collective-permute-start.29 = (bf16[256,3072]{1,0:T(8,128)(2,1)S(1)}, bf16[256,3072]{1,0:T(8,128)(2,1)S(1)}, u32[]{:S(2)}, u32[]{:S(2)}) collective-permute-start(bf16[256,3072]{1,0:T(8,128)(2,1)S(1)} %collective-permute-done.28.refs_1_), channel_id=1, source_target_pairs={{0,8},{8,16},{16,24},{24,28},{28,20},{20,12},{12,4},{4,0},{1,9},{9... | collective-permute-start | bytes 4718600 | tf_op jit(solution)/shard_map/ppermute | solution.py:49
  375.0 37.4 %collective-permute-start.33 = (bf16[128,3072]{1,0:T(8,128)(2,1)S(1)}, bf16[128,3072]{1,0:T(8,128)(2,1)S(1)}, u32[]{:S(2)}, u32[]{:S(2)}) collective-permute-start(bf16[128,3072]{1,0:T(8,128)(2,1)S(1)} %slice.341), channel_id=1, source_target_pairs={{0,8},{8,16},{16,24},{24,28},{28,20},{20,12},{12,4},{4,0},{1,9},{9... | collective-permute-start | bytes 2359304 | tf_op jit(solution)/shard_map/ppermute | solution.py:49
  400.1 62.4 %collective-permute-start.47 = (bf16[256,3072]{1,0:T(8,128)(2,1)}, bf16[256,3072]{1,0:T(8,128)(2,1)}, u32[]{:S(2)}, u32[]{:S(2)}) collective-permute-start(bf16[256,3072]{1,0:T(8,128)(2,1)} %pad_maximum_fusion.4), channel_id=1, source_target_pairs={{0,8},{8,16},{16,24},{24,28},{28,20},{20,12},{12,4},{4,0},{1,9},{9... | collective-permute-start | bytes 4718600 | tf_op jit(solution)/shard_map/ppermute | solution.py:49
  401.4 61.1 %collective-permute-start.49 = (bf16[256,3072]{1,0:T(8,128)(2,1)}, bf16[256,3072]{1,0:T(8,128)(2,1)}, u32[]{:S(2)}, u32[]{:S(2)}) collective-permute-start(bf16[256,3072]{1,0:T(8,128)(2,1)} %pad_maximum_fusion.5), channel_id=1, source_target_pairs={{0,4},{8,0},{16,8},{24,16},{28,24},{20,28},{12,20},{4,12},{1,5},{9... | collective-permute-start | bytes 4718600 | tf_op jit(solution)/shard_map/ppermute | solution.py:49
  468.4 58.8 %collective-permute-start.50 = (bf16[256,3072]{1,0:T(8,128)(2,1)}, bf16[256,3072]{1,0:T(8,128)(2,1)}, u32[]{:S(2)}, u32[]{:S(2)}) collective-permute-start(bf16[256,3072]{1,0:T(8,128)(2,1)} %get-tuple-element.117), channel_id=1, source_target_pairs={{0,4},{8,0},{16,8},{24,16},{28,24},{20,28},{12,20},{4,12},{1,5},{9... | collective-permute-start | bytes 4718600 | tf_op jit(solution)/shard_map/ppermute | solution.py:49
  470.1 57.0 %collective-permute-start.48 = (bf16[256,3072]{1,0:T(8,128)(2,1)}, bf16[256,3072]{1,0:T(8,128)(2,1)}, u32[]{:S(2)}, u32[]{:S(2)}) collective-permute-start(bf16[256,3072]{1,0:T(8,128)(2,1)} %get-tuple-element.116), channel_id=1, source_target_pairs={{0,8},{8,16},{16,24},{24,28},{28,20},{20,12},{12,4},{4,0},{1,9},{9... | collective-permute-start | bytes 4718600 | tf_op jit(solution)/shard_map/ppermute | solution.py:49
  510.3 40.8 %collective-permute-start.38 = (bf16[2,256,2048]{2,1,0:T(8,128)(2,1)S(1)}, bf16[2,256,2048]{2,1,0:T(8,128)(2,1)S(1)}, u32[]{:S(2)}, u32[]{:S(2)}) collective-permute-start(bf16[2,256,2048]{2,1,0:T(8,128)(2,1)S(1)} %dynamic-slice_bitcast_fusion.1), channel_id=1, source_target_pairs={{0,1},{1,0},{2,3},{3,2},{4,5},{5,4},{6,7},{7,6},{8,9},{9,8},{10,11... | collective-permute-start | bytes 6291464 | tf_op jit(solution)/shard_map/ppermute | solution.py:194
  532.8 54.7 %collective-permute-start.83 = (bf16[256,3072]{1,0:T(8,128)(2,1)S(1)}, bf16[256,3072]{1,0:T(8,128)(2,1)}, u32[]{:S(2)}, u32[]{:S(2)}) collective-permute-start(bf16[256,3072]{1,0:T(8,128)(2,1)S(1)} %get-tuple-element.137), channel_id=1, source_target_pairs={{0,8},{8,16},{16,24},{24,28},{28,20},{20,12},{12,4},{4,0},{1,9},{9... | collective-permute-start | bytes 4718600 | tf_op jit(solution)/shard_map/ppermute | solution.py:49
  546.9 40.7 %collective-permute-start.84 = (bf16[256,3072]{1,0:T(8,128)(2,1)S(1)}, bf16[256,3072]{1,0:T(8,128)(2,1)}, u32[]{:S(2)}, u32[]{:S(2)}) collective-permute-start(bf16[256,3072]{1,0:T(8,128)(2,1)S(1)} %get-tuple-element.138), channel_id=1, source_target_pairs={{0,4},{8,0},{16,8},{24,16},{28,24},{20,28},{12,20},{4,12},{1,5},{9... | collective-permute-start | bytes 4718600 | tf_op jit(solution)/shard_map/ppermute | solution.py:49
  551.0 65.4 %collective-permute-start.54 = (bf16[256,3072]{1,0:T(8,128)(2,1)}, bf16[256,3072]{1,0:T(8,128)(2,1)S(1)}, u32[]{:S(2)}, u32[]{:S(2)}) collective-permute-start(bf16[256,3072]{1,0:T(8,128)(2,1)} %pad_maximum_fusion.7), channel_id=1, source_target_pairs={{0,4},{8,0},{16,8},{24,16},{28,24},{20,28},{12,20},{4,12},{1,5},{9... | collective-permute-start | bytes 4718600 | tf_op jit(solution)/shard_map/ppermute | solution.py:49
  615.0 57.1 %collective-permute-start.44 = (bf16[256,2048]{1,0:T(8,128)(2,1)}, bf16[256,2048]{1,0:T(8,128)(2,1)}, u32[]{:S(2)}, u32[]{:S(2)}) collective-permute-start(bf16[256,2048]{1,0:T(8,128)(2,1)} %get-tuple-element.284), channel_id=1, source_target_pairs={{0,1},{1,0},{2,3},{3,2},{4,5},{5,4},{6,7},{7,6},{8,9},{9,8},{10,11... | collective-permute-start | bytes 3145736 | tf_op jit(solution)/shard_map/ppermute | solution.py:194
  615.0 55.5 %collective-permute-start.45 = (bf16[256,2048]{1,0:T(8,128)(2,1)}, bf16[256,2048]{1,0:T(8,128)(2,1)}, u32[]{:S(2)}, u32[]{:S(2)}) collective-permute-start(bf16[256,2048]{1,0:T(8,128)(2,1)} %get-tuple-element.284), channel_id=1, source_target_pairs={{0,2},{1,3},{2,0},{3,1},{4,6},{5,7},{6,4},{7,5},{8,10},{9,11},{10,... | collective-permute-start | bytes 3145736 | tf_op jit(solution)/shard_map/ppermute | solution.py:199
  629.7 40.9 %collective-permute-start.55 = (bf16[256,3072]{1,0:T(8,128)(2,1)}, bf16[256,3072]{1,0:T(8,128)(2,1)}, u32[]{:S(2)}, u32[]{:S(2)}) collective-permute-start(bf16[256,3072]{1,0:T(8,128)(2,1)} %get-tuple-element.297), channel_id=1, source_target_pairs={{0,8},{8,16},{16,24},{24,28},{28,20},{20,12},{12,4},{4,0},{1,9},{9... | collective-permute-start | bytes 4718600 | tf_op jit(solution)/shard_map/ppermute | solution.py:49
  630.0 40.6 %collective-permute-start.56 = (bf16[256,3072]{1,0:T(8,128)(2,1)}, bf16[256,3072]{1,0:T(8,128)(2,1)}, u32[]{:S(2)}, u32[]{:S(2)}) collective-permute-start(bf16[256,3072]{1,0:T(8,128)(2,1)} %get-tuple-element.296), channel_id=1, source_target_pairs={{0,4},{8,0},{16,8},{24,16},{28,24},{20,28},{12,20},{4,12},{1,5},{9... | collective-permute-start | bytes 4718600 | tf_op jit(solution)/shard_map/ppermute | solution.py:49
  670.5 43.7 %collective-permute-start.46 = (bf16[256,2048]{1,0:T(8,128)(2,1)}, bf16[256,2048]{1,0:T(8,128)(2,1)S(1)}, u32[]{:S(2)}, u32[]{:S(2)}) collective-permute-start(bf16[256,2048]{1,0:T(8,128)(2,1)} %collective-permute-done.45), channel_id=1, source_target_pairs={{0,1},{1,0},{2,3},{3,2},{4,5},{5,4},{6,7},{7,6},{8,9},{9,8},{10,11... | collective-permute-start | bytes 3145736 | tf_op jit(solution)/shard_map/ppermute | solution.py:194
  680.2 39.5 %collective-permute-start.62 = (bf16[8,2,80,128]{3,2,1,0:T(8,128)(2,1)S(1)}, bf16[8,2,80,128]{3,2,1,0:T(8,128)(2,1)S(1)}, u32[]{:S(2)}, u32[]{:S(2)}) collective-permute-start(bf16[8,2,80,128]{3,2,1,0:T(8,128)(2,1)S(1)} %get-tuple-element.128), channel_id=1, source_target_pairs={{4,0},{8,4},{12,8},{16,12},{20,16},{24,20},{28,24},{5,1},{9,5},{13... | collective-permute-start | bytes 983048 | tf_op jit(solution)/shard_map/ppermute | solution.py:39
  681.5 38.2 %collective-permute-start.57 = (bf16[8,64,512]{2,1,0:T(8,128)(2,1)S(1)}, bf16[8,64,512]{2,1,0:T(8,128)(2,1)S(1)}, u32[]{:S(2)}, u32[]{:S(2)}) collective-permute-start(bf16[8,64,512]{2,1,0:T(8,128)(2,1)S(1)} %get-tuple-element.127), channel_id=1, source_target_pairs={{4,0},{8,4},{12,8},{16,12},{20,16},{24,20},{28,24},{5,1},{9,5},{13... | collective-permute-start | bytes 1572872 | tf_op jit(solution)/shard_map/ppermute | solution.py:39
  741.8 36.6 %collective-permute-start.68 = (bf16[256,3072]{1,0:T(8,128)(2,1)}, bf16[256,3072]{1,0:T(8,128)(2,1)S(1)}, u32[]{:S(2)}, u32[]{:S(2)}) collective-permute-start(bf16[256,3072]{1,0:T(8,128)(2,1)} %get-tuple-element.132), channel_id=1, source_target_pairs={{0,8},{8,16},{16,24},{24,28},{28,20},{20,12},{12,4},{4,0},{1,9},{9... | collective-permute-start | bytes 4718600 | tf_op jit(solution)/shard_map/ppermute | solution.py:49
  758.8 47.3 %collective-permute-start.63 = (bf16[2,256,2048]{2,1,0:T(8,128)(2,1)}, bf16[2,256,2048]{2,1,0:T(8,128)(2,1)}, u32[]{:S(2)}, u32[]{:S(2)}) collective-permute-start(bf16[2,256,2048]{2,1,0:T(8,128)(2,1)} %dynamic-slice_bitcast_fusion), channel_id=1, source_target_pairs={{0,1},{1,0},{2,3},{3,2},{4,5},{5,4},{6,7},{7,6},{8,9},{9,8},{10,11... | collective-permute-start | bytes 6291464 | tf_op jit(solution)/shard_map/ppermute | solution.py:194
  (211 other events, 2787.1 us)

commit v3 on v2

--- a/solution.py
+++ b/solution.py
@@ -10,7 +10,7 @@
 WIN = 64
 LANES = 128
 STATE_ROWS = 80
-MLP_CHUNKS = 2
+TOLD = 10_000_000
 
 epsilon = 1e-05
 rope_base = 500000.0
@@ -54,11 +54,67 @@
     mine = lax.axis_index("seq")
     place = jnp.where(mine % 2 == 0, mine // 2, count - 1 - mine // 2)
     there = (place + offset + count) % count
-    return jnp.where(there < count // 2, 2 * there, 2 * (count - 1 - there) + 1)
+    return jnp.where(there < count // 2, 2 * there, 2 * (count - 1 - there) + 1).astype(jnp.int32)
 
 
 def after(value, *others):
     return lax.optimization_barrier((value,) + others)[0]
+
+
+def told(microseconds):
+    return pl.CostEstimate(flops=int(microseconds * TOLD), bytes_accessed=0, transcendentals=0)
+
+
+def kernel_params():
+    return pltpu.CompilerParams(vmem_limit_bytes=56 * 1024 * 1024)
+
+
+def place_rows(pieces, places, origins, rows, widths):
+    starts = [sum(widths[:i]) for i in range(len(widths))]
+
+    def kernel(places_ref, *refs):
+        sources, rest = refs[: len(pieces)], refs[len(pieces) :]
+        targets, buffers, semaphores = rest[: len(widths)], rest[len(widths) : -1], rest[-1]
+        inward, outward = [], []
+        for turn, (source, (at, shift)) in enumerate(zip(sources, origins, strict=True)):
+            length = source.shape[0]
+            held = buffers[turn]
+            inward.append(pltpu.make_async_copy(source, held, semaphores.at[turn]))
+            first = pl.multiple_of(places_ref[at] + shift, length)
+            for target, start, width in zip(targets, starts, widths, strict=True):
+                outward.append(
+                    pltpu.make_async_copy(
+                        held.at[:, pl.ds(start, width)],
+                        target.at[pl.ds(first, length), :],
+                        semaphores.at[len(sources) + len(outward)],
+                    )
+                )
+        for copy in inward:
+            copy.start()
+        for turn, copy in enumerate(inward):
+            copy.wait()
+            for back in outward[turn * len(widths) : (turn + 1) * len(widths)]:
+                back.start()
+        for copy in outward:
+            copy.wait()
+
+    anywhere = pl.BlockSpec(memory_space=pl.ANY)
+    size = sum(piece.size for piece in pieces) * 2
+    return pl.pallas_call(
+        kernel,
+        grid_spec=pltpu.PrefetchScalarGridSpec(
+            num_scalar_prefetch=1,
+            grid=(1,),
+            in_specs=[anywhere] * len(pieces),
+            out_specs=[anywhere] * len(widths),
+            scratch_shapes=[pltpu.VMEM(piece.shape, piece.dtype) for piece in pieces]
+            + [pltpu.SemaphoreType.DMA((len(pieces) * (1 + len(widths)),))],
+        ),
+        out_shape=[jax.ShapeDtypeStruct((rows, width), pieces[0].dtype) for width in widths],
+        compiler_params=pltpu.CompilerParams(vmem_limit_bytes=size + 4 * 1024 * 1024),
+        cost_estimate=told(1 + size // 4_000_000),
+        name="place_rows",
+    )(places, *pieces)
 
 
 class Gather:
@@ -84,14 +140,13 @@
                 self.found[self.half] = (ring_move(up[:cut], 1), ring_move(down[cut:], -1))
 
     def edge(self):
-        return self.up, self.down
+        return self.found[self.half] if self.step == self.half else (self.up, self.down)
 
     def assemble(self, *widths):
         self.advance(quarters=4)
-        count = lax.axis_size("seq")
         rows = self.found[0].shape[0]
         offsets = sorted(self.found)
-        places = jnp.stack([ring_index(offset) * rows for offset in offsets]).astype(jnp.int32)
+        places = jnp.stack([ring_index(offset) * rows for offset in offsets])
         pieces, origins = [], []
         for at, offset in enumerate(offsets):
             block, shift = self.found[offset], 0
@@ -99,53 +154,31 @@
                 pieces.append(part)
                 origins.append((at, shift))
                 shift += part.shape[0]
-        starts = [sum(widths[:i]) for i in range(len(widths))]
-
-        def kernel(places_ref, *refs):
-            sources, rest = refs[: len(pieces)], refs[len(pieces) :]
-            targets, buffers, semaphores = rest[: len(widths)], rest[len(widths) : -1], rest[-1]
-            inward, outward = [], []
-            for turn, (source, (at, shift)) in enumerate(zip(sources, origins, strict=True)):
-                length = source.shape[0]
-                held = buffers[turn]
-                inward.append(pltpu.make_async_copy(source, held, semaphores.at[turn]))
-                first = pl.multiple_of(places_ref[at] + shift, length)
-                for target, start, width in zip(targets, starts, widths, strict=True):
-                    outward.append(
-                        pltpu.make_async_copy(
-                            held.at[:, pl.ds(start, width)],
-                            target.at[pl.ds(first, length), :],
-                            semaphores.at[len(sources) + len(outward)],
-                        )
-                    )
-            for copy in inward:
-                copy.start()
-            for turn, copy in enumerate(inward):
-                copy.wait()
-                for back in outward[turn * len(widths) : (turn + 1) * len(widths)]:
-                    back.start()
-            for copy in outward:
-                copy.wait()
-
-        anywhere = pl.BlockSpec(memory_space=pl.ANY)
-        size = sum(piece.size for piece in pieces) * 2
-        return pl.pallas_call(
-            kernel,
-            grid_spec=pltpu.PrefetchScalarGridSpec(
-                num_scalar_prefetch=1,
-                grid=(1,),
-                in_specs=[anywhere] * len(pieces),
-                out_specs=[anywhere] * len(widths),
-                scratch_shapes=[pltpu.VMEM(piece.shape, piece.dtype) for piece in pieces]
-                + [pltpu.SemaphoreType.DMA((len(pieces) * (1 + len(widths)),))],
-            ),
-            out_shape=[
-                jax.ShapeDtypeStruct((count * rows, width), pieces[0].dtype) for width in widths
-            ],
-            compiler_params=pltpu.CompilerParams(vmem_limit_bytes=size + 4 * 1024 * 1024),
-            cost_estimate=told(1 + size // 4_000_000),
-            name="assemble",
-        )(places, *pieces)
+        return place_rows(pieces, places, origins, lax.axis_size("seq") * rows, widths)
+
+
+def on_block(kernel, grads, others, outs, offset, rows, name):
+    cut, columns = rows // 2, grads.shape[1]
+
+    def half_of(length):
+        if length == rows:
+            return pl.BlockSpec((cut, columns), lambda h, at: (h, 0))
+        return pl.BlockSpec((cut, columns), lambda h, at: (0, 0))
+
+    return pl.pallas_call(
+        kernel,
+        grid_spec=pltpu.PrefetchScalarGridSpec(
+            num_scalar_prefetch=1,
+            grid=(2,),
+            in_specs=[pl.BlockSpec((cut, columns), lambda h, at: (2 * at[0] + h, 0))]
+            + [half_of(other.shape[0]) for other in others],
+            out_specs=[spec if spec else half_of(shape.shape[0]) for shape, spec in outs],
+        ),
+        out_shape=[shape for shape, _ in outs],
+        compiler_params=kernel_params(),
+        cost_estimate=told(2),
+        name=name,
+    )(ring_index(offset)[None], grads, *others)
 
 
 class Scatter:
@@ -154,10 +187,34 @@
         self.half = lax.axis_size("seq") // 2
         self.step = 0
 
-    def own(self, offset):
-        at = ring_index(offset) * self.rows
-        parts = [lax.dynamic_slice_in_dim(part, at, self.rows, 0) for part in self.grads]
-        return parts[0] if len(parts) == 1 else jnp.concatenate(parts, axis=1)
+    def shape(self, rows):
+        return jax.ShapeDtypeStruct((rows, self.grads.shape[1]), self.grads.dtype)
+
+    def far(self):
+        def kernel(at_ref, own_ref, up_ref, down_ref):
+            @pl.when(pl.program_id(0) == 0)
+            def _():
+                up_ref[...] = own_ref[...]
+
+            @pl.when(pl.program_id(0) == 1)
+            def _():
+                down_ref[...] = own_ref[...]
+
+        outs = [(self.shape(self.rows // 2), None)] * 2
+        return on_block(kernel, self.grads, [], outs, self.half, self.rows, "far_block")
+
+    def joined(self, received, offset, which):
+        full = received.shape[0] == self.rows
+
+        def kernel(at_ref, own_ref, got_ref, out_ref):
+            own, got = own_ref[...].astype(jnp.float32), got_ref[...].astype(jnp.float32)
+            if not full:
+                got = jnp.where(pl.program_id(0) == which, got, 0.0)
+            out_ref[...] = (own + got).astype(out_ref.dtype)
+
+        outs = [(self.shape(self.rows), None)]
+        (out,) = on_block(kernel, self.grads, [received], outs, offset, self.rows, "join_block")
+        return out
 
     def advance(self, *gates, quarters=1):
         for _ in range(quarters * max(1, self.half // 4)):
@@ -165,28 +222,42 @@
                 return
             self.step += 1
             offset = self.half - self.step + 1
-            cut = self.rows // 2
             if self.step == 1:
-                far = self.own(offset)
-                up, down = far[:cut], far[cut:]
+                up, down = self.far()
             else:
-                above, below = self.own(offset), self.own(-offset)
-                if self.step == 2:
-                    up = jnp.concatenate([above[:cut] + self.up, above[cut:]], axis=0)
-                    down = jnp.concatenate([below[:cut], below[cut:] + self.down], axis=0)
-                else:
-                    up, down = above + self.up, below + self.down
+                up, down = self.joined(self.up, offset, 0), self.joined(self.down, -offset, 1)
             if gates:
                 up, down = after(up, *gates), after(down, *gates)
+            self.sending = up, down
             self.up, self.down = ring_move(up, 1), ring_move(down, -1)
 
     def edge(self):
         return self.up, self.down
 
-    def total(self):
+    def total(self, widths, turned):
         self.advance(quarters=4)
-        mine = self.own(0).astype(jnp.float32)
-        return mine + self.up.astype(jnp.float32) + self.down.astype(jnp.float32)
+        starts = [sum(widths[:i]) for i in range(len(widths))]
+        cut = self.rows // 2
+        later = [turn and cut % LANES != 0 for turn in turned]
+        turned = [turn and not late for turn, late in zip(turned, later, strict=True)]
+
+        def kernel(at_ref, own_ref, up_ref, down_ref, *out_refs):
+            for start, width, turn, out_ref in zip(starts, widths, turned, out_refs, strict=True):
+                lanes = slice(start, start + width)
+                total = own_ref[:, lanes].astype(jnp.float32) + up_ref[:, lanes].astype(jnp.float32)
+                total = total + down_ref[:, lanes].astype(jnp.float32)
+                out_ref[...] = total.T if turn else total
+
+        outs = []
+        for width, turn in zip(widths, turned, strict=True):
+            shape = (width, self.rows) if turn else (self.rows, width)
+            block = (width, cut) if turn else (cut, width)
+            spec = pl.BlockSpec(block, (lambda h, at: (0, h)) if turn else (lambda h, at: (h, 0)))
+            outs.append((jax.ShapeDtypeStruct(shape, jnp.float32), spec))
+        sums = on_block(
+            kernel, self.grads, [self.up, self.down], outs, 0, self.rows, "own_block"
+        )
+        return [part.T if late else part for part, late in zip(sums, later, strict=True)]
 
 
 def core_swap(block):
@@ -199,41 +270,133 @@
     return lax.ppermute(block, "head", [(i, (i + 2 * step) % count) for i in range(count)])
 
 
-def head_pair_sum(part):
-    chips = lax.axis_size("head") // 2
-    core = lax.axis_index("head") % 2
-    rows = part.shape[0] // (2 * chips)
-    split = part.reshape(chips, 2, rows, part.shape[1])
-    theirs = core_swap(lax.dynamic_index_in_dim(split, 1 - core, 1, False))
-    return lax.dynamic_index_in_dim(split, core, 1, False).astype(jnp.float32) + theirs
-
-
-def head_finish(both, *gates):
-    chips = lax.axis_size("head") // 2
-    chip = lax.axis_index("head") // 2
-    total = lax.dynamic_index_in_dim(both, chip, 0, False)
-    for step in range(1, chips):
-        sent = lax.dynamic_index_in_dim(both, (chip + step) % chips, 0, False)
-        sent = sent.astype(jnp.bfloat16)
-        total = total + chip_move(after(sent, *gates) if gates else sent, step)
-    return total
-
-
-def head_scatter(part):
-    return head_finish(head_pair_sum(part))
-
-
-def head_gather(own):
-    chips = lax.axis_size("head") // 2
-    place = lax.axis_index("head")
-    chip, core = place // 2, place % 2
-    whole = jnp.zeros((2 * chips,) + own.shape, own.dtype)
-    for step in range(chips):
-        block = chip_move(own, step) if step else own
-        at = 2 * ((chip - step + chips) % chips)
-        whole = lax.dynamic_update_index_in_dim(whole, block, at + core, 0)
-        whole = lax.dynamic_update_index_in_dim(whole, core_swap(block), at + 1 - core, 0)
-    return whole.reshape((2 * chips * own.shape[0],) + own.shape[1:])
+class HeadSum:
+    def __init__(self, mine, *theirs):
+        self.mine = mine
+        self.got = [core_swap(piece) for piece in theirs]
+
+    def pair(self):
+        chips, rows, width = self.mine.shape
+        tile = self.tile = min(128, rows)
+        chip = (lax.axis_index("head") // 2).astype(jnp.int32)
+        cuts, tiles = len(self.got), rows // tile
+
+        def kernel(chip_ref, mine_ref, *refs):
+            got_refs, kept_ref, sent_refs = refs[:cuts], refs[cuts], refs[cuts + 1 :]
+
+            def both(step, out_ref):
+                at = (chip_ref[0] + step) % chips
+                for turn, got_ref in enumerate(got_refs):
+                    lanes = slice(turn * got_ref.shape[2], (turn + 1) * got_ref.shape[2])
+                    total = mine_ref[at, :, lanes].astype(jnp.float32)
+                    total = total + got_ref[at].astype(jnp.float32)
+                    out_ref[:, lanes] = total.astype(out_ref.dtype)
+
+            both(0, kept_ref)
+            for turn, sent_ref in enumerate(sent_refs):
+                pl.when(pl.program_id(0) == turn % tiles)(
+                    functools.partial(both, 1 + turn // tiles, sent_ref)
+                )
+
+        def cut(size, *first):
+            return pl.BlockSpec(first + (tile, size), lambda t, at: (0,) * len(first) + (t, 0))
+
+        count = (chips - 1) * tiles
+        piece = pl.BlockSpec((tile, width), lambda t, at: (0, 0))
+        self.kept, *self.sent = pl.pallas_call(
+            kernel,
+            grid_spec=pltpu.PrefetchScalarGridSpec(
+                num_scalar_prefetch=1,
+                grid=(tiles,),
+                in_specs=[cut(width, chips)] + [cut(piece.shape[2], chips) for piece in self.got],
+                out_specs=[cut(width)] + [piece] * count,
+            ),
+            out_shape=[jax.ShapeDtypeStruct((rows, width), jnp.float32)]
+            + [jax.ShapeDtypeStruct((tile, width), jnp.bfloat16)] * count,
+            compiler_params=kernel_params(),
+            cost_estimate=told(2),
+            name="pair_sum",
+        )(chip[None], self.mine, *self.got)
+        return self.sent
+
+    def finish(self, formula, blocks, gain, keep, add, name, *gates):
+        rows, width = self.kept.shape
+        tile, tiles = self.tile, self.kept.shape[0] // self.tile
+        moved = []
+        for turn, sent in enumerate(self.sent):
+            sent = after(sent, *gates) if gates else sent
+            moved.append(chip_move(sent, 1 + turn // tiles))
+        kept = after(self.kept, *moved)
+
+        def kernel(kept_ref, *refs):
+            moved_refs, refs = refs[: len(moved)], refs[len(moved) :]
+            block_refs, gain_ref, out_refs = refs[: len(blocks)], refs[len(blocks)], refs[len(blocks) + 1 :]
+            piece_refs = out_refs[keep : keep + tiles]
+
+            def one(turn):
+                total = kept_ref[...]
+                for moved_ref in moved_refs[turn::tiles]:
+                    total = total + moved_ref[...].astype(jnp.float32)
+                values = [ref[...].astype(jnp.float32) for ref in block_refs]
+                first, piece, column = formula(total, *values, gain_ref[...])
+                if keep:
+                    out_refs[0][...] = first
+                piece_refs[turn][...] = piece.astype(jnp.bfloat16)
+                if add:
+                    column = jnp.sum(column, axis=0, keepdims=True)
+                    out_refs[-1][...] = column if turn == 0 else out_refs[-1][...] + column
+
+            for turn in range(tiles):
+                pl.when(pl.program_id(0) == turn)(functools.partial(one, turn))
+
+        block = pl.BlockSpec((tile, width), lambda t: (t, 0))
+        piece = pl.BlockSpec((tile, width), lambda t: (0, 0))
+        line = pl.BlockSpec((1, width), lambda t: (0, 0))
+        wide = functools.partial(jax.ShapeDtypeStruct, dtype=jnp.float32)
+        outs = pl.pallas_call(
+            kernel,
+            grid=(tiles,),
+            in_specs=[block] + [piece] * len(moved) + [block] * len(blocks) + [line],
+            out_specs=[block] * keep + [piece] * tiles + [line] * add,
+            out_shape=[wide((rows, width))] * keep
+            + [jax.ShapeDtypeStruct((tile, width), jnp.bfloat16)] * tiles
+            + [wide((1, width))] * add,
+            compiler_params=kernel_params(),
+            cost_estimate=told(3),
+            name=name,
+        )(kept, *moved, *blocks, gain.astype(jnp.float32)[None])
+        pieces = outs[keep : keep + tiles]
+        return (outs[0] if keep else None), pieces, (outs[-1] if add else None)
+
+
+class HeadGather:
+    def __init__(self, own):
+        chips = lax.axis_size("head") // 2
+        self.steps = [own] + [[chip_move(part, step) for part in own] for step in range(1, chips)]
+
+    def edge(self):
+        return tuple(part for parts in self.steps[1:] for part in parts)
+
+    def rows(self, *gates):
+        chips = len(self.steps)
+        place = lax.axis_index("head")
+        chip, core = place // 2, place % 2
+        height = self.steps[0][0].shape[0]
+        count = len(self.steps[0])
+        pieces, places, origins = [], [], []
+        for step, parts in enumerate(self.steps):
+            at = 2 * ((chip - step + chips) % chips)
+            for other in range(2):
+                for turn, part in enumerate(parts):
+                    if other:
+                        part = core_swap(after(part, *gates) if gates and step else part)
+                    origins.append((len(places), turn * height))
+                    pieces.append(part)
+                places.append((at + (1 - core if other else core)) * count * height)
+        places = jnp.stack(places).astype(jnp.int32)
+        rows = 2 * chips * count * height
+        (whole,) = place_rows(pieces, places, origins, rows, [pieces[0].shape[1]])
+        return whole
 
 
 def exchange_sum(block, axis, bits):
@@ -447,7 +610,39 @@
     return grads * cos - swapped_halves(grads) * sin
 
 
-def backward_kernel(sizes, rot_ref, phi_ref, halo_ref, state_ref, meta_ref, keys_ref, att_ref, den_ref, grad_ref, cos_ref, sin_ref, mapq_ref, lin_ref, own_ref, back_ref, carry_ref, map_ref):
+def output_grads(sizes, pairs, att_ref, den_ref, grad_ref):
+    grads = stacked([group(grad_ref, p) for p in pairs]).astype(jnp.float32)
+    mixed = stacked([group(att_ref, p) for p in pairs]).astype(jnp.float32)
+    inverse = 1.0 / stacked([group(den_ref, p) for p in pairs])
+    grad_num = (grads * inverse).astype(jnp.bfloat16)
+    grad_den = -half_sums(grads * mixed) * inverse
+    rough = grad_den.astype(jnp.bfloat16)
+    rest = (grad_den - rough.astype(jnp.float32)).astype(jnp.bfloat16)
+    lane = lane_of(grad_den.shape)
+    grad_den = jnp.where(lane % 64 < 32, rough.astype(jnp.float32), rest.astype(jnp.float32))
+    return jnp.concatenate([grad_num, grad_den.astype(jnp.bfloat16)], axis=1)
+
+
+def carry_kernel(sizes, phi_ref, meta_ref, att_ref, den_ref, grad_ref, carry_ref):
+    reach = meta_ref[:, 3:4]
+    for g in range(sizes.kv):
+        pairs = pairs_of(sizes, g)
+        reach_all = stacked([reach] * len(pairs))
+        both = output_grads(sizes, pairs, att_ref, den_ref, grad_ref)
+        state_sum = []
+        for half in range(2):
+            phi = stacked([group(phi_ref, 2 * p + half) for p in pairs])
+            reached = (phi.astype(jnp.float32) * reach_all).astype(jnp.bfloat16)
+            state_sum.append(left_dot(both, reached))
+        low, high = state_sum
+        totals = low[128:129] + low[160:161] + high[192:193] + high[224:225]
+        state_grad = stacked(
+            [low[:64] + high[64:128], jnp.broadcast_to(totals, (STATE_ROWS - 64, LANES))]
+        )
+        carry_ref[g] = state_grad.astype(jnp.bfloat16)
+
+
+def backward_kernel(sizes, rot_ref, phi_ref, halo_ref, state_ref, meta_ref, keys_ref, att_ref, den_ref, grad_ref, cos_ref, sin_ref, mapq_ref, lin_ref, own_ref, back_ref, map_ref):
     shard = sizes.shard
     near, far = near_and_far(sizes, meta_ref, keys_ref)
     reach = meta_ref[:, 3:4]
@@ -466,20 +661,10 @@
         value_pair = value_sides(values, 1.0 / 32.0)
         state_pair = state_sides(state_ref[g], 1.0 / 32.0)
         queries = stacked([group(rot_ref, p) for p in pairs])
-        grads = stacked([group(grad_ref, p) for p in pairs]).astype(jnp.float32)
-        mixed = stacked([group(att_ref, p) for p in pairs]).astype(jnp.float32)
-        inverse = 1.0 / stacked([group(den_ref, p) for p in pairs])
-        grad_num = (grads * inverse).astype(jnp.bfloat16)
-        grad_den = -half_sums(grads * mixed) * inverse
-        rough = grad_den.astype(jnp.bfloat16)
-        rest = (grad_den - rough.astype(jnp.float32)).astype(jnp.bfloat16)
-        lane = lane_of(grad_den.shape)
-        grad_den = jnp.where(
-            lane % 64 < 32, rough.astype(jnp.float32), rest.astype(jnp.float32)
-        ).astype(jnp.bfloat16)
-        both = jnp.concatenate([grad_num, grad_den], axis=1)
+        both = output_grads(sizes, pairs, att_ref, den_ref, grad_ref)
+        grad_num = both[:, :LANES]
         grad_query = None
-        key_sum, value_sum, phi_sum, state_sum = [], [], None, []
+        key_sum, value_sum, phi_sum = [], [], None
         back = [[None, None] for _ in pairs]
         for half in range(2):
             key_half = keys[half].astype(jnp.bfloat16)
@@ -498,8 +683,6 @@
             value_sum.append(left_dot(weights, grad_num))
             term = left_dot(grad_kernel, phi)
             phi_sum = term if phi_sum is None else phi_sum + term
-            reached = (phi.astype(jnp.float32) * reach_all).astype(jnp.bfloat16)
-            state_sum.append(left_dot(both, reached))
             grad_phi = forward_product(grad_kernel, phi_key)
             grad_phi = grad_phi + forward_product(both, state_pair[half]) * reach_all
             projected = feature_back(phi, grad_phi)
@@ -518,12 +701,6 @@
         ):
             total = in_half(sums[0], 0, half) + in_half(sums[1], 1, half)
             kv_grads[at] = kv_grads[at] + total * scale
-        low, high = state_sum
-        totals = low[128:129] + low[160:161] + high[192:193] + high[224:225]
-        state_grad = stacked(
-            [low[:64] + high[64:128], jnp.broadcast_to(totals, (STATE_ROWS - 64, LANES))]
-        )
-        carry_ref[g] = state_grad.astype(jnp.bfloat16)
         at = sizes.kv_lanes + g * LANES
         own_ref[:, at : at + LANES] = phi_sum[WIN:]
         back_ref[:, at : at + LANES] = phi_sum[:WIN].astype(jnp.bfloat16)
@@ -577,12 +754,6 @@
         lin_ref[:, lanes] = unrotated(kv_grads[at], cos, sin).astype(jnp.bfloat16)
 
 
-def told(microseconds):
-    return pl.CostEstimate(
-        flops=int(microseconds * 500_000_000), bytes_accessed=0, transcendentals=0
-    )
-
-
 def by_row(kernel, name, rows, inputs, outputs, microseconds):
     def spec(shape, kind):
         rest = tuple(shape[1:])
@@ -642,10 +813,6 @@
 
 def fixed(shape):
     return pl.BlockSpec(shape, lambda t: (0,) * len(shape), pipeline_mode=pl.Buffered(1))
-
-
-def kernel_params():
-    return pltpu.CompilerParams(vmem_limit_bytes=56 * 1024 * 1024)
 
 
 def mlp_forward(rows, cotangent, weights, microseconds):
@@ -690,58 +857,141 @@
     )(rows, cotangent, weights, weights, weights)
 
 
-def turned_product(terms, before, dtype, microseconds):
+def turned_product(terms, before, dtype, microseconds, split=False, weigh=None):
     count, width = terms[0][0].shape[0], terms[0][1].shape[0]
     tile = min(512, width)
-
-    def kernel(*refs):
-        total = None if before is None else refs[-2][...]
+    tiles = width // tile
+    chips = lax.axis_size("head") // 2
+    rows = count // (2 * chips)
+    core = (lax.axis_index("head") % 2).astype(jnp.int32)
+    extra = [] if before is None else [before]
+    extra += [] if weigh is None else [weigh[0], weigh[1].astype(jnp.float32)[None]]
+
+    def kernel(core_ref, *refs):
+        total = None if before is None else refs[2 * len(terms)][...]
         for left_ref, weight_ref in zip(refs, refs[len(terms) : 2 * len(terms)], strict=False):
             term = right_dot(left_ref[...], weight_ref[...])
             total = term if total is None else total + term
-        refs[-1][...] = total.astype(dtype)
+        if weigh is not None:
+            rows_ref, factors_ref = refs[2 * len(terms) + len(extra) - 2 :][:2]
+            column = jnp.sum(total * rows_ref[...].astype(jnp.float32), axis=0, keepdims=True)
+            refs[-2][...] = column * factors_ref[...]
+            refs = refs[:-2] + refs[-1:]
+        if not split:
+            refs[-1][...] = total.astype(dtype)
+            return
+        mine_ref, *their_refs, held_ref = refs[-2 - tiles :]
+        held_ref[...] = total.astype(dtype)
+
+        def take(out_ref, which):
+            for chip in range(chips):
+                at = pl.multiple_of((2 * chip + which) * rows, rows)
+                out_ref[chip] = held_ref[pl.ds(at, rows), :]
+
+        take(mine_ref, core_ref[0])
+        for turn, their_ref in enumerate(their_refs):
+            pl.when(pl.program_id(0) == turn)(
+                functools.partial(take, their_ref, 1 - core_ref[0])
+            )
 
     def rows_of(section, chunk):
-        return pl.BlockSpec((tile, chunk), lambda t: (t, section))
-
-    out = pl.BlockSpec((count, tile), lambda t: (0, t))
+        return pl.BlockSpec((tile, chunk), lambda t, at: (t, section))
+
+    def whole(shape):
+        return pl.BlockSpec(shape, lambda t, at: (0, 0), pipeline_mode=pl.Buffered(1))
+
+    out = pl.BlockSpec((count, tile), lambda t, at: (0, t))
+    part = pl.BlockSpec((chips, rows, tile), lambda t, at: (0, 0, t))
+    piece = pl.BlockSpec((chips, rows, tile), lambda t, at: (0, 0, 0))
+    line = pl.BlockSpec((1, tile), lambda t, at: (0, t))
+    added = [] if before is None else [out]
+    added += [] if weigh is None else [out, line]
     lefts = [left for left, _, _ in terms]
-    return pl.pallas_call(
+    result = pl.pallas_call(
         kernel,
-        grid=(width // tile,),
-        in_specs=[fixed(left.shape) for left in lefts]
-        + [rows_of(section, left.shape[1]) for left, _, section in terms]
-        + ([] if before is None else [out]),
-        out_specs=out,
-        out_shape=jax.ShapeDtypeStruct((count, width), dtype),
+        grid_spec=pltpu.PrefetchScalarGridSpec(
+            num_scalar_prefetch=1,
+            grid=(tiles,),
+            in_specs=[whole(left.shape) for left in lefts]
+            + [rows_of(section, left.shape[1]) for left, _, section in terms]
+            + added,
+            out_specs=([part] + [piece] * tiles if split else [out])
+            + ([] if weigh is None else [line]),
+            scratch_shapes=[pltpu.VMEM((count, tile), dtype)] if split else [],
+        ),
+        out_shape=(
+            [jax.ShapeDtypeStruct((chips, rows, width), dtype)]
+            + [jax.ShapeDtypeStruct((chips, rows, tile), dtype)] * tiles
+            if split
+            else [jax.ShapeDtypeStruct((count, width), dtype)]
+        )
+        + ([] if weigh is None else [jax.ShapeDtypeStruct((1, width), jnp.float32)]),
         compiler_params=kernel_params(),
         cost_estimate=told(microseconds),
         name="turned_product",
-    )(*lefts, *[weights for _, weights, _ in terms], *([] if before is None else [before]))
-
-
-def weight_gradients(rows, cotangent, grad_gate, grad_up, inner, microseconds):
-    count, width = rows.shape
-    chunk = inner.shape[1]
+    )(core[None], *lefts, *[weights for _, weights, _ in terms], *extra)
+    return result if split else result[0]
+
+
+def weight_gradients(sides, microseconds):
+    count, width = sides[0][0].shape
     tile = min(512, width)
-
-    def kernel(x_ref, c_ref, gate_ref, up_ref, inner_ref, out_ref):
-        sides = ((x_ref, gate_ref), (x_ref, up_ref), (c_ref, inner_ref))
-        for at, (left_ref, right_ref) in enumerate(sides):
-            total = left_dot(left_ref[...], right_ref[...])
-            out_ref[:, at * chunk : (at + 1) * chunk] = total.astype(jnp.bfloat16)
+    lefts, which = [], []
+    for left, _ in sides:
+        at = next((i for i, other in enumerate(lefts) if other is left), len(lefts))
+        if at == len(lefts):
+            lefts.append(left)
+        which.append(at)
+    widths = [right.shape[1] for _, right in sides]
+    starts = [sum(widths[:i]) for i in range(len(widths))]
+
+    def kernel(*refs):
+        for at, right_ref, start, size in zip(
+            which, refs[len(lefts) : -1], starts, widths, strict=True
+        ):
+            total = left_dot(refs[at][...], right_ref[...])
+            refs[-1][:, start : start + size] = total.astype(jnp.bfloat16)
 
     column = pl.BlockSpec((count, tile), lambda t: (0, t))
     return pl.pallas_call(
         kernel,
         grid=(width // tile,),
-        in_specs=[column, column] + [fixed(inner.shape)] * 3,
-        out_specs=pl.BlockSpec((tile, 3 * chunk), lambda t: (t, 0)),
-        out_shape=jax.ShapeDtypeStruct((width, 3 * chunk), jnp.bfloat16),
+        in_specs=[column] * len(lefts) + [fixed(right.shape) for _, right in sides],
+        out_specs=pl.BlockSpec((tile, sum(widths)), lambda t: (t, 0)),
+        out_shape=jax.ShapeDtypeStruct((width, sum(widths)), jnp.bfloat16),
         compiler_params=kernel_params(),
         cost_estimate=told(microseconds),
         name="weight_gradients",
-    )(rows, cotangent, grad_gate, grad_up, inner)
+    )(*lefts, *[right for _, right in sides])
+
+
+def attended_back(grads, weights, lowrank_up, lowrank_down, microseconds):
+    count, width = grads.shape
+    heads, rank = lowrank_down.shape
+    part = min(256, count)
+
+    def kernel(x_ref, w_ref, up_ref, down_ref, out_ref, low_ref):
+        low = (adapter_scale * right_dot(x_ref[...], up_ref[...])).astype(jnp.bfloat16)
+        total = forward_product(x_ref[...], w_ref[...]) + right_dot(low, down_ref[...])
+        out_ref[...] = total.astype(jnp.bfloat16)
+        low_ref[...] = low
+
+    def rows(size):
+        return pl.BlockSpec((part, size), lambda t: (t, 0))
+
+    return pl.pallas_call(
+        kernel,
+        grid=(count // part,),
+        in_specs=[rows(width), fixed(weights.shape), fixed(lowrank_up.shape), fixed(lowrank_down.shape)],
+        out_specs=[rows(heads), rows(rank)],
+        out_shape=[
+            jax.ShapeDtypeStruct((count, heads), jnp.bfloat16),
+            jax.ShapeDtypeStruct((count, rank), jnp.bfloat16),
+        ],
+        compiler_params=kernel_params(),
+        cost_estimate=told(microseconds),
+        name="attended_back",
+    )(grads, weights, lowrank_up, lowrank_down)
 
 
 def document_facts(document_index, shard):
@@ -819,8 +1069,8 @@
         odd = self.half(self.carried_of(self.pair + 1), True) == self.end(1)
         return even, odd
 
-    def forward(self, whole, first):
-        before = shifted(first, 1)
+    def forward(self, whole, first, tail):
+        before, halo = shifted(first, 1), shifted(tail, 1)
         even, odd = self.split(whole)
         window = odd + masked(even, self.end(0) == self.end(-1))
         sums = None
@@ -839,14 +1089,16 @@
                 )
             window = window + masked(got, self.end(2 * distance - 1) == self.end(-1))
         reach = self.reach()
+        sums = after(sums, before, halo)
         total = self.join(masked(sums[0], reach[0]), masked(sums[1], reach[1]))
-        return (total + before.astype(jnp.float32)).astype(jnp.bfloat16)
-
-    def backward(self, grads):
-        first = shifted(grads, -1)
+        return (total + before.astype(jnp.float32)).astype(jnp.bfloat16), halo
+
+    def backward(self, grads, back, other):
+        first, returned = shifted(grads, -1), shifted(back, -1)
         even, odd = self.split(grads)
         reach = self.reach()
         even, odd = masked(even, reach[0]), masked(odd, reach[1])
+        even, odd = after((even, odd), other)
         window = None
         for distance in reversed(self.steps):
             there = self.end(2 * distance - 1)
@@ -862,7 +1114,8 @@
                 got = shifted(sent.astype(jnp.bfloat16), -2 * distance).astype(jnp.float32)
                 window = got if window is None else window + got
         even = masked(window, self.end(0) == self.end(-1)) + direct
-        return self.join(even, window).astype(jnp.bfloat16), first
+        even, window = after((even, window), first, returned)
+        return self.join(even, window).astype(jnp.bfloat16), first, returned
 
 
 def body(
@@ -896,7 +1149,7 @@
     tokens_here = row_count * shard
     block_rows = query_weight.shape[0]
     hidden_units = gate_weight.shape[1]
-    chunk = hidden_units // MLP_CHUNKS
+    chunk = hidden_units // 2
     query_width, key_width = query_weight.shape[1], key_weight.shape[1]
     key_end = query_width + key_width
 
@@ -906,18 +1159,15 @@
     )
     first_gather.advance(quarters=4)
     down_turned = down_weight.T
-    gathers = []
-    for turn in range(MLP_CHUNKS):
-        span = slice(turn * chunk, (turn + 1) * chunk)
-        gathers.append(
-            Gather(
-                jnp.concatenate(
-                    [gate_weight[:, span], up_weight[:, span], down_turned[:, span]], axis=1
-                )
+    early, late = [
+        Gather(
+            jnp.concatenate(
+                [gate_weight[:, span], up_weight[:, span], down_turned[:, span]], axis=1
             )
         )
-    early, late = gathers
-    early.advance(*first_gather.found[first_gather.half])
+        for span in (slice(0, chunk), slice(chunk, hidden_units))
+    ]
+    early.advance(*first_gather.edge())
     complete_qkv, out_turned = first_gather.assemble(sizes.linear, out_width)
 
     adapters = jnp.zeros((3 * rank, sizes.linear), jnp.bfloat16)
@@ -962,10 +1212,10 @@
         ],
         16,
     )
+    early.advance(rotated)
     tail, whole, first = after((tail, whole, first), *early.edge())
-    halo = shifted(tail, 1)
     carries = Carries(last_of, carried_of, row_count)
-    carry = carries.forward(whole, first)
+    carry, halo = carries.forward(whole, first, tail)
     early.advance(carry, halo)
     attended, denominator = by_row(
         functools.partial(attend_kernel, sizes),
@@ -987,87 +1237,134 @@
     )
 
     lowrank_output = forward_product(attended, adapter_output_down).astype(jnp.bfloat16)
-    out_part = right_dot(attended, out_turned) + adapter_scale * forward_product(
-        lowrank_output, adapter_output_up
-    )
-    out_part = after(out_part.astype(jnp.bfloat16), *early.edge())
-    early.advance(out_part)
+    out_sum = HeadSum(
+        *turned_product(
+            [(attended, out_turned, 0), (lowrank_output, (adapter_scale * adapter_output_up.T).astype(jnp.bfloat16), 0)],
+            None,
+            jnp.bfloat16,
+            5,
+            split=True,
+        )
+    )
+    out_sent = out_sum.pair()
     own_rows = row_count // lax.axis_size("head")
     first_row = lax.axis_index("head") * own_rows
     own_tokens = lax.dynamic_slice_in_dim(tokens, first_row, own_rows, 0)
-    own_tokens = own_tokens.reshape(own_rows * shard, width).astype(jnp.float32)
+    own_tokens = own_tokens.reshape(own_rows * shard, width)
     own_cotangent = lax.dynamic_slice_in_dim(cotangent, first_row, own_rows, 0)
-    own_cotangent = own_cotangent.reshape(own_rows * shard, width).astype(jnp.float32)
-    out_sum = head_scatter(out_part)
-    hidden_state = own_tokens + out_sum
-    scale_two = lax.rsqrt(jnp.mean(hidden_state * hidden_state, axis=-1, keepdims=True) + epsilon)
-    unit_two = hidden_state * scale_two
-    own_normed = (unit_two * second_norm_gain.astype(jnp.float32)).astype(jnp.bfloat16)
-    own_normed = after(own_normed, *early.edge())
-    early.advance(own_normed)
-    late.advance(own_normed)
-    normed_rows = head_gather(own_normed)
+    own_cotangent = own_cotangent.reshape(own_rows * shard, width)
+
+    def normed_forward(total, own, gain):
+        hidden = own + total
+        scale = lax.rsqrt(jnp.mean(hidden * hidden, axis=1, keepdims=True) + epsilon)
+        return hidden, hidden * scale * gain, None
+
+    def normed_backward(total, own, values, gain):
+        scale = lax.rsqrt(jnp.mean(values * values, axis=1, keepdims=True) + epsilon)
+        unit = values * scale
+        inner = total * gain
+        inner = inner - unit * jnp.mean(inner * unit, axis=1, keepdims=True)
+        grad = own + scale * inner
+        return grad, grad, total * unit
+
+    out_sum.kept = after(out_sum.kept, *early.edge())
+    early.advance(*out_sent)
+    hidden_state, own_normed, _ = out_sum.finish(
+        normed_forward, [own_tokens], second_norm_gain, True, False, "second_norm"
+    )
+    normed_gather = HeadGather(own_normed)
+    late.advance(*early.edge())
+    first_edge = late.edge()
+    late.advance(*normed_gather.edge())
+    normed_rows = normed_gather.rows(*first_edge)
 
     grad_out = cotangent.reshape(tokens_here, width)
-
     (weights_early,) = early.assemble(3 * chunk)
     gate_early, up_early, inner_early = mlp_forward(normed_rows, grad_out, weights_early, 22)
     gate_early = after(gate_early, *late.edge())
-    late.advance()
+    late.advance(up_early)
     part_early = turned_product(
         [(gate_early, weights_early, 0), (up_early, weights_early, 1)], None, jnp.float32, 14
     )
     grads_early = weight_gradients(
-        normed_rows, grad_out, gate_early, up_early, after(inner_early, part_early), 19
-    )
-    grads_early = after(grads_early, *late.edge())
-    late.advance()
-    scatter_early = Scatter([grads_early], block_rows)
+        [
+            (normed_rows, gate_early),
+            (normed_rows, up_early),
+            (grad_out, after(inner_early, part_early)),
+        ],
+        19,
+    )
+    late.advance(grads_early)
+    scatter_early = Scatter(grads_early, block_rows)
     scatter_early.advance(*late.edge())
-    late.advance()
     (weights_late,) = late.assemble(3 * chunk)
     gate_late, up_late, inner_late = mlp_forward(normed_rows, grad_out, weights_late, 22)
     gate_late = after(gate_late, *scatter_early.edge())
-    scatter_early.advance()
-    normed_two_part = turned_product(
-        [(gate_late, weights_late, 0), (up_late, weights_late, 1)], part_early, jnp.bfloat16, 14
-    )
-    both_cores = head_pair_sum(normed_two_part)
-    scatter_early.advance(normed_two_part)
+    scatter_early.advance(up_late)
+    normed_two_sum = HeadSum(
+        *turned_product(
+            [(gate_late, weights_late, 0), (up_late, weights_late, 1)],
+            part_early,
+            jnp.bfloat16,
+            15,
+            split=True,
+        )
+    )
+    normed_two_sent = normed_two_sum.pair()
+    inner_late = after(inner_late, *normed_two_sent, *scatter_early.edge())
+    scatter_early.advance(*normed_two_sent)
     grads_late = weight_gradients(
-        normed_rows, grad_out, gate_late, up_late, after(inner_late, both_cores), 19
-    )
-    grad_normed_two = head_finish(both_cores)
-    scatter_late = Scatter([grads_late], block_rows)
-    scatter_late.advance(*scatter_early.edge())
-    scatter_early.advance(grads_late)
-    grad_gain_two = jnp.sum(grad_normed_two * unit_two, axis=0, keepdims=True)
-    inner_two = grad_normed_two * second_norm_gain.astype(jnp.float32)
-    grad_hidden = own_cotangent + scale_two * (
-        inner_two - unit_two * jnp.mean(inner_two * unit_two, axis=-1, keepdims=True)
-    )
-    grad_branch = head_gather(grad_hidden.astype(jnp.bfloat16))
-    down_part = turned_product(
-        [(inner_early, weights_early, 2), (after(inner_late, grads_late), weights_late, 2)],
-        None,
-        jnp.bfloat16,
-        13,
-    )
-    down_sum = head_finish(head_pair_sum(down_part), grad_branch)
-    scatter_late.advance(grad_hidden)
-    grad_branch = after(grad_branch, *scatter_late.edge())
+        [(normed_rows, gate_late), (normed_rows, up_late), (grad_out, inner_late)], 19
+    )
+    normed_two_sum.kept = after(normed_two_sum.kept, grads_late)
+    grad_hidden, branch_pieces, grad_gain_two = normed_two_sum.finish(
+        normed_backward,
+        [own_cotangent, hidden_state],
+        second_norm_gain,
+        True,
+        True,
+        "second_norm_back",
+    )
+    branch_gather = HeadGather(branch_pieces)
+    scatter_early.advance(grad_hidden)
+    down_sum = HeadSum(
+        *turned_product(
+            [(inner_early, weights_early, 2), (after(inner_late, grad_hidden, *scatter_early.sending), weights_late, 2)],
+            None,
+            jnp.bfloat16,
+            1500,
+            split=True,
+        )
+    )
+    grad_branch = branch_gather.rows(down_sum.mine)
+    scatter_late = Scatter(grads_late, block_rows)
+    scatter_late.advance(grad_branch)
+    down_sum.mine = after(down_sum.mine, grad_branch)
+    down_sum.pair()
+    grad_attended, grad_lowrank_out = attended_back(
+        grad_branch, out_turned, adapter_output_up, adapter_output_down, 4
+    )
+    grad_attended = after(grad_attended, *scatter_early.edge(), *down_sum.sent)
+    (carry_grads,) = by_row(
+        functools.partial(carry_kernel, sizes),
+        "carry_back",
+        row_count,
+        [
+            (phi, "flat"),
+            (meta, "row"),
+            (attended, "flat"),
+            (denominator, "flat"),
+            (grad_attended, "flat"),
+        ],
+        [(states, "row")],
+        5,
+    )
+    scatter_late.up, scatter_late.down = after(scatter_late.edge(), carry_grads)
     scatter_late.advance()
-    out_up_gradient = adapter_scale * left_dot(lowrank_output, grad_branch)
-    grad_w_out = left_dot(grad_branch, attended).astype(jnp.bfloat16)
-    grad_lowrank_out = adapter_scale * right_dot(grad_branch, adapter_output_up)
-    grad_lowrank_out = grad_lowrank_out.astype(jnp.bfloat16)
-    out_down_gradient = left_dot(grad_lowrank_out, attended)
-    grad_attended = forward_product(grad_branch, out_turned) + right_dot(
-        grad_lowrank_out, adapter_output_down
-    )
+    grad_attended = after(grad_attended, *scatter_late.sending)
 
     own_lanes = sizes.halo_lanes
-    grad_query_lin, own_grads, back, carry_grads, map_query_pairs = by_row(
+    grad_query_lin, own_grads, back, map_query_pairs = by_row(
         functools.partial(backward_kernel, sizes),
         "backward",
         row_count,
@@ -1080,7 +1377,7 @@
             (key_documents, "row"),
             (attended, "flat"),
             (denominator, "flat"),
-            (grad_attended.astype(jnp.bfloat16), "flat"),
+            (grad_attended, "flat"),
             (cosine, "all"),
             (sine, "all"),
             (map_query, "all"),
@@ -1089,18 +1386,33 @@
             (low((tokens_here, query_width)), "flat"),
             (wide((tokens_here, own_lanes)), "flat"),
             (low((row_count, WIN, own_lanes)), "row"),
-            (states, "row"),
             (wide(map_query.shape), "all"),
         ],
-        26,
-    )
-    carry_grads, back = after((carry_grads, back), down_sum, *scatter_late.edge())
-    layer_rows = head_gather((hidden_state + down_sum).astype(jnp.bfloat16))
-    returned = shifted(back, -1)
-    grad_whole, grad_first = carries.backward(carry_grads)
+        2000,
+    )
+    grad_whole, grad_first, returned = carries.backward(
+        carry_grads, back, (grad_query_lin, *scatter_late.edge())
+    )
+    out_up_gradient = adapter_scale * left_dot(lowrank_output, grad_branch)
+    late_edge = scatter_late.edge()
     scatter_late.advance(grad_whole)
-    grad_w_query = left_dot(normalized_input, grad_query_lin).astype(jnp.bfloat16)
-    query_part = right_dot(grad_query_lin, complete_qkv[:, :query_width])
+    grad_whole = after(grad_whole, *late_edge)
+    down_sum.kept = after(down_sum.kept, grad_whole)
+    _, layer_pieces, _ = down_sum.finish(
+        lambda total, values, gain: (None, values + total, None),
+        [hidden_state],
+        second_norm_gain,
+        False,
+        False,
+        "layer_rows",
+        *branch_gather.edge(),
+    )
+    layer_gather = HeadGather(layer_pieces)
+    layer_rows = layer_gather.rows()
+    out_down_gradient = left_dot(grad_lowrank_out, attended)
+    fill = scatter_early.total([chunk] * 3, [False, False, True])
+    grad_whole = after(grad_whole, out_down_gradient, out_up_gradient, *fill, *layer_pieces)
+    mlp_sums = [fill]
     grad_key_lin, map_key_pairs = by_row(
         functools.partial(key_kernel, sizes),
         "keys",
@@ -1125,28 +1437,50 @@
     )
     grad_linear = jnp.concatenate([grad_query_lin, grad_key_lin], axis=1)
     lowrank_gradient = (adapter_scale * right_dot(grad_linear, adapters)).astype(jnp.bfloat16)
-    normed_part = (
-        query_part
-        + right_dot(grad_key_lin, complete_qkv[:, query_width:])
-        + right_dot(lowrank_gradient, adapter_down_weight)
-    ).astype(jnp.bfloat16)
-    normalized_gradient = head_scatter(after(normed_part, layer_rows))
-    grad_w_kv = left_dot(normalized_input, grad_key_lin).astype(jnp.bfloat16)
-    last_scatter = Scatter([grad_w_query, grad_w_out, grad_w_kv], block_rows)
-    last_scatter.advance(*scatter_late.edge())
+    kv_section = query_width // sizes.kv_lanes
+    normed_sum = HeadSum(
+        *turned_product(
+            [
+                (grad_query_lin, complete_qkv, 0),
+                (grad_key_lin, complete_qkv, kv_section),
+                (lowrank_gradient, adapter_down_weight, 0),
+            ],
+            None,
+            jnp.bfloat16,
+            7,
+            split=True,
+        )
+    )
+    normed_sent = normed_sum.pair()
+    late_edge = scatter_late.edge()
+    scatter_late.advance(*normed_sent)
+    last_grads = weight_gradients(
+        [
+            (normalized_input, grad_query_lin),
+            (normalized_input, grad_key_lin),
+            (grad_branch, after(attended, *normed_sent, *scatter_late.sending)),
+        ],
+        10,
+    )
     adapter_gradient = adapter_scale * left_dot(lowrank_input, grad_linear)
     down_gradient = left_dot(lowrank_gradient, normalized_input)
-    gain_one = normed_part.astype(jnp.float32) * (tokens.reshape(tokens_here, width) * scale_one)
-    grad_gain_one = jnp.sum(gain_one, axis=0, keepdims=True)
-    own_scale = lax.rsqrt(jnp.mean(own_tokens * own_tokens, axis=-1, keepdims=True) + epsilon)
-    own_unit = own_tokens * own_scale
-    inner_one = normalized_gradient * first_norm_gain.astype(jnp.float32)
-    own_grad_tokens = grad_hidden + own_scale * (
-        inner_one - own_unit * jnp.mean(inner_one * own_unit, axis=-1, keepdims=True)
-    )
-    grad_tokens_rows = head_gather(own_grad_tokens.astype(jnp.bfloat16)).astype(jnp.float32)
-    last_sum = last_scatter.total()
-    mlp_sums = [scatter_early.total(), scatter_late.total()]
+    last_scatter = Scatter(last_grads, block_rows)
+    last_scatter.advance(*scatter_late.sending)
+    normed_sum.kept = after(normed_sum.kept, last_grads, *scatter_late.sending, layer_rows)
+    _, tokens_pieces, grad_gain_one = normed_sum.finish(
+        normed_backward,
+        [grad_hidden, own_tokens],
+        first_norm_gain,
+        False,
+        True,
+        "first_norm_back",
+    )
+    tokens_gather = HeadGather(tokens_pieces)
+    grad_tokens_rows = tokens_gather.rows().astype(jnp.float32)
+    last_sums = last_scatter.total(
+        [query_width, key_width, key_width, out_width], [False, False, False, True]
+    )
+    mlp_sums.append(scatter_late.total([chunk] * 3, [False, False, True]))
 
     everywhere = jnp.concatenate(
         [down_gradient, out_up_gradient, grad_gain_one, grad_gain_two], axis=0
@@ -1177,21 +1511,15 @@
     maps_sum = small[second:, :64].reshape(-1, 64, 64)
     end = 3 * rank + rank
 
-    def columns(at):
-        return jnp.concatenate([part[:, at * chunk : (at + 1) * chunk] for part in mlp_sums], axis=1)
-
     return (
         layer_rows.reshape(row_count, shard, width),
         grad_tokens_rows.reshape(row_count, shard, width),
         everywhere[end],
         everywhere[end + 1],
-        last_sum[:, :query_width],
-        last_sum[:, query_width + out_width : key_end + out_width],
-        last_sum[:, key_end + out_width :],
-        last_sum[:, query_width : query_width + out_width].T,
-        columns(0),
-        columns(1),
-        columns(2).T,
+        *last_sums,
+        jnp.concatenate([part[0] for part in mlp_sums], axis=1),
+        jnp.concatenate([part[1] for part in mlp_sums], axis=1),
+        jnp.concatenate([part[2] for part in mlp_sums], axis=0),
         everywhere[: 3 * rank].T,
         adapter_sum[:, :query_width],
         adapter_sum[:, query_width:key_end],

time: 903 us -> 849 us (0.940)
  Pallas kernels: 191 us -> 340 us
  waiting for transfers between devices: 349 us -> 266 us
  other arithmetic: 96.3 us -> 29.8 us
  local copies, waits for them, and re-layouts: 120 us -> 74.9 us
  matrix products: 46.4 us -> 15.7 us
  starting transfers between devices: 90.1 us -> 113 us
    pallas_call x8 -> x48, Pallas kernels: 91.3 us -> 234 us  [the longest x24 64.7 us: on_block(): pl.pallas_call(kernel, grid_spec=pltpu.PrefetchScalarGridSpec(num_scalar_...]
    ppermute x48, waiting for transfers between devices: 212 us -> 141 us  [ring_move(): lax.ppermute(block, 'seq', [(order[i], order[(i + step) % count]) for i i...]
    add x17 -> x2, other arithmetic: 38.3 us -> 1.16 us  [the longest x1 1.02 us: backward(): even = masked(window, self.end(0) == self.end(-1)) + direct]
    dot_general x7 -> x1, matrix products: 23 us -> 1.25 us  [right_dot(): lax.dot_general(left, right, (((1,), (1,)), ((), ())), preferred_element_...]
    dynamic_update_slice x13 -> x0, local copies, waits for them, and re-layouts: 18.1 us -> none  [the longest x8 9.59 us: head_gather(): lax.dynamic_update_index_in_dim(whole, core_swap(block), at + 1 - core, 0)]
    ppermute x8, waiting for transfers between devices: 44.2 us -> 29.8 us  [shifted(): return lax.ppermute(block, 'seq', route)]
    unnamed x307 -> x297, local copies, waits for them, and re-layouts: 39.2 us -> 50.9 us
    ppermute x8 -> x16, starting transfers between devices: 6.94 us -> 18.3 us  [chip_move(): lax.ppermute(block, 'head', [(i, (i + 2 * step) % count) for i in range(c...]
  transfers between devices with their start and end apart: 85 -> 113, of which waited for: 42 -> 54; matrix products, arithmetic and copies ran while one was open for 22% -> 8% of each run, Pallas kernels for 20% -> 40%
where the time goes in v3:
time: 849 us; the launch traced here: 842 us
  Pallas kernels  340 us (40%)
  waiting for transfers between devices  266 us (31%)
  starting transfers between devices  113 us (13%)
  local copies, waits for them, and re-layouts  74.9 us (9%)
  other arithmetic  29.8 us (4%)
  matrix products  15.7 us (2%)
    ppermute x48, waiting for transfers between devices, ring_move(): lax.ppermute(block, 'seq', [(order[i], order[(i + step) % count]) for i i...  141 us
    pallas_call x5, Pallas kernels, by_row(): pl.pallas_call(kernel, grid=(rows,), in_specs=[spec(a.shape, kind) for a,...  64.7 us
    pallas_call x24, Pallas kernels, on_block(): pl.pallas_call(kernel, grid_spec=pltpu.PrefetchScalarGridSpec(num_scalar_...  64.7 us
    pallas_call x5, Pallas kernels, turned_product(): pl.pallas_call(kernel, grid_spec=pltpu.PrefetchScalarGridSpec(num_scalar_...  60 us
    ppermute x48, starting transfers between devices, ring_move(): lax.ppermute(block, 'seq', [(order[i], order[(i + step) % count]) for i i...  56.8 us
    unnamed x297, local copies, waits for them, and re-layouts  50.9 us
    ppermute x16, waiting for transfers between devices, chip_move(): lax.ppermute(block, 'head', [(i, (i + 2 * step) % count) for i in range(c...  48.8 us
    pallas_call x3, Pallas kernels, weight_gradients(): pl.pallas_call(kernel, grid=(width // tile,), in_specs=[column] * len(lef...  48.4 us
  transfers between devices with their start and end apart: 113, of which 54 were waited for; matrix products, arithmetic and copies ran while one was open for 8% of the time, Pallas kernels for 40%

profile of v3, /device:TPU:0, one launch (start us, length us, event | category | flops | bytes accessed | tf_op | source)
XLA Modules:
  0.0 841.7 jit_solution(13706386490501841185)
XLA Ops:
  24.8 11.8 %collective-permute-done.1.refs_1_ = bf16[256,1280]{1,0:T(8,128)(2,1)S(1)} collective-permute-done((bf16[256,1280]{1,0:T(8,128)(2,1)S(1)}, bf16[256,1280]{1,0:T(8,128)(2,1)S(1)}, u32[]{:S(2)}, u32[]{:S(2)}) %collective-permute-start.1) | collective-permute-done | bytes 655392 | tf_op jit(solution)/shard_map/ppermute | solution.py:49
  39.7 12.0 %collective-permute-done.2.refs_0_ = bf16[256,1280]{1,0:T(8,128)(2,1)S(1)} collective-permute-done((bf16[256,1280]{1,0:T(8,128)(2,1)S(1)}, bf16[256,1280]{1,0:T(8,128)(2,1)S(1)}, u32[]{:S(2)}, u32[]{:S(2)}) %collective-permute-start.2) | collective-permute-done | bytes 655392 | tf_op jit(solution)/shard_map/ppermute | solution.py:49
  76.2 16.6 %prepare.1 = (bf16[1024,768]{1,0:T(8,128)(2,1)S(1)}, bf16[1024,1280]{1,0:T(8,128)(2,1)}, bf16[8,64,512]{2,1,0:T(8,128)(2,1)S(1)}, bf16[8,2,80,128]{3,2,1,0:T(8,128)(2,1)S(1)}, bf16[8,2,80,128]{3,2,1,0:T(8,128)(2,1)S(1)}) custom-call(f32[1024,768]{1,0:T(8,128)} %multiply_add_fusion.lin_ref, f32[128,768]{1,0:T(8,128)S(1)} %concatenate.88.cos_ref, ...), custom_call_target="tpu_custom_call" | custom-call | flops 160000000 | tf_op jit(solution)/shard_map/prepare/pallas_call | solution.py:766
  96.4 31.3 %collective-permute-done.9.refs_1_ = bf16[256,3072]{1,0:T(8,128)(2,1)} collective-permute-done((bf16[256,3072]{1,0:T(8,128)(2,1)}, bf16[256,3072]{1,0:T(8,128)(2,1)}, u32[]{:S(2)}, u32[]{:S(2)}) %collective-permute-start.9) | collective-permute-done | bytes 1572896 | tf_op jit(solution)/shard_map/ppermute | solution.py:49
  175.9 8.3 attend.1
  212.3 13.3 %collective-permute-done.30.refs_7_ = bf16[128,3072]{1,0:T(8,128)(2,1)S(1)} collective-permute-done((bf16[128,3072]{1,0:T(8,128)(2,1)S(1)}, bf16[128,3072]{1,0:T(8,128)(2,1)S(1)}, u32[]{:S(2)}, u32[]{:S(2)}) %collective-permute-start.30) | collective-permute-done | bytes 786464 | tf_op jit(solution)/shard_map/ppermute | solution.py:49
  236.7 10.1 %collective-permute-done.24.refs_0_ = bf16[128,2048]{1,0:T(8,128)(2,1)S(1)} collective-permute-done((bf16[128,2048]{1,0:T(8,128)(2,1)}, bf16[128,2048]{1,0:T(8,128)(2,1)S(1)}, u32[]{:S(2)}, u32[]{:S(2)}) %collective-permute-start.24) | collective-permute-done | bytes 524320 | tf_op jit(solution)/shard_map/ppermute | solution.py:270
  260.7 13.2 %collective-permute-done.28.refs_4_ = bf16[128,2048]{1,0:T(8,128)(2,1)} collective-permute-done((bf16[128,2048]{1,0:T(8,128)(2,1)}, bf16[128,2048]{1,0:T(8,128)(2,1)}, u32[]{:S(2)}, u32[]{:S(2)}) %collective-permute-start.28) | collective-permute-done | bytes 524320 | tf_op jit(solution)/shard_map/ppermute | solution.py:270
  300.7 20.7 %hidden_units.2 = (bf16[1024,1024]{1,0:T(8,128)(2,1)}, bf16[1024,1024]{1,0:T(8,128)(2,1)}, bf16[1024,1024]{1,0:T(8,128)(2,1)}) custom-call(bf16[1024,2048]{1,0:T(8,128)(2,1)} %copy-done.2, bf16[1024,2048]{1,0:T(8,128)(2,1)} %bitcast.133, bf16[2048,3072]{1,0:T(8,128)(2,1)} %copy-done, bf16[2048,3072]{1,0:T(8,128)(2,1)} %copy-done, bf16[2048,3072]{1,0:T(8,128)(2,1)} %copy-done), custom_call_target="tpu_custom_call" | custom-call | flops 220000000 | tf_op jit(solution)/shard_map/hidden_units/pallas_call | solution.py:847
  323.5 13.7 %turned_product.6.refs_4_ = f32[1024,2048]{1,0:T(8,128)} custom-call(s32[1]{0:T(128)} %bitcast.5.core_ref, bf16[1024,1024]{1,0:T(8,128)(2,1)} %get-tuple-element.211.refs_0_.refs_2_, bf16[1024,1024]{1,0:T(8,128)(2,1)} %get-tuple-element.206.refs_1_.refs_3_, bf16[2048,3072]{1,0:T(8,128)(2,1)} %copy-done, bf16[2048,3072]{1,0:T(8,128)(2,1)} %copy-done), custom_call_target="tpu_custom_call" | custom-call | flops 140000000 | tf_op jit(solution)/shard_map/turned_product/pallas_call | solution.py:910
  337.2 19.0 %weight_gradients.3.own_ref = bf16[2048,3072]{1,0:T(8,128)(2,1)} custom-call(bf16[1024,2048]{1,0:T(8,128)(2,1)} %copy-done.2, bf16[1024,2048]{1,0:T(8,128)(2,1)} %bitcast.134, bf16[1024,1024]{1,0:T(8,128)(2,1)} %get-tuple-element.211.refs_0_.refs_2_, bf16[1024,1024]{1,0:T(8,128)(2,1)} %get-tuple-element.206.refs_1_.refs_3_, ...), custom_call_target="tpu_custom_call" | custom-call | flops 190000000 | tf_op jit(solution)/shard_map/weight_gradients/pallas_call | solution.py:956
  363.1 14.3 %collective-permute-done.40.refs_7_ = bf16[128,3072]{1,0:T(8,128)(2,1)S(1)} collective-permute-done((bf16[128,3072]{1,0:T(8,128)(2,1)S(1)}, bf16[128,3072]{1,0:T(8,128)(2,1)S(1)}, u32[]{:S(2)}, u32[]{:S(2)}) %collective-permute-start.40) | collective-permute-done | bytes 786464 | tf_op jit(solution)/shard_map/ppermute | solution.py:49
  389.5 20.7 %hidden_units.3 = (bf16[1024,1024]{1,0:T(8,128)(2,1)}, bf16[1024,1024]{1,0:T(8,128)(2,1)}, bf16[1024,1024]{1,0:T(8,128)(2,1)}) custom-call(bf16[1024,2048]{1,0:T(8,128)(2,1)} %copy-done.2, bf16[1024,2048]{1,0:T(8,128)(2,1)} %bitcast.135, bf16[2048,3072]{1,0:T(8,128)(2,1)} %copy-done.1, bf16[2048,3072]{1,0:T(8,128)(2,1)} %copy-done.1, ...), custom_call_target="tpu_custom_call" | custom-call | flops 220000000 | tf_op jit(solution)/shard_map/hidden_units/pallas_call | solution.py:847
  419.7 15.3 %turned_product.7 = (bf16[2,256,2048]{2,1,0:T(8,128)(2,1)}, bf16[2,256,512]{2,1,0:T(8,128)(2,1)}, bf16[2,256,512]{2,1,0:T(8,128)(2,1)}, bf16[2,256,512]{2,1,0:T(8,128)(2,1)}, bf16[2,256,512]{2,1,0:T(8,128)(2,1)}) custom-call(s32[1]{0:T(128)} %bitcast.5.core_ref, bf16[1024,1024]{1,0:T(8,128)(2,1)} %get-tuple-element.221.refs_0_.refs_2_, ...), custom_call_target="tpu_custom_call" | custom-call | flops 150000000 | tf_op jit(solution)/shard_map/turned_product/pallas_call | solution.py:910
  462.9 19.0 %weight_gradients.4.own_ref = bf16[2048,3072]{1,0:T(8,128)(2,1)} custom-call(bf16[1024,2048]{1,0:T(8,128)(2,1)} %copy-done.2, bf16[1024,2048]{1,0:T(8,128)(2,1)} %bitcast.136, bf16[1024,1024]{1,0:T(8,128)(2,1)} %get-tuple-element.221.refs_0_.refs_2_, bf16[1024,1024]{1,0:T(8,128)(2,1)} %get-tuple-element.222.refs_1_.refs_3_, ...), custom_call_target="tpu_custom_call" | custom-call | flops 190000000 | tf_op jit(solution)/shard_map/weight_gradients/pallas_call | solution.py:956
  498.2 14.4 %turned_product.8 = (bf16[2,256,2048]{2,1,0:T(8,128)(2,1)}, bf16[2,256,512]{2,1,0:T(8,128)(2,1)}, bf16[2,256,512]{2,1,0:T(8,128)(2,1)}, bf16[2,256,512]{2,1,0:T(8,128)(2,1)}, bf16[2,256,512]{2,1,0:T(8,128)(2,1)}) custom-call(s32[1]{0:T(128)} %bitcast.5.core_ref, bf16[1024,1024]{1,0:T(8,128)(2,1)} %get-tuple-element.212.refs_4_.refs_0_, ...), custom_call_target="tpu_custom_call" | custom-call | flops 15000000512 | tf_op jit(solution)/shard_map/turned_product/pallas_call | solution.py:910
  538.3 13.2 %collective-permute-done.64.up_ref = bf16[256,3072]{1,0:T(8,128)(2,1)} collective-permute-done((bf16[256,3072]{1,0:T(8,128)(2,1)}, bf16[256,3072]{1,0:T(8,128)(2,1)}, u32[]{:S(2)}, u32[]{:S(2)}) %collective-permute-start.64) | collective-permute-done | bytes 1572896 | tf_op jit(solution)/shard_map/ppermute | solution.py:49
  577.9 25.2 %backward.1 = (bf16[1024,512]{1,0:T(8,128)(2,1)S(1)}, f32[1024,512]{1,0:T(8,128)}, bf16[8,64,512]{2,1,0:T(8,128)(2,1)S(1)}, f32[4,128,256]{2,1,0:T(8,128)S(1)}) custom-call(bf16[1024,768]{1,0:T(8,128)(2,1)} %copy-done.9, bf16[1024,1280]{1,0:T(8,128)(2,1)} %get-tuple-element.171.phi_ref, bf16[8,64,512]{2,1,0:T(8,128)(2,1)S(1)} %copy-done.43, ...), custom_call_target="tpu_custom_call" | custom-call | flops 20000000000 | tf_op jit(solution)/shard_map/backward/pallas_call | solution.py:766
  604.8 9.8 %collective-permute-done.66 = bf16[4,2,80,128]{3,2,1,0:T(8,128)(2,1)S(1)} collective-permute-done((bf16[4,2,80,128]{3,2,1,0:T(8,128)(2,1)S(1)}, bf16[4,2,80,128]{3,2,1,0:T(8,128)(2,1)S(1)}, u32[]{:S(2)}, u32[]{:S(2)}) %collective-permute-start.66) | collective-permute-done | bytes 163872 | tf_op jit(solution)/shard_map/ppermute | solution.py:1054
  635.4 16.2 %collective-permute-done.72 = bf16[2,4,2,80,128]{4,3,2,1,0:T(8,128)(2,1)S(1)} collective-permute-done((bf16[2,4,2,80,128]{4,3,2,1,0:T(8,128)(2,1)S(1)}, bf16[2,4,2,80,128]{4,3,2,1,0:T(8,128)(2,1)S(1)}, u32[]{:S(2)}, u32[]{:S(2)}) %collective-permute-start.72) | collective-permute-done | bytes 327712 | tf_op jit(solution)/shard_map/ppermute | solution.py:39
  679.6 9.0 %turned_product.9 = (bf16[2,256,2048]{2,1,0:T(8,128)(2,1)}, bf16[2,256,512]{2,1,0:T(8,128)(2,1)}, bf16[2,256,512]{2,1,0:T(8,128)(2,1)}, bf16[2,256,512]{2,1,0:T(8,128)(2,1)}, bf16[2,256,512]{2,1,0:T(8,128)(2,1)}) custom-call(s32[1]{0:T(128)} %bitcast.5.core_ref, bf16[1024,512]{1,0:T(8,128)(2,1)} %copy-done.7, bf16[1024,256]{1,0:T(8,128)(2,1)} %copy-done.13, ...), custom_call_target="tpu_custom_call" | custom-call | flops 70000000 | tf_op jit(solution)/shard_map/turned_product/pallas_call | solution.py:910
  709.8 8.4 %collective-permute-done.81.refs_5_ = bf16[128,2048]{1,0:T(8,128)(2,1)S(1)} collective-permute-done((bf16[128,2048]{1,0:T(8,128)(2,1)S(1)}, bf16[128,2048]{1,0:T(8,128)(2,1)S(1)}, u32[]{:S(2)}, u32[]{:S(2)}) %collective-permute-start.81) | collective-permute-done | bytes 524320 | tf_op jit(solution)/shard_map/ppermute | solution.py:270
  722.7 10.3 %weight_gradients.5.own_ref = bf16[2048,1280]{1,0:T(8,128)(2,1)} custom-call(bf16[1024,2048]{1,0:T(8,128)(2,1)} %copy-done.50, bf16[1024,2048]{1,0:T(8,128)(2,1)} %copy-done.3, bf16[1024,512]{1,0:T(8,128)(2,1)} %copy-done.7, bf16[1024,256]{1,0:T(8,128)(2,1)} %copy-done.13, bf16[1024,512]{1,0:T(8,128)(2,1)} %copy-done.4), custom_call_target="tpu_custom_call" | custom-call | flops 100000000 | tf_op jit(solution)/shard_map/weight_gradients/pallas_call | solution.py:956
  820.0 10.5 %collective-permute-done.102 = bf16[1264,128]{1,0:T(8,128)(2,1)S(1)} collective-permute-done((bf16[1264,128]{1,0:T(8,128)(2,1)S(1)}, bf16[1264,128]{1,0:T(8,128)(2,1)S(1)}, u32[]{:S(2)}, u32[]{:S(2)}) %collective-permute-start.102) | collective-permute-done | bytes 323616 | tf_op jit(solution)/shard_map/ppermute | solution.py:406
  (677 shorter events, 482.4 us)
Async XLA Ops:
  170.5 33.8 %collective-permute-start.22 = (bf16[256,3072]{1,0:T(8,128)(2,1)}, bf16[256,3072]{1,0:T(8,128)(2,1)}, u32[]{:S(2)}, u32[]{:S(2)}) collective-permute-start(bf16[256,3072]{1,0:T(8,128)(2,1)} %collective-permute-done.9.refs_1_), channel_id=1, source_target_pairs={{0,8},{8,16},{16,24},{24,28},{28,20},{20,12},{12,4},{4,0},{1,9},{9... | collective-permute-start | bytes 4718600 | tf_op jit(solution)/shard_map/ppermute | solution.py:49
  174.8 34.9 %collective-permute-start.23 = (bf16[256,3072]{1,0:T(8,128)(2,1)}, bf16[256,3072]{1,0:T(8,128)(2,1)}, u32[]{:S(2)}, u32[]{:S(2)}) collective-permute-start(bf16[256,3072]{1,0:T(8,128)(2,1)} %collective-permute-done.11.refs_5_), channel_id=1, source_target_pairs={{0,4},{8,0},{16,8},{24,16},{28,24},{20,28},{12,20},{4,12},{1,5},{9... | collective-permute-start | bytes 4718600 | tf_op jit(solution)/shard_map/ppermute | solution.py:49
  229.3 50.9 %collective-permute-start.32 = (bf16[256,3072]{1,0:T(8,128)(2,1)}, bf16[256,3072]{1,0:T(8,128)(2,1)}, u32[]{:S(2)}, u32[]{:S(2)}) collective-permute-start(bf16[256,3072]{1,0:T(8,128)(2,1)} %pad_maximum_fusion.4.refs_3_), channel_id=1, source_target_pairs={{0,8},{8,16},{16,24},{24,28},{28,20},{20,12},{12,4},{4,0},{1,9},{9... | collective-permute-start | bytes 4718600 | tf_op jit(solution)/shard_map/ppermute | solution.py:49
  231.0 50.4 %collective-permute-start.33 = (bf16[256,3072]{1,0:T(8,128)(2,1)}, bf16[256,3072]{1,0:T(8,128)(2,1)}, u32[]{:S(2)}, u32[]{:S(2)}) collective-permute-start(bf16[256,3072]{1,0:T(8,128)(2,1)} %pad_maximum_fusion.4.refs_3_), channel_id=1, source_target_pairs={{0,4},{8,0},{16,8},{24,16},{28,24},{20,28},{12,20},{4,12},{1,5},{9... | collective-permute-start | bytes 4718600 | tf_op jit(solution)/shard_map/ppermute | solution.py:49
  280.2 41.2 %collective-permute-start.36 = (bf16[256,3072]{1,0:T(8,128)(2,1)}, bf16[256,3072]{1,0:T(8,128)(2,1)}, u32[]{:S(2)}, u32[]{:S(2)}) collective-permute-start(bf16[256,3072]{1,0:T(8,128)(2,1)} %collective-permute-done.32.refs_2_), channel_id=1, source_target_pairs={{0,8},{8,16},{16,24},{24,28},{28,20},{20,12},{12,4},{4,0},{1,9},{9... | collective-permute-start | bytes 4718600 | tf_op jit(solution)/shard_map/ppermute | solution.py:49
  281.4 41.2 %collective-permute-start.38 = (bf16[256,3072]{1,0:T(8,128)(2,1)}, bf16[256,3072]{1,0:T(8,128)(2,1)}, u32[]{:S(2)}, u32[]{:S(2)}) collective-permute-start(bf16[256,3072]{1,0:T(8,128)(2,1)} %collective-permute-done.33.refs_4_), channel_id=1, source_target_pairs={{0,4},{8,0},{16,8},{24,16},{28,24},{20,28},{12,20},{4,12},{1,5},{9... | collective-permute-start | bytes 4718600 | tf_op jit(solution)/shard_map/ppermute | solution.py:49
  321.4 36.9 %collective-permute-start.37 = (bf16[256,3072]{1,0:T(8,128)(2,1)}, bf16[256,3072]{1,0:T(8,128)(2,1)S(1)}, u32[]{:S(2)}, u32[]{:S(2)}) collective-permute-start(bf16[256,3072]{1,0:T(8,128)(2,1)} %collective-permute-done.36.refs_1_), channel_id=1, source_target_pairs={{0,8},{8,16},{16,24},{24,28},{28,20},{20,12},{12,4},{4,0},{1,9},{9... | collective-permute-start | bytes 4718600 | tf_op jit(solution)/shard_map/ppermute | solution.py:49
  322.6 37.0 %collective-permute-start.39 = (bf16[256,3072]{1,0:T(8,128)(2,1)}, bf16[256,3072]{1,0:T(8,128)(2,1)S(1)}, u32[]{:S(2)}, u32[]{:S(2)}) collective-permute-start(bf16[256,3072]{1,0:T(8,128)(2,1)} %collective-permute-done.38.refs_5_), channel_id=1, source_target_pairs={{0,4},{8,0},{16,8},{24,16},{28,24},{20,28},{12,20},{4,12},{1,5},{9... | collective-permute-start | bytes 4718600 | tf_op jit(solution)/shard_map/ppermute | solution.py:49
  378.8 35.4 %collective-permute-start.43 = (bf16[128,3072]{1,0:T(8,128)(2,1)}, bf16[128,3072]{1,0:T(8,128)(2,1)S(1)}, u32[]{:S(2)}, u32[]{:S(2)}) collective-permute-start(bf16[128,3072]{1,0:T(8,128)(2,1)} %get-tuple-element.220), channel_id=1, source_target_pairs={{0,4},{8,0},{16,8},{24,16},{28,24},{20,28},{12,20},{4,12},{1,5},{9... | collective-permute-start | bytes 2359304 | tf_op jit(solution)/shard_map/ppermute | solution.py:49
  413.8 34.3 %collective-permute-start.48 = (bf16[256,3072]{1,0:T(8,128)(2,1)}, bf16[256,3072]{1,0:T(8,128)(2,1)S(1)}, u32[]{:S(2)}, u32[]{:S(2)}) collective-permute-start(bf16[256,3072]{1,0:T(8,128)(2,1)} %join_block.18), channel_id=1, source_target_pairs={{0,8},{8,16},{16,24},{24,28},{28,20},{20,12},{12,4},{4,0},{1,9},{9... | collective-permute-start | bytes 4718600 | tf_op jit(solution)/shard_map/ppermute | solution.py:49
  417.9 34.9 %collective-permute-start.49 = (bf16[256,3072]{1,0:T(8,128)(2,1)}, bf16[256,3072]{1,0:T(8,128)(2,1)S(1)}, u32[]{:S(2)}, u32[]{:S(2)}) collective-permute-start(bf16[256,3072]{1,0:T(8,128)(2,1)} %join_block.19), channel_id=1, source_target_pairs={{0,4},{8,0},{16,8},{24,16},{28,24},{20,28},{12,20},{4,12},{1,5},{9... | collective-permute-start | bytes 4718600 | tf_op jit(solution)/shard_map/ppermute | solution.py:49
  452.3 37.7 %collective-permute-start.52 = (bf16[256,3072]{1,0:T(8,128)(2,1)}, bf16[256,3072]{1,0:T(8,128)(2,1)S(1)}, u32[]{:S(2)}, u32[]{:S(2)}) collective-permute-start(bf16[256,3072]{1,0:T(8,128)(2,1)} %join_block.20), channel_id=1, source_target_pairs={{0,8},{8,16},{16,24},{24,28},{28,20},{20,12},{12,4},{4,0},{1,9},{9... | collective-permute-start | bytes 4718600 | tf_op jit(solution)/shard_map/ppermute | solution.py:49
  456.9 37.2 %collective-permute-start.53 = (bf16[256,3072]{1,0:T(8,128)(2,1)}, bf16[256,3072]{1,0:T(8,128)(2,1)S(1)}, u32[]{:S(2)}, u32[]{:S(2)}) collective-permute-start(bf16[256,3072]{1,0:T(8,128)(2,1)} %join_block.22), channel_id=1, source_target_pairs={{0,4},{8,0},{16,8},{24,16},{28,24},{20,28},{12,20},{4,12},{1,5},{9... | collective-permute-start | bytes 4718600 | tf_op jit(solution)/shard_map/ppermute | solution.py:49
  514.0 37.5 %collective-permute-start.64 = (bf16[256,3072]{1,0:T(8,128)(2,1)}, bf16[256,3072]{1,0:T(8,128)(2,1)}, u32[]{:S(2)}, u32[]{:S(2)}) collective-permute-start(bf16[256,3072]{1,0:T(8,128)(2,1)} %join_block.21), channel_id=1, source_target_pairs={{0,8},{8,16},{16,24},{24,28},{28,20},{20,12},{12,4},{4,0},{1,9},{9... | collective-permute-start | bytes 4718600 | tf_op jit(solution)/shard_map/ppermute | solution.py:49
  514.4 37.7 %collective-permute-start.65 = (bf16[256,3072]{1,0:T(8,128)(2,1)}, bf16[256,3072]{1,0:T(8,128)(2,1)}, u32[]{:S(2)}, u32[]{:S(2)}) collective-permute-start(bf16[256,3072]{1,0:T(8,128)(2,1)} %join_block.23), channel_id=1, source_target_pairs={{0,4},{8,0},{16,8},{24,16},{28,24},{20,28},{12,20},{4,12},{1,5},{9... | collective-permute-start | bytes 4718600 | tf_op jit(solution)/shard_map/ppermute | solution.py:49
  522.8 45.0 %collective-permute-start.67 = (bf16[128,3072]{1,0:T(8,128)(2,1)}, bf16[128,3072]{1,0:T(8,128)(2,1)S(1)}, u32[]{:S(2)}, u32[]{:S(2)}) collective-permute-start(bf16[128,3072]{1,0:T(8,128)(2,1)} %get-tuple-element.260), channel_id=1, source_target_pairs={{0,8},{8,16},{16,24},{24,28},{28,20},{20,12},{12,4},{4,0},{1,9},{9... | collective-permute-start | bytes 2359304 | tf_op jit(solution)/shard_map/ppermute | solution.py:49
  523.3 44.9 %collective-permute-start.68 = (bf16[128,3072]{1,0:T(8,128)(2,1)}, bf16[128,3072]{1,0:T(8,128)(2,1)S(1)}, u32[]{:S(2)}, u32[]{:S(2)}) collective-permute-start(bf16[128,3072]{1,0:T(8,128)(2,1)} %get-tuple-element.262), channel_id=1, source_target_pairs={{0,4},{8,0},{16,8},{24,16},{28,24},{20,28},{12,20},{4,12},{1,5},{9... | collective-permute-start | bytes 2359304 | tf_op jit(solution)/shard_map/ppermute | solution.py:49
  574.7 40.0 %collective-permute-start.69 = (bf16[256,3072]{1,0:T(8,128)(2,1)}, bf16[256,3072]{1,0:T(8,128)(2,1)S(1)}, u32[]{:S(2)}, u32[]{:S(2)}) collective-permute-start(bf16[256,3072]{1,0:T(8,128)(2,1)} %join_block.24), channel_id=1, source_target_pairs={{0,8},{8,16},{16,24},{24,28},{28,20},{20,12},{12,4},{4,0},{1,9},{9... | collective-permute-start | bytes 4718600 | tf_op jit(solution)/shard_map/ppermute | solution.py:49
  575.3 39.5 %collective-permute-start.70 = (bf16[256,3072]{1,0:T(8,128)(2,1)}, bf16[256,3072]{1,0:T(8,128)(2,1)S(1)}, u32[]{:S(2)}, u32[]{:S(2)}) collective-permute-start(bf16[256,3072]{1,0:T(8,128)(2,1)} %join_block.25), channel_id=1, source_target_pairs={{0,4},{8,0},{16,8},{24,16},{28,24},{20,28},{12,20},{4,12},{1,5},{9... | collective-permute-start | bytes 4718600 | tf_op jit(solution)/shard_map/ppermute | solution.py:49
  576.8 37.7 %collective-permute-start.66 = (bf16[4,2,80,128]{3,2,1,0:T(8,128)(2,1)S(1)}, bf16[4,2,80,128]{3,2,1,0:T(8,128)(2,1)S(1)}, u32[]{:S(2)}, u32[]{:S(2)}) collective-permute-start(bf16[4,2,80,128]{3,2,1,0:T(8,128)(2,1)S(1)} %constant_dynamic-slice_fusion), channel_id=1, source_target_pairs={{0,4},{4,0},{8,12},{12,8},{16,20},{20,16},{24,28},{28,24},{1,5},{5... | collective-permute-start | bytes 491528 | tf_op jit(solution)/shard_map/ppermute | solution.py:1054
  662.9 36.4 %collective-permute-start.88 = (bf16[256,3072]{1,0:T(8,128)(2,1)}, bf16[256,3072]{1,0:T(8,128)(2,1)}, u32[]{:S(2)}, u32[]{:S(2)}) collective-permute-start(bf16[256,3072]{1,0:T(8,128)(2,1)} %join_block.26), channel_id=1, source_target_pairs={{0,8},{8,16},{16,24},{24,28},{28,20},{20,12},{12,4},{4,0},{1,9},{9... | collective-permute-start | bytes 4718600 | tf_op jit(solution)/shard_map/ppermute | solution.py:49
  663.5 40.3 %collective-permute-start.89 = (bf16[256,3072]{1,0:T(8,128)(2,1)}, bf16[256,3072]{1,0:T(8,128)(2,1)}, u32[]{:S(2)}, u32[]{:S(2)}) collective-permute-start(bf16[256,3072]{1,0:T(8,128)(2,1)} %join_block.28), channel_id=1, source_target_pairs={{0,4},{8,0},{16,8},{24,16},{28,24},{20,28},{12,20},{4,12},{1,5},{9... | collective-permute-start | bytes 4718600 | tf_op jit(solution)/shard_map/ppermute | solution.py:49
  706.7 49.8 %collective-permute-start.98 = (bf16[256,3072]{1,0:T(8,128)(2,1)}, bf16[256,3072]{1,0:T(8,128)(2,1)}, u32[]{:S(2)}, u32[]{:S(2)}) collective-permute-start(bf16[256,3072]{1,0:T(8,128)(2,1)} %join_block.27), channel_id=1, source_target_pairs={{0,8},{8,16},{16,24},{24,28},{28,20},{20,12},{12,4},{4,0},{1,9},{9... | collective-permute-start | bytes 4718600 | tf_op jit(solution)/shard_map/ppermute | solution.py:49
  707.0 49.6 %collective-permute-start.99 = (bf16[256,3072]{1,0:T(8,128)(2,1)}, bf16[256,3072]{1,0:T(8,128)(2,1)}, u32[]{:S(2)}, u32[]{:S(2)}) collective-permute-start(bf16[256,3072]{1,0:T(8,128)(2,1)} %join_block.29), channel_id=1, source_target_pairs={{0,4},{8,0},{16,8},{24,16},{28,24},{20,28},{12,20},{4,12},{1,5},{9... | collective-permute-start | bytes 4718600 | tf_op jit(solution)/shard_map/ppermute | solution.py:49
  (235 other events, 2963.8 us)

commit v4 on v3

--- a/solution.py
+++ b/solution.py
@@ -1273,14 +1273,16 @@
         normed_forward, [own_tokens], second_norm_gain, True, False, "second_norm"
     )
     normed_gather = HeadGather(own_normed)
-    late.advance(*early.edge())
-    first_edge = late.edge()
-    late.advance(*normed_gather.edge())
-    normed_rows = normed_gather.rows(*first_edge)
+    late.advance(*early.edge(), *own_normed)
+    normed_rows = normed_gather.rows()
+    late_edge = late.edge()
+    late.advance(normed_rows)
 
     grad_out = cotangent.reshape(tokens_here, width)
     (weights_early,) = early.assemble(3 * chunk)
-    gate_early, up_early, inner_early = mlp_forward(normed_rows, grad_out, weights_early, 22)
+    gate_early, up_early, inner_early = mlp_forward(
+        normed_rows, after(grad_out, *late_edge), weights_early, 22
+    )
     gate_early = after(gate_early, *late.edge())
     late.advance(up_early)
     part_early = turned_product(

time: 849 us -> 841 us (level)
    ppermute x48, waiting for transfers between devices: 141 us -> 130 us  [ring_move(): lax.ppermute(block, 'seq', [(order[i], order[(i + step) % count]) for i i...]
    unnamed x297 -> x281, local copies, waits for them, and re-layouts: 50.9 us -> 48.6 us
where the time goes in v4:
time: 841 us; the launch traced here: 834 us
  Pallas kernels  339 us (40%)
  waiting for transfers between devices  259 us (31%)
  starting transfers between devices  112 us (13%)
  local copies, waits for them, and re-layouts  76.2 us (9%)
  other arithmetic  29.8 us (4%)
  matrix products  15.7 us (2%)
    ppermute x48, waiting for transfers between devices, ring_move(): lax.ppermute(block, 'seq', [(order[i], order[(i + step) % count]) for i i...  130 us
    pallas_call x5, Pallas kernels, by_row(): pl.pallas_call(kernel, grid=(rows,), in_specs=[spec(a.shape, kind) for a,...  64.7 us
    pallas_call x24, Pallas kernels, on_block(): pl.pallas_call(kernel, grid_spec=pltpu.PrefetchScalarGridSpec(num_scalar_...  64.6 us
    pallas_call x5, Pallas kernels, turned_product(): pl.pallas_call(kernel, grid_spec=pltpu.PrefetchScalarGridSpec(num_scalar_...  59.9 us
    ppermute x48, starting transfers between devices, ring_move(): lax.ppermute(block, 'seq', [(order[i], order[(i + step) % count]) for i i...  57.9 us
    ppermute x16, waiting for transfers between devices, chip_move(): lax.ppermute(block, 'head', [(i, (i + 2 * step) % count) for i in range(c...  54.1 us
    unnamed x281, local copies, waits for them, and re-layouts  48.6 us
    pallas_call x3, Pallas kernels, weight_gradients(): pl.pallas_call(kernel, grid=(width // tile,), in_specs=[column] * len(lef...  48.3 us
  transfers between devices with their start and end apart: 113, of which 54 were waited for; matrix products, arithmetic and copies ran while one was open for 8% of the time, Pallas kernels for 40%

profile of v4, /device:TPU:0, one launch (start us, length us, event | category | flops | bytes accessed | tf_op | source)
XLA Modules:
  0.0 833.8 jit_solution(2838382308431172333)
XLA Ops:
  24.8 11.9 %collective-permute-done.1.refs_1_ = bf16[256,1280]{1,0:T(8,128)(2,1)S(1)} collective-permute-done((bf16[256,1280]{1,0:T(8,128)(2,1)S(1)}, bf16[256,1280]{1,0:T(8,128)(2,1)S(1)}, u32[]{:S(2)}, u32[]{:S(2)}) %collective-permute-start.1) | collective-permute-done | bytes 655392 | tf_op jit(solution)/shard_map/ppermute | solution.py:49
  39.7 12.0 %collective-permute-done.2.refs_0_ = bf16[256,1280]{1,0:T(8,128)(2,1)S(1)} collective-permute-done((bf16[256,1280]{1,0:T(8,128)(2,1)S(1)}, bf16[256,1280]{1,0:T(8,128)(2,1)S(1)}, u32[]{:S(2)}, u32[]{:S(2)}) %collective-permute-start.2) | collective-permute-done | bytes 655392 | tf_op jit(solution)/shard_map/ppermute | solution.py:49
  76.3 16.6 %prepare.1 = (bf16[1024,768]{1,0:T(8,128)(2,1)S(1)}, bf16[1024,1280]{1,0:T(8,128)(2,1)}, bf16[8,64,512]{2,1,0:T(8,128)(2,1)S(1)}, bf16[8,2,80,128]{3,2,1,0:T(8,128)(2,1)S(1)}, bf16[8,2,80,128]{3,2,1,0:T(8,128)(2,1)S(1)}) custom-call(f32[1024,768]{1,0:T(8,128)} %multiply_add_fusion.lin_ref, f32[128,768]{1,0:T(8,128)S(1)} %concatenate.88.cos_ref, ...), custom_call_target="tpu_custom_call" | custom-call | flops 160000000 | tf_op jit(solution)/shard_map/prepare/pallas_call | solution.py:766
  96.4 31.1 %collective-permute-done.9.refs_1_ = bf16[256,3072]{1,0:T(8,128)(2,1)} collective-permute-done((bf16[256,3072]{1,0:T(8,128)(2,1)}, bf16[256,3072]{1,0:T(8,128)(2,1)}, u32[]{:S(2)}, u32[]{:S(2)}) %collective-permute-start.9) | collective-permute-done | bytes 1572896 | tf_op jit(solution)/shard_map/ppermute | solution.py:49
  219.5 9.4 %collective-permute-done.24.refs_0_ = bf16[128,2048]{1,0:T(8,128)(2,1)S(1)} collective-permute-done((bf16[128,2048]{1,0:T(8,128)(2,1)}, bf16[128,2048]{1,0:T(8,128)(2,1)S(1)}, u32[]{:S(2)}, u32[]{:S(2)}) %collective-permute-start.24) | collective-permute-done | bytes 524320 | tf_op jit(solution)/shard_map/ppermute | solution.py:270
  228.9 8.7 %collective-permute-done.25.refs_1_ = bf16[128,2048]{1,0:T(8,128)(2,1)S(1)} collective-permute-done((bf16[128,2048]{1,0:T(8,128)(2,1)}, bf16[128,2048]{1,0:T(8,128)(2,1)S(1)}, u32[]{:S(2)}, u32[]{:S(2)}) %collective-permute-start.25) | collective-permute-done | bytes 524320 | tf_op jit(solution)/shard_map/ppermute | solution.py:270
  246.6 12.8 %collective-permute-done.28.refs_4_ = bf16[128,2048]{1,0:T(8,128)(2,1)} collective-permute-done((bf16[128,2048]{1,0:T(8,128)(2,1)}, bf16[128,2048]{1,0:T(8,128)(2,1)}, u32[]{:S(2)}, u32[]{:S(2)}) %collective-permute-start.28) | collective-permute-done | bytes 524320 | tf_op jit(solution)/shard_map/ppermute | solution.py:270
  259.4 10.8 %collective-permute-done.29.refs_5_ = bf16[128,2048]{1,0:T(8,128)(2,1)} collective-permute-done((bf16[128,2048]{1,0:T(8,128)(2,1)}, bf16[128,2048]{1,0:T(8,128)(2,1)}, u32[]{:S(2)}, u32[]{:S(2)}) %collective-permute-start.29) | collective-permute-done | bytes 524320 | tf_op jit(solution)/shard_map/ppermute | solution.py:270
  290.3 20.7 %hidden_units.2 = (bf16[1024,1024]{1,0:T(8,128)(2,1)}, bf16[1024,1024]{1,0:T(8,128)(2,1)}, bf16[1024,1024]{1,0:T(8,128)(2,1)}) custom-call(bf16[1024,2048]{1,0:T(8,128)(2,1)} %copy-done.2, bf16[1024,2048]{1,0:T(8,128)(2,1)} %bitcast.133, bf16[2048,3072]{1,0:T(8,128)(2,1)} %copy-done, bf16[2048,3072]{1,0:T(8,128)(2,1)} %copy-done, bf16[2048,3072]{1,0:T(8,128)(2,1)} %copy-done), custom_call_target="tpu_custom_call" | custom-call | flops 220000000 | tf_op jit(solution)/shard_map/hidden_units/pallas_call | solution.py:847
  317.9 13.7 %turned_product.6.refs_4_ = f32[1024,2048]{1,0:T(8,128)} custom-call(s32[1]{0:T(128)} %bitcast.5.core_ref, bf16[1024,1024]{1,0:T(8,128)(2,1)} %get-tuple-element.209.refs_0_.refs_2_, bf16[1024,1024]{1,0:T(8,128)(2,1)} %get-tuple-element.204.refs_1_.refs_3_, bf16[2048,3072]{1,0:T(8,128)(2,1)} %copy-done, bf16[2048,3072]{1,0:T(8,128)(2,1)} %copy-done), custom_call_target="tpu_custom_call" | custom-call | flops 140000000 | tf_op jit(solution)/shard_map/turned_product/pallas_call | solution.py:910
  331.6 19.0 %weight_gradients.3.own_ref = bf16[2048,3072]{1,0:T(8,128)(2,1)} custom-call(bf16[1024,2048]{1,0:T(8,128)(2,1)} %copy-done.2, bf16[1024,2048]{1,0:T(8,128)(2,1)} %bitcast.134, bf16[1024,1024]{1,0:T(8,128)(2,1)} %get-tuple-element.209.refs_0_.refs_2_, bf16[1024,1024]{1,0:T(8,128)(2,1)} %get-tuple-element.204.refs_1_.refs_3_, ...), custom_call_target="tpu_custom_call" | custom-call | flops 190000000 | tf_op jit(solution)/shard_map/weight_gradients/pallas_call | solution.py:956
  358.0 12.6 %collective-permute-done.40.refs_7_ = bf16[128,3072]{1,0:T(8,128)(2,1)S(1)} collective-permute-done((bf16[128,3072]{1,0:T(8,128)(2,1)}, bf16[128,3072]{1,0:T(8,128)(2,1)S(1)}, u32[]{:S(2)}, u32[]{:S(2)}) %collective-permute-start.40) | collective-permute-done | bytes 786464 | tf_op jit(solution)/shard_map/ppermute | solution.py:49
  383.6 20.7 %hidden_units.3 = (bf16[1024,1024]{1,0:T(8,128)(2,1)}, bf16[1024,1024]{1,0:T(8,128)(2,1)}, bf16[1024,1024]{1,0:T(8,128)(2,1)}) custom-call(bf16[1024,2048]{1,0:T(8,128)(2,1)} %copy-done.2, bf16[1024,2048]{1,0:T(8,128)(2,1)} %bitcast.135, bf16[2048,3072]{1,0:T(8,128)(2,1)} %copy-done.1, bf16[2048,3072]{1,0:T(8,128)(2,1)} %copy-done.1, ...), custom_call_target="tpu_custom_call" | custom-call | flops 220000000 | tf_op jit(solution)/shard_map/hidden_units/pallas_call | solution.py:847
  412.1 15.2 %turned_product.7 = (bf16[2,256,2048]{2,1,0:T(8,128)(2,1)}, bf16[2,256,512]{2,1,0:T(8,128)(2,1)}, bf16[2,256,512]{2,1,0:T(8,128)(2,1)}, bf16[2,256,512]{2,1,0:T(8,128)(2,1)}, bf16[2,256,512]{2,1,0:T(8,128)(2,1)}) custom-call(s32[1]{0:T(128)} %bitcast.5.core_ref, bf16[1024,1024]{1,0:T(8,128)(2,1)} %get-tuple-element.219.refs_0_.refs_2_, ...), custom_call_target="tpu_custom_call" | custom-call | flops 150000000 | tf_op jit(solution)/shard_map/turned_product/pallas_call | solution.py:910
  455.3 19.0 %weight_gradients.4.own_ref = bf16[2048,3072]{1,0:T(8,128)(2,1)} custom-call(bf16[1024,2048]{1,0:T(8,128)(2,1)} %copy-done.2, bf16[1024,2048]{1,0:T(8,128)(2,1)} %bitcast.136, bf16[1024,1024]{1,0:T(8,128)(2,1)} %get-tuple-element.219.refs_0_.refs_2_, bf16[1024,1024]{1,0:T(8,128)(2,1)} %get-tuple-element.220.refs_1_.refs_3_, ...), custom_call_target="tpu_custom_call" | custom-call | flops 190000000 | tf_op jit(solution)/shard_map/weight_gradients/pallas_call | solution.py:956
  490.5 14.3 %turned_product.8 = (bf16[2,256,2048]{2,1,0:T(8,128)(2,1)}, bf16[2,256,512]{2,1,0:T(8,128)(2,1)}, bf16[2,256,512]{2,1,0:T(8,128)(2,1)}, bf16[2,256,512]{2,1,0:T(8,128)(2,1)}, bf16[2,256,512]{2,1,0:T(8,128)(2,1)}) custom-call(s32[1]{0:T(128)} %bitcast.5.core_ref, bf16[1024,1024]{1,0:T(8,128)(2,1)} %get-tuple-element.210.refs_4_.refs_0_, ...), custom_call_target="tpu_custom_call" | custom-call | flops 15000000512 | tf_op jit(solution)/shard_map/turned_product/pallas_call | solution.py:910
  530.7 13.1 %collective-permute-done.64.up_ref = bf16[256,3072]{1,0:T(8,128)(2,1)} collective-permute-done((bf16[256,3072]{1,0:T(8,128)(2,1)}, bf16[256,3072]{1,0:T(8,128)(2,1)}, u32[]{:S(2)}, u32[]{:S(2)}) %collective-permute-start.64) | collective-permute-done | bytes 1572896 | tf_op jit(solution)/shard_map/ppermute | solution.py:49
  570.3 25.2 %backward.1 = (bf16[1024,512]{1,0:T(8,128)(2,1)S(1)}, f32[1024,512]{1,0:T(8,128)}, bf16[8,64,512]{2,1,0:T(8,128)(2,1)S(1)}, f32[4,128,256]{2,1,0:T(8,128)S(1)}) custom-call(bf16[1024,768]{1,0:T(8,128)(2,1)} %copy-done.9, bf16[1024,1280]{1,0:T(8,128)(2,1)} %get-tuple-element.170.phi_ref, bf16[8,64,512]{2,1,0:T(8,128)(2,1)S(1)} %copy-done.39, ...), custom_call_target="tpu_custom_call" | custom-call | flops 20000000000 | tf_op jit(solution)/shard_map/backward/pallas_call | solution.py:766
  597.2 10.2 %collective-permute-done.66 = bf16[4,2,80,128]{3,2,1,0:T(8,128)(2,1)S(1)} collective-permute-done((bf16[4,2,80,128]{3,2,1,0:T(8,128)(2,1)S(1)}, bf16[4,2,80,128]{3,2,1,0:T(8,128)(2,1)S(1)}, u32[]{:S(2)}, u32[]{:S(2)}) %collective-permute-start.66) | collective-permute-done | bytes 163872 | tf_op jit(solution)/shard_map/ppermute | solution.py:1054
  628.3 16.2 %collective-permute-done.72 = bf16[2,4,2,80,128]{4,3,2,1,0:T(8,128)(2,1)S(1)} collective-permute-done((bf16[2,4,2,80,128]{4,3,2,1,0:T(8,128)(2,1)S(1)}, bf16[2,4,2,80,128]{4,3,2,1,0:T(8,128)(2,1)S(1)}, u32[]{:S(2)}, u32[]{:S(2)}) %collective-permute-start.72) | collective-permute-done | bytes 327712 | tf_op jit(solution)/shard_map/ppermute | solution.py:39
  672.5 9.0 %turned_product.9 = (bf16[2,256,2048]{2,1,0:T(8,128)(2,1)}, bf16[2,256,512]{2,1,0:T(8,128)(2,1)}, bf16[2,256,512]{2,1,0:T(8,128)(2,1)}, bf16[2,256,512]{2,1,0:T(8,128)(2,1)}, bf16[2,256,512]{2,1,0:T(8,128)(2,1)}) custom-call(s32[1]{0:T(128)} %bitcast.5.core_ref, bf16[1024,512]{1,0:T(8,128)(2,1)} %copy-done.7, bf16[1024,256]{1,0:T(8,128)(2,1)} %copy-done.13, ...), custom_call_target="tpu_custom_call" | custom-call | flops 70000000 | tf_op jit(solution)/shard_map/turned_product/pallas_call | solution.py:910
  702.7 8.5 %collective-permute-done.81.refs_5_ = bf16[128,2048]{1,0:T(8,128)(2,1)S(1)} collective-permute-done((bf16[128,2048]{1,0:T(8,128)(2,1)S(1)}, bf16[128,2048]{1,0:T(8,128)(2,1)S(1)}, u32[]{:S(2)}, u32[]{:S(2)}) %collective-permute-start.81) | collective-permute-done | bytes 524320 | tf_op jit(solution)/shard_map/ppermute | solution.py:270
  715.7 10.3 %weight_gradients.5.own_ref = bf16[2048,1280]{1,0:T(8,128)(2,1)} custom-call(bf16[1024,2048]{1,0:T(8,128)(2,1)} %copy-done.46, bf16[1024,2048]{1,0:T(8,128)(2,1)} %copy-done.3, bf16[1024,512]{1,0:T(8,128)(2,1)} %copy-done.7, bf16[1024,256]{1,0:T(8,128)(2,1)} %copy-done.13, bf16[1024,512]{1,0:T(8,128)(2,1)} %copy-done.4), custom_call_target="tpu_custom_call" | custom-call | flops 100000000 | tf_op jit(solution)/shard_map/weight_gradients/pallas_call | solution.py:956
  812.8 10.0 %collective-permute-done.102 = bf16[1264,128]{1,0:T(8,128)(2,1)S(1)} collective-permute-done((bf16[1264,128]{1,0:T(8,128)(2,1)S(1)}, bf16[1264,128]{1,0:T(8,128)(2,1)S(1)}, u32[]{:S(2)}, u32[]{:S(2)}) %collective-permute-start.102) | collective-permute-done | bytes 323616 | tf_op jit(solution)/shard_map/ppermute | solution.py:406
  (661 shorter events, 480.0 us)
Async XLA Ops:
  169.4 35.0 %collective-permute-start.22 = (bf16[256,3072]{1,0:T(8,128)(2,1)}, bf16[256,3072]{1,0:T(8,128)(2,1)}, u32[]{:S(2)}, u32[]{:S(2)}) collective-permute-start(bf16[256,3072]{1,0:T(8,128)(2,1)} %collective-permute-done.9.refs_1_), channel_id=1, source_target_pairs={{0,8},{8,16},{16,24},{24,28},{28,20},{20,12},{12,4},{4,0},{1,9},{9... | collective-permute-start | bytes 4718600 | tf_op jit(solution)/shard_map/ppermute | solution.py:49
  174.9 35.7 %collective-permute-start.23 = (bf16[256,3072]{1,0:T(8,128)(2,1)}, bf16[256,3072]{1,0:T(8,128)(2,1)}, u32[]{:S(2)}, u32[]{:S(2)}) collective-permute-start(bf16[256,3072]{1,0:T(8,128)(2,1)} %collective-permute-done.11.refs_5_), channel_id=1, source_target_pairs={{0,4},{8,0},{16,8},{24,16},{28,24},{20,28},{12,20},{4,12},{1,5},{9... | collective-permute-start | bytes 4718600 | tf_op jit(solution)/shard_map/ppermute | solution.py:49
  206.4 35.8 %collective-permute-start.32 = (bf16[128,3072]{1,0:T(8,128)(2,1)}, bf16[128,3072]{1,0:T(8,128)(2,1)S(1)}, u32[]{:S(2)}, u32[]{:S(2)}) collective-permute-start(bf16[128,3072]{1,0:T(8,128)(2,1)} %slice.178), channel_id=1, source_target_pairs={{0,8},{8,16},{16,24},{24,28},{28,20},{20,12},{12,4},{4,0},{1,9},{9... | collective-permute-start | bytes 2359304 | tf_op jit(solution)/shard_map/ppermute | solution.py:49
  242.3 36.8 %collective-permute-start.34 = (bf16[256,3072]{1,0:T(8,128)(2,1)S(1)}, bf16[256,3072]{1,0:T(8,128)(2,1)}, u32[]{:S(2)}, u32[]{:S(2)}) collective-permute-start(bf16[256,3072]{1,0:T(8,128)(2,1)S(1)} %pad_maximum_fusion.4.refs_3_), channel_id=1, source_target_pairs={{0,8},{8,16},{16,24},{24,28},{28,20},{20,12},{12,4},{4,0},{1,9},{9... | collective-permute-start | bytes 4718600 | tf_op jit(solution)/shard_map/ppermute | solution.py:49
  244.3 36.8 %collective-permute-start.35 = (bf16[256,3072]{1,0:T(8,128)(2,1)S(1)}, bf16[256,3072]{1,0:T(8,128)(2,1)}, u32[]{:S(2)}, u32[]{:S(2)}) collective-permute-start(bf16[256,3072]{1,0:T(8,128)(2,1)S(1)} %pad_maximum_fusion.4.refs_3_), channel_id=1, source_target_pairs={{0,4},{8,0},{16,8},{24,16},{28,24},{20,28},{12,20},{4,12},{1,5},{9... | collective-permute-start | bytes 4718600 | tf_op jit(solution)/shard_map/ppermute | solution.py:49
  279.1 36.6 %collective-permute-start.36 = (bf16[256,3072]{1,0:T(8,128)(2,1)}, bf16[256,3072]{1,0:T(8,128)(2,1)S(1)}, u32[]{:S(2)}, u32[]{:S(2)}) collective-permute-start(bf16[256,3072]{1,0:T(8,128)(2,1)} %collective-permute-done.34.refs_2_), channel_id=1, source_target_pairs={{0,8},{8,16},{16,24},{24,28},{28,20},{20,12},{12,4},{4,0},{1,9},{9... | collective-permute-start | bytes 4718600 | tf_op jit(solution)/shard_map/ppermute | solution.py:49
  281.1 36.6 %collective-permute-start.38 = (bf16[256,3072]{1,0:T(8,128)(2,1)}, bf16[256,3072]{1,0:T(8,128)(2,1)}, u32[]{:S(2)}, u32[]{:S(2)}) collective-permute-start(bf16[256,3072]{1,0:T(8,128)(2,1)} %collective-permute-done.35.refs_4_), channel_id=1, source_target_pairs={{0,4},{8,0},{16,8},{24,16},{28,24},{20,28},{12,20},{4,12},{1,5},{9... | collective-permute-start | bytes 4718600 | tf_op jit(solution)/shard_map/ppermute | solution.py:49
  315.8 35.7 %collective-permute-start.37 = (bf16[256,3072]{1,0:T(8,128)(2,1)S(1)}, bf16[256,3072]{1,0:T(8,128)(2,1)S(1)}, u32[]{:S(2)}, u32[]{:S(2)}) collective-permute-start(bf16[256,3072]{1,0:T(8,128)(2,1)S(1)} %collective-permute-done.36.refs_1_), channel_id=1, source_target_pairs={{0,8},{8,16},{16,24},{24,28},{28,20},{20,12},{12,4},{4,0},{1,9},{9... | collective-permute-start | bytes 4718600 | tf_op jit(solution)/shard_map/ppermute | solution.py:49
  317.8 36.6 %collective-permute-start.39 = (bf16[256,3072]{1,0:T(8,128)(2,1)}, bf16[256,3072]{1,0:T(8,128)(2,1)S(1)}, u32[]{:S(2)}, u32[]{:S(2)}) collective-permute-start(bf16[256,3072]{1,0:T(8,128)(2,1)} %collective-permute-done.38.refs_5_), channel_id=1, source_target_pairs={{0,4},{8,0},{16,8},{24,16},{28,24},{20,28},{12,20},{4,12},{1,5},{9... | collective-permute-start | bytes 4718600 | tf_op jit(solution)/shard_map/ppermute | solution.py:49
  375.1 33.9 %collective-permute-start.43 = (bf16[128,3072]{1,0:T(8,128)(2,1)}, bf16[128,3072]{1,0:T(8,128)(2,1)}, u32[]{:S(2)}, u32[]{:S(2)}) collective-permute-start(bf16[128,3072]{1,0:T(8,128)(2,1)} %get-tuple-element.218), channel_id=1, source_target_pairs={{0,4},{8,0},{16,8},{24,16},{28,24},{20,28},{12,20},{4,12},{1,5},{9... | collective-permute-start | bytes 2359304 | tf_op jit(solution)/shard_map/ppermute | solution.py:49
  411.8 34.6 %collective-permute-start.49 = (bf16[256,3072]{1,0:T(8,128)(2,1)}, bf16[256,3072]{1,0:T(8,128)(2,1)S(1)}, u32[]{:S(2)}, u32[]{:S(2)}) collective-permute-start(bf16[256,3072]{1,0:T(8,128)(2,1)} %join_block.19), channel_id=1, source_target_pairs={{0,4},{8,0},{16,8},{24,16},{28,24},{20,28},{12,20},{4,12},{1,5},{9... | collective-permute-start | bytes 4718600 | tf_op jit(solution)/shard_map/ppermute | solution.py:49
  444.7 37.6 %collective-permute-start.52 = (bf16[256,3072]{1,0:T(8,128)(2,1)}, bf16[256,3072]{1,0:T(8,128)(2,1)S(1)}, u32[]{:S(2)}, u32[]{:S(2)}) collective-permute-start(bf16[256,3072]{1,0:T(8,128)(2,1)} %join_block.20), channel_id=1, source_target_pairs={{0,8},{8,16},{16,24},{24,28},{28,20},{20,12},{12,4},{4,0},{1,9},{9... | collective-permute-start | bytes 4718600 | tf_op jit(solution)/shard_map/ppermute | solution.py:49
  450.6 35.8 %collective-permute-start.53 = (bf16[256,3072]{1,0:T(8,128)(2,1)}, bf16[256,3072]{1,0:T(8,128)(2,1)S(1)}, u32[]{:S(2)}, u32[]{:S(2)}) collective-permute-start(bf16[256,3072]{1,0:T(8,128)(2,1)} %join_block.22), channel_id=1, source_target_pairs={{0,4},{8,0},{16,8},{24,16},{28,24},{20,28},{12,20},{4,12},{1,5},{9... | collective-permute-start | bytes 4718600 | tf_op jit(solution)/shard_map/ppermute | solution.py:49
  506.4 37.5 %collective-permute-start.64 = (bf16[256,3072]{1,0:T(8,128)(2,1)}, bf16[256,3072]{1,0:T(8,128)(2,1)}, u32[]{:S(2)}, u32[]{:S(2)}) collective-permute-start(bf16[256,3072]{1,0:T(8,128)(2,1)} %join_block.21), channel_id=1, source_target_pairs={{0,8},{8,16},{16,24},{24,28},{28,20},{20,12},{12,4},{4,0},{1,9},{9... | collective-permute-start | bytes 4718600 | tf_op jit(solution)/shard_map/ppermute | solution.py:49
  508.1 37.7 %collective-permute-start.65 = (bf16[256,3072]{1,0:T(8,128)(2,1)}, bf16[256,3072]{1,0:T(8,128)(2,1)}, u32[]{:S(2)}, u32[]{:S(2)}) collective-permute-start(bf16[256,3072]{1,0:T(8,128)(2,1)} %join_block.23), channel_id=1, source_target_pairs={{0,4},{8,0},{16,8},{24,16},{28,24},{20,28},{12,20},{4,12},{1,5},{9... | collective-permute-start | bytes 4718600 | tf_op jit(solution)/shard_map/ppermute | solution.py:49
  515.2 45.0 %collective-permute-start.67 = (bf16[128,3072]{1,0:T(8,128)(2,1)}, bf16[128,3072]{1,0:T(8,128)(2,1)S(1)}, u32[]{:S(2)}, u32[]{:S(2)}) collective-permute-start(bf16[128,3072]{1,0:T(8,128)(2,1)} %get-tuple-element.258), channel_id=1, source_target_pairs={{0,8},{8,16},{16,24},{24,28},{28,20},{20,12},{12,4},{4,0},{1,9},{9... | collective-permute-start | bytes 2359304 | tf_op jit(solution)/shard_map/ppermute | solution.py:49
  517.0 44.9 %collective-permute-start.68 = (bf16[128,3072]{1,0:T(8,128)(2,1)}, bf16[128,3072]{1,0:T(8,128)(2,1)S(1)}, u32[]{:S(2)}, u32[]{:S(2)}) collective-permute-start(bf16[128,3072]{1,0:T(8,128)(2,1)} %get-tuple-element.260), channel_id=1, source_target_pairs={{0,4},{8,0},{16,8},{24,16},{28,24},{20,28},{12,20},{4,12},{1,5},{9... | collective-permute-start | bytes 2359304 | tf_op jit(solution)/shard_map/ppermute | solution.py:49
  567.9 39.7 %collective-permute-start.69 = (bf16[256,3072]{1,0:T(8,128)(2,1)}, bf16[256,3072]{1,0:T(8,128)(2,1)S(1)}, u32[]{:S(2)}, u32[]{:S(2)}) collective-permute-start(bf16[256,3072]{1,0:T(8,128)(2,1)} %join_block.24), channel_id=1, source_target_pairs={{0,8},{8,16},{16,24},{24,28},{28,20},{20,12},{12,4},{4,0},{1,9},{9... | collective-permute-start | bytes 4718600 | tf_op jit(solution)/shard_map/ppermute | solution.py:49
  568.9 38.7 %collective-permute-start.70 = (bf16[256,3072]{1,0:T(8,128)(2,1)}, bf16[256,3072]{1,0:T(8,128)(2,1)S(1)}, u32[]{:S(2)}, u32[]{:S(2)}) collective-permute-start(bf16[256,3072]{1,0:T(8,128)(2,1)} %join_block.25), channel_id=1, source_target_pairs={{0,4},{8,0},{16,8},{24,16},{28,24},{20,28},{12,20},{4,12},{1,5},{9... | collective-permute-start | bytes 4718600 | tf_op jit(solution)/shard_map/ppermute | solution.py:49
  570.0 37.4 %collective-permute-start.66 = (bf16[4,2,80,128]{3,2,1,0:T(8,128)(2,1)S(1)}, bf16[4,2,80,128]{3,2,1,0:T(8,128)(2,1)S(1)}, u32[]{:S(2)}, u32[]{:S(2)}) collective-permute-start(bf16[4,2,80,128]{3,2,1,0:T(8,128)(2,1)S(1)} %constant_dynamic-slice_fusion), channel_id=1, source_target_pairs={{0,4},{4,0},{8,12},{12,8},{16,20},{20,16},{24,28},{28,24},{1,5},{5... | collective-permute-start | bytes 491528 | tf_op jit(solution)/shard_map/ppermute | solution.py:1054
  655.8 36.4 %collective-permute-start.88 = (bf16[256,3072]{1,0:T(8,128)(2,1)}, bf16[256,3072]{1,0:T(8,128)(2,1)}, u32[]{:S(2)}, u32[]{:S(2)}) collective-permute-start(bf16[256,3072]{1,0:T(8,128)(2,1)} %join_block.26), channel_id=1, source_target_pairs={{0,8},{8,16},{16,24},{24,28},{28,20},{20,12},{12,4},{4,0},{1,9},{9... | collective-permute-start | bytes 4718600 | tf_op jit(solution)/shard_map/ppermute | solution.py:49
  656.4 40.2 %collective-permute-start.89 = (bf16[256,3072]{1,0:T(8,128)(2,1)}, bf16[256,3072]{1,0:T(8,128)(2,1)}, u32[]{:S(2)}, u32[]{:S(2)}) collective-permute-start(bf16[256,3072]{1,0:T(8,128)(2,1)} %join_block.28), channel_id=1, source_target_pairs={{0,4},{8,0},{16,8},{24,16},{28,24},{20,28},{12,20},{4,12},{1,5},{9... | collective-permute-start | bytes 4718600 | tf_op jit(solution)/shard_map/ppermute | solution.py:49
  699.6 49.8 %collective-permute-start.98 = (bf16[256,3072]{1,0:T(8,128)(2,1)}, bf16[256,3072]{1,0:T(8,128)(2,1)}, u32[]{:S(2)}, u32[]{:S(2)}) collective-permute-start(bf16[256,3072]{1,0:T(8,128)(2,1)} %join_block.27), channel_id=1, source_target_pairs={{0,8},{8,16},{16,24},{24,28},{28,20},{20,12},{12,4},{4,0},{1,9},{9... | collective-permute-start | bytes 4718600 | tf_op jit(solution)/shard_map/ppermute | solution.py:49
  699.8 49.6 %collective-permute-start.99 = (bf16[256,3072]{1,0:T(8,128)(2,1)}, bf16[256,3072]{1,0:T(8,128)(2,1)}, u32[]{:S(2)}, u32[]{:S(2)}) collective-permute-start(bf16[256,3072]{1,0:T(8,128)(2,1)} %join_block.29), channel_id=1, source_target_pairs={{0,4},{8,0},{16,8},{24,16},{28,24},{20,28},{12,20},{4,12},{1,5},{9... | collective-permute-start | bytes 4718600 | tf_op jit(solution)/shard_map/ppermute | solution.py:49
  (227 other events, 2878.6 us)
